TPU v7x, 32 devices: a whole 2x2x4 slice. The times are simulated.
32 devices in a mesh: dp: 8 (over y, x, core), mp: 4 (over z).
Axes of the slice: x: 2, y: 2, z: 4, core: 2. Of those that a mesh axis runs over, the one named last changes fastest.
Arguments:
- inputs: bfloat16 [1024, 2048], P('dp'), may hold values from -6 to 6
- segment_ids: int32 [8, 128], P('dp'), may hold values from 0 to 5, never falling along the last dimension, each value on 1 to 64 neighbouring positions
- cotangent: bfloat16 [1024, 2048], P('dp'), may hold values from -6 to 6
- query_key_value: float32 [3, 2048, 2048], P(None, 'dp', 'mp'), may hold values from -1 to 1
- attention_out: float32 [2048, 2048], P(('mp', 'dp')), may hold values from -1 to 1
- expand_weight: float32 [2048, 8192], P('dp', 'mp'), may hold values from -0.125 to 0.125
- contract_weight: float32 [8192, 2048], P(('mp', 'dp')), may hold values from -0.25 to 0.25
- norm_params: float32 [4, 2048], P(None, 'dp'), may hold values from -2 to 2
- first_query_key_value: float32 [3, 2048, 2048], P(None, 'dp', 'mp'), may hold values from -2 to 2
- first_attention_out: float32 [2048, 2048], P(('mp', 'dp')), may hold values from -0.375 to 0.375
- first_expand_weight: float32 [2048, 8192], P('dp', 'mp'), may hold values from -1.5 to 1.5
- first_contract_weight: float32 [8192, 2048], P(('mp', 'dp')), may hold values from -2 to 2
- first_norm_params: float32 [4, 2048], P(None, 'dp'), may hold values from -2 to 2
- second_query_key_value: float32 [3, 2048, 2048], P(None, 'dp', 'mp'), may hold values from 0.03 to 0.3
- second_attention_out: float32 [2048, 2048], P(('mp', 'dp')), may hold values from 0.0008 to 0.008
- second_expand_weight: float32 [2048, 8192], P('dp', 'mp'), may hold values from 0.015 to 0.15
- second_contract_weight: float32 [8192, 2048], P(('mp', 'dp')), may hold values from 0.03 to 0.3
- second_norm_params: float32 [4, 2048], P(None, 'dp'), may hold values from 0.03 to 0.3
Outputs:
- layer_output: bfloat16 [1024, 2048], P('dp')
- input_grad: float32 [1024, 2048], P('dp')
- grad_query_key_value: float32 [3, 2048, 2048], P(None, 'dp', 'mp')
- grad_attention_out: float32 [2048, 2048], P(('mp', 'dp'))
- grad_expand_weight: float32 [2048, 8192], P('dp', 'mp')
- grad_contract_weight: float32 [8192, 2048], P(('mp', 'dp'))
- grad_norm_params: float32 [4, 2048], P(None, 'dp')
- new_first_query_key_value: float32 [3, 2048, 2048], P(None, 'dp', 'mp')
- new_first_attention_out: float32 [2048, 2048], P(('mp', 'dp'))
- new_first_expand_weight: float32 [2048, 8192], P('dp', 'mp')
- new_first_contract_weight: float32 [8192, 2048], P(('mp', 'dp'))
- new_first_norm_params: float32 [4, 2048], P(None, 'dp')
- new_second_query_key_value: float32 [3, 2048, 2048], P(None, 'dp', 'mp')
- new_second_attention_out: float32 [2048, 2048], P(('mp', 'dp'))
- new_second_expand_weight: float32 [2048, 8192], P('dp', 'mp')
- new_second_contract_weight: float32 [8192, 2048], P(('mp', 'dp'))
- new_second_norm_params: float32 [4, 2048], P(None, 'dp')
- new_query_key_value: float32 [3, 2048, 2048], P(None, 'dp', 'mp')
- new_attention_out: float32 [2048, 2048], P(('mp', 'dp'))
- new_expand_weight: float32 [2048, 8192], P('dp', 'mp')
- new_contract_weight: float32 [8192, 2048], P(('mp', 'dp'))
- new_norm_params: float32 [4, 2048], P(None, 'dp')
- copy_query_key_value: bfloat16 [3, 2048, 2048], P(None, 'dp', 'mp')
- copy_attention_out: bfloat16 [2048, 2048], P(('mp', 'dp'))
- copy_expand_weight: bfloat16 [2048, 8192], P('dp', 'mp')
- copy_contract_weight: bfloat16 [8192, 2048], P(('mp', 'dp'))
- copy_norm_params: bfloat16 [4, 2048], P(None, 'dp')
- gradient_norm: float32 [], replicated
Inputs may be any that keep to these rules, and one draw needn't show every extreme that they name: `segment_ids`: along each row the ids never fall; a segment holds 1 to 64 positions.
All inputs are finite; a program needn't handle non-finite values.
Results may differ from a plain program's by a relative error of at most 0.015.
Values may be sent and summed in bfloat16 or wider, within the bound.
A program may use at most 256 MiB of HBM per device.

v0:
```python
import math

import jax
import jax.numpy as jnp
from jax import lax
from jax.sharding import PartitionSpec as P

HEAD_DIM = 128
ADAM_STEP = 5
MAX_NORM = 8192


BETA_ONE = 0.9
BETA_TWO = 0.95
ADAM_EPSILON = 1e-08
WEIGHT_DECAY = 0.1
NORM_EPSILON = 1e-05
CLIP_EPSILON = 1e-06
LEARN_RATES = (0.01, 0.08, 0.012, 0.02, 0.3)
MASKED_SCORE = -1e30


def layer_norm(values, gain_row, shift_row):
    row_mean = jnp.mean(values, axis=-1, keepdims=True)
    centered = values - row_mean
    spread = jnp.mean(centered * centered, axis=-1, keepdims=True)
    return centered * lax.rsqrt(spread + NORM_EPSILON) * gain_row + shift_row


def gelu_tanh(values):
    return jax.nn.gelu(values, approximate=True)


def adam_update(weight, grad, first, second, rate, clip_factor):
    clipped = grad * clip_factor
    new_first = BETA_ONE * first + (1.0 - BETA_ONE) * clipped
    new_second = BETA_TWO * second + (1.0 - BETA_TWO) * clipped * clipped
    first_hat = new_first / (1.0 - BETA_ONE**ADAM_STEP)
    second_hat = new_second / (1.0 - BETA_TWO**ADAM_STEP)
    new_weight = weight - rate * (
        first_hat / (jnp.sqrt(second_hat) + ADAM_EPSILON) + WEIGHT_DECAY * weight
    )
    return (new_first, new_second, new_weight)


def local(
    inputs,
    segment_ids,
    cotangent,
    query_key_value,
    attention_out,
    expand_weight,
    contract_weight,
    norm_params,
    first_query_key_value,
    first_attention_out,
    first_expand_weight,
    first_contract_weight,
    first_norm_params,
    second_query_key_value,
    second_attention_out,
    second_expand_weight,
    second_contract_weight,
    second_norm_params,
):
    params = (query_key_value, attention_out, expand_weight, contract_weight, norm_params)
    firsts = (
        first_query_key_value,
        first_attention_out,
        first_expand_weight,
        first_contract_weight,
        first_norm_params,
    )
    seconds = (
        second_query_key_value,
        second_attention_out,
        second_expand_weight,
        second_contract_weight,
        second_norm_params,
    )
    joint_weight, output_weight, expand_full, contract_full, norm_copy = (
        lax.all_gather(query_key_value.astype(jnp.bfloat16), "dp", axis=1, tiled=True),
        lax.all_gather(attention_out.astype(jnp.bfloat16), "dp", axis=0, tiled=True),
        lax.all_gather(expand_weight.astype(jnp.bfloat16), "dp", axis=0, tiled=True),
        lax.all_gather(contract_weight.astype(jnp.bfloat16), "dp", axis=0, tiled=True),
        lax.all_gather(norm_params.astype(jnp.bfloat16), "dp", axis=1, tiled=True),
    )
    norm_weights = norm_copy.astype(jnp.float32)
    tokens = inputs.astype(jnp.float32)
    row_length = tokens.shape[0]
    local_width = joint_weight.shape[2]
    local_heads = local_width // HEAD_DIM
    block_rows = min(512, row_length)
    score_scale = 1.0 / math.sqrt(HEAD_DIM)
    row_segments = segment_ids[0]
    places = jnp.arange(row_length, dtype=jnp.int32)
    normed_one, pull_one = jax.vjp(layer_norm, tokens, norm_weights[0], norm_weights[1])
    normed_low = normed_one.astype(jnp.bfloat16)
    joint = jnp.einsum(
        "td,cde->cte", normed_low, joint_weight, preferred_element_type=jnp.float32
    ).astype(jnp.bfloat16)
    query_rows = joint[0].reshape(row_length, local_heads, HEAD_DIM)
    key_rows = joint[1].reshape(row_length, local_heads, HEAD_DIM)
    value_rows = joint[2].reshape(row_length, local_heads, HEAD_DIM)

    def block_scores(first_row):
        raw_scores = jnp.einsum(
            "qhd,khd->hqk", query_rows, key_rows, preferred_element_type=jnp.float32
        )
        allowed = (
            row_segments[first_row : first_row + block_rows, None] == row_segments[None, :]
        ) & (places[None, :] <= places[first_row : first_row + block_rows, None])
        return jnp.where(allowed[None], raw_scores * score_scale, MASKED_SCORE)

    attended_parts, row_peaks, row_totals = ([], [], [])
    block_index = 0
    scores = block_scores(block_index * block_rows)
    row_peak = jnp.max(scores, axis=-1, keepdims=True)
    exponent = jnp.exp(scores - row_peak)
    row_total = jnp.sum(exponent, axis=-1, keepdims=True)
    prob_block = (exponent / row_total).astype(jnp.bfloat16)
    attended_parts.append(
        jnp.einsum("hqk,khd->qhd", prob_block, value_rows, preferred_element_type=jnp.float32)
    )
    row_peaks.append(row_peak)
    row_totals.append(row_total)
    attended = attended_parts[0].reshape(row_length, local_width).astype(jnp.bfloat16)
    branch_one = lax.psum(
        jnp.dot(attended, output_weight, preferred_element_type=jnp.float32), "mp"
    )
    hidden = tokens + branch_one
    normed_two, pull_two = jax.vjp(layer_norm, hidden, norm_weights[2], norm_weights[3])
    second_low = normed_two.astype(jnp.bfloat16)
    pre_gelu = jnp.dot(second_low, expand_full, preferred_element_type=jnp.float32)
    activated, pull_gelu = jax.vjp(gelu_tanh, pre_gelu)
    activated_low = activated.astype(jnp.bfloat16)
    branch_two = lax.psum(
        jnp.dot(activated_low, contract_full, preferred_element_type=jnp.float32).astype(
            jnp.bfloat16
        ),
        "mp",
    ).astype(jnp.float32)
    layer_output = (hidden + branch_two).astype(jnp.bfloat16)
    grad_output = cotangent.astype(jnp.float32)
    d_activated = jnp.einsum(
        "td,fd->tf", cotangent, contract_full, preferred_element_type=jnp.float32
    )
    grad_contract = jnp.einsum(
        "tf,td->fd", activated_low, cotangent, preferred_element_type=jnp.float32
    )
    (d_pre,) = pull_gelu(d_activated)
    d_pre_low = d_pre.astype(jnp.bfloat16)
    grad_expand = jnp.einsum("td,tf->df", second_low, d_pre_low, preferred_element_type=jnp.float32)
    d_normed_two = lax.psum(
        jnp.einsum("tf,df->td", d_pre_low, expand_full, preferred_element_type=jnp.float32), "mp"
    )
    d_hidden_norm, gain_two, shift_two = pull_two(d_normed_two)
    d_hidden = grad_output + d_hidden_norm
    branch_grad_low = d_hidden.astype(jnp.bfloat16)
    grad_output_weight = jnp.einsum(
        "te,td->ed", attended, branch_grad_low, preferred_element_type=jnp.float32
    )
    d_attended = jnp.einsum(
        "td,ed->te", branch_grad_low, output_weight, preferred_element_type=jnp.float32
    ).astype(jnp.bfloat16)
    d_attended = d_attended.reshape(row_length, local_heads, HEAD_DIM)
    block_index = 0
    first_row = block_index * block_rows
    scores = block_scores(first_row)
    prob_full = jnp.exp(scores - row_peaks[block_index]) / row_totals[block_index]
    prob_block = prob_full.astype(jnp.bfloat16)
    d_prob = jnp.einsum("qhd,khd->hqk", d_attended, value_rows, preferred_element_type=jnp.float32)
    d_values = jnp.einsum(
        "hqk,qhd->khd", prob_block, d_attended, preferred_element_type=jnp.float32
    )
    row_delta = jnp.sum(d_prob * prob_full, axis=-1, keepdims=True)
    d_raw = (prob_full * (d_prob - row_delta) * score_scale).astype(jnp.bfloat16)
    d_queries = jnp.einsum("hqk,khd->qhd", d_raw, key_rows, preferred_element_type=jnp.float32)
    d_keys = jnp.einsum("hqk,qhd->khd", d_raw, query_rows, preferred_element_type=jnp.float32)
    d_joint = jnp.stack(
        [
            d_queries.reshape(row_length, local_width),
            d_keys.reshape(row_length, local_width),
            d_values.reshape(row_length, local_width),
        ]
    ).astype(jnp.bfloat16)
    grad_joint = jnp.einsum("td,cte->cde", normed_low, d_joint, preferred_element_type=jnp.float32)
    d_normed_one = lax.psum(
        jnp.einsum("cte,cde->td", d_joint, joint_weight, preferred_element_type=jnp.float32).astype(
            jnp.bfloat16
        ),
        "mp",
    ).astype(jnp.float32)
    d_tokens_norm, gain_one, shift_one = pull_one(d_normed_one)
    input_grad = d_hidden + d_tokens_norm
    grad_norm_rows = jnp.stack([gain_one, shift_one, gain_two, shift_two])
    reduced_joint, reduced_output, reduced_expand, reduced_contract, reduced_norms = (
        lax.psum_scatter(grad_joint, "dp", scatter_dimension=1, tiled=True),
        lax.psum_scatter(grad_output_weight, "dp", scatter_dimension=0, tiled=True),
        lax.psum_scatter(grad_expand, "dp", scatter_dimension=0, tiled=True),
        lax.psum_scatter(grad_contract, "dp", scatter_dimension=0, tiled=True),
        lax.psum_scatter(grad_norm_rows, "dp", scatter_dimension=1, tiled=True),
    )
    grads = (reduced_joint, reduced_output, reduced_expand, reduced_contract, reduced_norms)
    squares = sum((jnp.sum(entry * entry) for entry in grads[:4])) + jnp.sum(
        reduced_norms * reduced_norms
    ) / lax.axis_size("mp")
    gradient_norm = jnp.sqrt(lax.psum(squares, ("dp", "mp")))
    clip_factor = jnp.minimum(1.0, MAX_NORM / (gradient_norm + CLIP_EPSILON))
    updates = [
        adam_update(params[k], grads[k], firsts[k], seconds[k], LEARN_RATES[k], clip_factor)
        for k in range(5)
    ]
    copies = [entry[2].astype(jnp.bfloat16) for entry in updates]
    return (
        layer_output,
        input_grad,
        grads[0],
        grads[1],
        grads[2],
        grads[3],
        grads[4],
        updates[0][0],
        updates[1][0],
        updates[2][0],
        updates[3][0],
        updates[4][0],
        updates[0][1],
        updates[1][1],
        updates[2][1],
        updates[3][1],
        updates[4][1],
        updates[0][2],
        updates[1][2],
        updates[2][2],
        updates[3][2],
        updates[4][2],
        copies[0],
        copies[1],
        copies[2],
        copies[3],
        copies[4],
        gradient_norm,
    )


def solution(mesh):
    placed = (
        P("dp", None),
        P("dp", None),
        P("dp", None),
        P(None, "dp", "mp"),
        P(("mp", "dp"), None),
        P("dp", "mp"),
        P(("mp", "dp"), None),
        P(None, "dp"),
        P(None, "dp", "mp"),
        P(("mp", "dp"), None),
        P("dp", "mp"),
        P(("mp", "dp"), None),
        P(None, "dp"),
        P(None, "dp", "mp"),
        P(("mp", "dp"), None),
        P("dp", "mp"),
        P(("mp", "dp"), None),
        P(None, "dp"),
    )
    return jax.shard_map(
        local,
        mesh=mesh,
        in_specs=placed,
        out_specs=(
            P("dp", None),
            P("dp", None),
            P(None, "dp", "mp"),
            P(("mp", "dp"), None),
            P("dp", "mp"),
            P(("mp", "dp"), None),
            P(None, "dp"),
            P(None, "dp", "mp"),
            P(("mp", "dp"), None),
            P("dp", "mp"),
            P(("mp", "dp"), None),
            P(None, "dp"),
            P(None, "dp", "mp"),
            P(("mp", "dp"), None),
            P("dp", "mp"),
            P(("mp", "dp"), None),
            P(None, "dp"),
            P(None, "dp", "mp"),
            P(("mp", "dp"), None),
            P("dp", "mp"),
            P(("mp", "dp"), None),
            P(None, "dp"),
            P(None, "dp", "mp"),
            P(("mp", "dp"), None),
            P("dp", "mp"),
            P(("mp", "dp"), None),
            P(None, "dp"),
            P(),
        ),
        check_vma=False,
    )
```

profile of v0, /device:TPU:0, one launch (start us, length us, event | category | flops | bytes accessed | tf_op | source)
XLA Modules:
  0.0 906.9 jit_solution(11532134231325504937)
XLA Ops:
  7.3 2.5 convert_element_type.99
  10.7 10.4 %all_gather.15 = bf16[4,2048]{1,0:T(4,128)(2,1)S(1)} all-gather(bf16[4,256]{1,0:T(4,128)(2,1)S(1)} %convert_element_type.96), channel_id=1, replica_groups=mesh['dp'=8,'mp'=4] {'dp'}, dimensions={1}, use_global_device_ids=true | all-gather | bytes 18432 | tf_op jit(solution)/shard_map/all_gather | solution.py:86
  22.7 36.1 %all-gather.5.cloned.1.call-done = bf16[3,2048,512]{2,1,0:T(8,128)(2,1)} async-done(((bf16[3,256,512]{2,1,0:T(8,128)(2,1)}), bf16[3,2048,512]{2,1,0:T(8,128)(2,1)}) %all-gather.5.cloned.1.call-update) | async-done | bytes 6291472 | tf_op jit(solution)/shard_map/all_gather | solution.py:82
  58.8 3.8 fusion.12
  64.3 24.9 %all-gather.7.cloned.1.call-done = bf16[512,2048]{1,0:T(8,128)(2,1)} async-done(((bf16[64,2048]{1,0:T(8,128)(2,1)}), bf16[512,2048]{1,0:T(8,128)(2,1)}) %all-gather.7.cloned.1.call-update) | async-done | bytes 2097168 | tf_op jit(solution)/shard_map/all_gather | solution.py:83
  89.2 3.0 fusion.77
  92.3 2.7 convert_element_type.110
  95.1 2.7 convert_element_type.108
  97.9 46.3 %all-reduce.5.cloned.1.call-done = f32[128,2048]{1,0:T(8,128)} async-done(((f32[128,2048]{1,0:T(8,128)}), f32[128,2048]{1,0:T(8,128)}) %all-reduce.5.cloned.1.call-update) | async-done | bytes 1048592 | tf_op jit(solution)/shard_map/psum | solution.py:128
  147.5 53.1 %all-gather.11.cloned.1.call-done = bf16[2048,2048]{1,0:T(8,128)(2,1)} async-done(((bf16[256,2048]{1,0:T(8,128)(2,1)}), bf16[2048,2048]{1,0:T(8,128)(2,1)}) %all-gather.11.cloned.1.call-update) | async-done | bytes 8388624 | tf_op jit(solution)/shard_map/all_gather | solution.py:85
  200.5 7.2 fusion.78
  207.8 49.7 %all-gather.9.cloned.1.call-done = bf16[2048,2048]{1,0:T(8,128)(2,1)} async-done(((bf16[256,2048]{1,0:T(8,128)(2,1)}), bf16[2048,2048]{1,0:T(8,128)(2,1)}) %all-gather.9.cloned.1.call-update) | async-done | bytes 8388624 | tf_op jit(solution)/shard_map/all_gather | solution.py:84
  257.4 5.8 fusion.28
  264.1 3.9 fusion.79
  268.2 5.6 convolution_convert_fusion
  273.8 46.1 %all-reduce.7.cloned.1.call-done = f32[128,2048]{1,0:T(8,128)} async-done(((f32[128,2048]{1,0:T(8,128)}), f32[128,2048]{1,0:T(8,128)}) %all-reduce.7.cloned.1.call-update) | async-done | bytes 1048592 | tf_op jit(solution)/shard_map/psum | solution.py:154
  319.9 2.3 multiply_reduce_fusion.3
  325.7 1.7 copy.105
  327.4 1.8 convolution_convert_fusion.3
  330.4 1.9 convolution_convert_fusion.5
  335.8 5.7 fusion.2
  341.6 51.7 %all-reduce.9.cloned.1.call-done = (bf16[128,2048]{1,0:T(8,128)(2,1)}, bf16[128,2048]{1,0:T(8,128)(2,1)}) async-done(((bf16[128,2048]{1,0:T(8,128)(2,1)}, bf16[128,2048]{1,0:T(8,128)(2,1)}), (bf16[128,2048]{1,0:T(8,128)(2,1)}, bf16[128,2048]{1,0:T(8,128)(2,1)})) %all-reduce.9.cloned.1.call-update) | async-done | bytes 1048592 | tf_op jit(solution)/shard_map/psum | solution.py:137
  395.8 2.2 fusion.31
  398.6 2.1 copy.101
  400.8 3.7 fusion.80
  404.6 7.2 convolution_bitcast_fusion
  412.5 9.2 %fusion.60 = f32[2048,2048]{1,0:T(8,128)} fusion(bf16[128,2048]{1,0:T(8,128)(2,1)} %copy-done.12, f32[128,2048]{1,0:T(8,128)S(1)} %get-tuple-element.115, f32[2048]{0:T(1024)S(1)} %bitcast.86, f32[2048]{0:T(1024)S(1)} %bitcast.80, f32[128]{0:T(128)S(1)} %copy-done.34, f32[128]{0:T(128)S(1)} %copy-done.32), kind=kOutput, calls=%fused_computation.117 | convolution fusion | flops 1075052544 | bytes 18367488 | tf_op jit(solution)/shard_map/td,tf->df/dot_general | solution.py:153
  422.0 9.3 %fusion.59 = f32[2048,2048]{1,0:T(8,128)} fusion(bf16[128,2048]{1,0:T(8,128)(2,1)S(1)} %copy-done.5, f32[128,2048]{1,0:T(8,128)} %copy-done.16), kind=kOutput, calls=%fused_computation.116 | convolution fusion | flops 1076101120 | bytes 18350080 | tf_op jit(solution)/shard_map/tf,td->fd/dot_general | solution.py:148
  431.4 3.0 copy.90
  434.4 3.0 copy.87
  437.5 3.1 copy.88
  440.6 2.9 add_add_fusion.2
  445.8 46.2 %reduce-scatter.10.cloned.1.call-done = f32[64,2048]{1,0:T(8,128)} async-done(((f32[512,2048]{1,0:T(8,128)}), f32[64,2048]{1,0:T(8,128)}) %reduce-scatter.10.cloned.1.call-update) | async-done | bytes 524304 | tf_op jit(solution)/shard_map/reduce_scatter | solution.py:199
  492.0 1.8 multiply_reduce_fusion.6
  493.8 94.0 %reduce-scatter.8.cloned.1.call-done = f32[3,256,512]{1,2,0:T(8,128)} async-done(((f32[3,2048,512]{1,2,0:T(8,128)}), f32[3,256,512]{1,2,0:T(8,128)}) %reduce-scatter.8.cloned.1.call-update) | async-done | bytes 1572880 | tf_op jit(solution)/shard_map/reduce_scatter | solution.py:198
  587.7 2.4 multiply_reduce_fusion.2
  591.5 116.4 %reduce-scatter.12.cloned.1.call-done = f32[256,2048]{1,0:T(8,128)} async-done(((f32[2048,2048]{1,0:T(8,128)}), f32[256,2048]{1,0:T(8,128)}) %reduce-scatter.12.cloned.1.call-update) | async-done | bytes 2097168 | tf_op jit(solution)/shard_map/reduce_scatter | solution.py:200
  707.9 2.7 multiply_reduce_fusion.1
  711.3 116.6 %reduce-scatter.14.cloned.1.call-done = f32[256,2048]{1,0:T(8,128)} async-done(((f32[2048,2048]{1,0:T(8,128)}), f32[256,2048]{1,0:T(8,128)}) %reduce-scatter.14.cloned.1.call-update) | async-done | bytes 2097168 | tf_op jit(solution)/shard_map/reduce_scatter | solution.py:201
  827.9 2.7 multiply_reduce_fusion
  831.4 1.6 copy.91
  833.0 39.5 %psum.39 = f32[]{:T(128)} all-reduce(f32[]{:T(128)S(6)} %add.180), channel_id=1, replica_groups=mesh['dp'=8,'mp'=4] {'dp','mp'}, use_global_device_ids=true, to_apply=%region_29.30 | all-reduce | flops 1 | bytes 8 | tf_op jit(solution)/shard_map/psum | solution.py:208
  873.3 5.1 fusion.70
  878.4 2.4 copy.95
  882.5 1.6 copy.93
  884.2 1.6 copy.92
  886.4 2.5 fusion.68
  889.0 10.0 %fusion.64 = (bf16[256,2048]{1,0:T(8,128)(2,1)}, f32[256,2048]{1,0:T(8,128)}, f32[256,2048]{1,0:T(8,128)}, f32[256,2048]{1,0:T(8,128)}, bf16[256,2048]{1,0:T(8,1...) fusion(f32[256,2048]{1,0:T(8,128)S(1)} %copy-done.2, ...), kind=kLoop, calls=%fused_computation.120 | loop fusion | flops 17825792 | bytes 31457284 | tf_op jit(solution)/shard_map/convert_element_type | solution.py:214
  (160 shorter events, 24.9 us)
Async XLA Ops:
  7.2 2.6 copy-start.13
  7.2 3.4 copy-start.26
  7.2 13.8 %copy-start = (bf16[128,2048]{1,0:T(8,128)(2,1)S(1)}, bf16[128,2048]{1,0:T(8,128)(2,1)}, u32[]{:S(2)}) copy-start(bf16[128,2048]{1,0:T(8,128)(2,1)} %param.18) | copy-start | bytes 1572868
  7.2 14.8 %copy-start.44 = (s32[1,128]{1,0:T(1,128)S(1)}, s32[1,128]{1,0:T(1,128)}, u32[]{:S(2)}) copy-start(s32[1,128]{1,0:T(1,128)} %param.19) | copy-start | bytes 1540
  7.2 51.6 %all-gather.5.cloned.1.call-start = ((), (), s32[]{:S(2)}) async-start(), calls=%async_computation.5 | async-start | bytes 7077888 | tf_op jit(solution)/shard_map/all_gather | solution.py:82
  9.8 79.4 %all-gather.7.cloned.1.call-start = ((), (), s32[]{:S(2)}) async-start(), calls=%async_computation.6 | async-start | bytes 2359296 | tf_op jit(solution)/shard_map/all_gather | solution.py:83
  10.6 133.7 %all-reduce.5.cloned.1.call-start = ((), (), s32[]{:S(2)}) async-start(), calls=%async_computation.7 | async-start | bytes 2097152 | tf_op jit(solution)/shard_map/psum | solution.py:128
  21.2 41.5 %copy-start.28 = (f32[128]{0:T(128)}, f32[128]{0:T(128)S(1)}, u32[]{:S(2)}) copy-start(f32[128]{0:T(128)S(1)} %broadcast_multiply_fusion.1) | copy-start | bytes 1540
  21.5 41.2 %copy-start.35 = (f32[128]{0:T(128)}, f32[128]{0:T(128)S(1)}, u32[]{:S(2)}) copy-start(f32[128]{0:T(128)S(1)} %fusion.53) | copy-start | bytes 1540
  22.7 39.9 %copy-start.25 = (f32[1,2048]{1,0:T(1,128)}, f32[1,2048]{1,0:T(1,128)S(1)}, u32[]{:S(2)}) copy-start(f32[1,2048]{1,0:T(1,128)S(1)} %get-tuple-element.122) | copy-start | bytes 24580
  62.9 29.4 %copy-start.20 = (bf16[128,4,128]{2,1,0:T(4,128)(2,1)}, bf16[128,4,128]{2,1,0:T(4,128)(2,1)S(1)}, u32[]{:S(2)}) copy-start(bf16[128,4,128]{2,1,0:T(4,128)(2,1)S(1)} %reshape_squeeze.9) | copy-start | bytes 393220
  64.0 28.2 %copy-start.39 = (f32[4,128]{1,0:T(4,128)}, f32[4,128]{1,0:T(4,128)S(1)}, u32[]{:S(2)}) copy-start(f32[4,128]{1,0:T(4,128)S(1)} %get-tuple-element.123) | copy-start | bytes 6148
  64.3 28.0 %copy-start.18 = (bf16[4,128,128]{2,1,0:T(8,128)(2,1)}, bf16[4,128,128]{2,1,0:T(8,128)(2,1)S(1)}, u32[]{:S(2)}) copy-start(bf16[4,128,128]{2,1,0:T(8,128)(2,1)S(1)} %convolution_convert_fusion.6) | copy-start | bytes 393220
  92.3 108.3 %all-gather.11.cloned.1.call-start = ((), (), s32[]{:S(2)}) async-start(), calls=%async_computation.9 | async-start | bytes 9437184 | tf_op jit(solution)/shard_map/all_gather | solution.py:85
  95.1 162.4 %all-gather.9.cloned.1.call-start = ((), (), s32[]{:S(2)}) async-start(), calls=%async_computation.8 | async-start | bytes 9437184 | tf_op jit(solution)/shard_map/all_gather | solution.py:84
  97.9 102.7 %copy-start.5 = (bf16[128,2048]{1,0:T(8,128)(2,1)S(1)}, bf16[128,2048]{1,0:T(8,128)(2,1)}, u32[]{:S(2)}) copy-start(bf16[128,2048]{1,0:T(8,128)(2,1)} %param.20) | copy-start | bytes 1572868
  97.9 222.0 %all-reduce.7.cloned.1.call-start = ((), (), s32[]{:S(2)}) async-start(), calls=%async_computation.10 | async-start | bytes 2097152 | tf_op jit(solution)/shard_map/psum | solution.py:154
  257.4 6.7 copy-start.3
  263.3 4.9 copy-start.16
  268.0 125.3 %all-reduce.9.cloned.1.call-start = ((), (), s32[]{:S(2)}) async-start(), calls=%async_computation.16 | async-start | bytes 2097152 | tf_op jit(solution)/shard_map/psum | solution.py:137
  273.8 48.5 %copy-start.46 = (f32[128]{0:T(128)S(1)}, f32[128]{0:T(128)}, u32[]{:S(2)}) copy-start(f32[128]{0:T(128)} %copy-done.45) | copy-start | bytes 1540
  319.9 2.4 copy-start.11
  319.9 2.4 copy-start.31
  319.9 2.4 copy-start.33
  322.3 1.9 copy-start.4
  341.5 102.0 %reduce-scatter.16.cloned.1.call-start = ((), (), s32[]{:S(2)}) async-start(), calls=%async_computation.15 | async-start | bytes 1179648
  393.2 4.7 copy-start.23
  393.2 4.7 copy-start.24
  400.7 91.2 %reduce-scatter.10.cloned.1.call-start = ((), (), s32[]{:S(2)}) async-start(), calls=%async_computation.12 | async-start | bytes 4718592 | tf_op jit(solution)/shard_map/reduce_scatter | solution.py:199
  404.6 183.2 %reduce-scatter.8.cloned.1.call-start = ((), (), s32[]{:S(2)}) async-start(), calls=%async_computation.11 | async-start | bytes 14155776 | tf_op jit(solution)/shard_map/reduce_scatter | solution.py:198
  411.8 296.1 %reduce-scatter.12.cloned.1.call-start = ((), (), s32[]{:S(2)}) async-start(), calls=%async_computation.13 | async-start | bytes 18874368 | tf_op jit(solution)/shard_map/reduce_scatter | solution.py:200
  421.8 406.1 %reduce-scatter.14.cloned.1.call-start = ((), (), s32[]{:S(2)}) async-start(), calls=%async_computation.14 | async-start | bytes 18874368 | tf_op jit(solution)/shard_map/reduce_scatter | solution.py:201
  437.5 3.1 copy-start.47
  437.5 3.1 copy-start.29
  437.5 3.1 copy-start.36
  437.5 3.1 copy-start.41
  437.5 3.1 copy-start.43
  444.5 441.3 %copy-start.22 = (f32[4,256]{1,0:T(4,128)}, f32[4,256]{1,0:T(4,128)S(1)}, u32[]{:S(2)}) copy-start(f32[4,256]{1,0:T(4,128)S(1)} %copy.102) | copy-start | bytes 12292
  591.5 239.9 %copy-start.1 = (f32[3,256,512]{1,2,0:T(8,128)S(1)}, f32[3,256,512]{1,2,0:T(8,128)}, u32[]{:S(2)}) copy-start(f32[3,256,512]{1,2,0:T(8,128)} %reduce-scatter.8.cloned.1.call-done) | copy-start | bytes 4718596
  830.6 42.7 %copy-start.6 = (f32[3,256,512]{1,2,0:T(8,128)S(1)}, f32[3,256,512]{1,2,0:T(8,128)}, u32[]{:S(2)}) copy-start(f32[3,256,512]{1,2,0:T(8,128)} %copy.90) | copy-start | bytes 4718596
  878.4 2.4 copy-start.9
  878.4 4.1 copy-start.8
  884.1 1.7 copy-start.37
  884.1 1.7 copy-start.38
  884.1 2.3 copy-start.14
  884.1 2.3 copy-start.15
  884.1 2.3 copy-start.17
  885.8 3.2 copy-start.2
  (13 other events, 10.6 us)
Sparse Core Ops, SparseCore 0:
  10.6 48.2 all-gather.4
  61.3 27.8 all-gather.6
  92.4 51.8 all-reduce.4
  146.7 53.7 all-gather.10
  203.0 54.3 all-gather.8
  268.1 51.7 all-reduce.6
  341.6 51.5 all-reduce.8
  400.9 35.4 reduce-scatter.15
  440.6 51.3 reduce-scatter.9
  495.3 92.3 reduce-scatter.7
  591.9 115.9 reduce-scatter.11
  711.9 115.9 reduce-scatter.13
where the time goes:
time: 908 us; the launch traced here: 907 us
  waiting for transfers between devices  681 us (75%)
  matrix products  72.7 us (8%)
  other arithmetic  51.4 us (6%)
  blocking collectives  49.9 us (5%)
  local copies, waits for them, and re-layouts  30.7 us (3%)
  between operations  20 us (2%)
    reduce_scatter x1, waiting for transfers between devices, local(): lax.psum_scatter(grad_contract, 'dp', scatter_dimension=0, tiled=True)  117 us
    reduce_scatter x1, waiting for transfers between devices, local(): lax.psum_scatter(grad_expand, 'dp', scatter_dimension=0, tiled=True)  116 us
    reduce_scatter x1, waiting for transfers between devices, local(): lax.psum_scatter(grad_joint, 'dp', scatter_dimension=1, tiled=True)  94 us
    all_gather x1, waiting for transfers between devices, local(): lax.all_gather(contract_weight.astype(jnp.bfloat16), 'dp', axis=0, tiled=...  53.1 us
    psum x1, waiting for transfers between devices, local(): lax.psum(jnp.dot(activated_low, contract_full, preferred_element_type=jnp...  51.7 us
    all_gather x1, waiting for transfers between devices, local(): lax.all_gather(expand_weight.astype(jnp.bfloat16), 'dp', axis=0, tiled=True)  49.7 us
    psum x1, waiting for transfers between devices, local(): lax.psum(jnp.dot(attended, output_weight, preferred_element_type=jnp.floa...  46.3 us
    reduce_scatter x1, waiting for transfers between devices, local(): lax.psum_scatter(grad_output_weight, 'dp', scatter_dimension=0, tiled=True)  46.2 us
  transfers between devices with their start and end apart: 12, of which 11 were waited for; matrix products, arithmetic and copies ran while one was open for 9% of the time, Pallas kernels for 0%

commit v1 on v0

v1 whole, which is shorter than its diff:
```python
import functools
import math

import jax
import jax.numpy as jnp
from jax import lax
from jax.experimental import pallas as pl
from jax.experimental.pallas import tpu as pltpu
from jax.sharding import PartitionSpec as P

HEAD_DIM = 128
ADAM_STEP = 5
MAX_NORM = 8192


BETA_ONE = 0.9
BETA_TWO = 0.95
ADAM_EPSILON = 1e-08
WEIGHT_DECAY = 0.1
NORM_EPSILON = 1e-05
CLIP_EPSILON = 1e-06
LEARN_RATES = (0.01, 0.08, 0.012, 0.02, 0.3)
MASKED_SCORE = -1e30
SCALE = 1.0 / math.sqrt(HEAD_DIM)
F32 = jnp.float32
BF16 = jnp.bfloat16
ROWS_COLS = (((1,), (0,)), ((), ()))
COLS_COLS = (((1,), (1,)), ((), ()))
ROWS_ROWS = (((0,), (0,)), ((), ()))


def mul(left, right, dims=ROWS_COLS):
    return lax.dot_general(left, right, dims, preferred_element_type=F32)


def layer_norm(values, gain_row, shift_row):
    row_mean = jnp.mean(values, axis=-1, keepdims=True)
    centered = values - row_mean
    spread = jnp.mean(centered * centered, axis=-1, keepdims=True)
    return centered * lax.rsqrt(spread + NORM_EPSILON) * gain_row + shift_row


def gelu_tanh(values):
    return jax.nn.gelu(values, approximate=True)


def adam_update(weight, grad, first, second, rate, clip_factor):
    clipped = grad * clip_factor
    new_first = BETA_ONE * first + (1.0 - BETA_ONE) * clipped
    new_second = BETA_TWO * second + (1.0 - BETA_TWO) * clipped * clipped
    first_hat = new_first / (1.0 - BETA_ONE**ADAM_STEP)
    second_hat = new_second / (1.0 - BETA_TWO**ADAM_STEP)
    new_weight = weight - rate * (
        first_hat / (jnp.sqrt(second_hat) + ADAM_EPSILON) + WEIGHT_DECAY * weight
    )
    return (new_first, new_second, new_weight)


class Group:
    def __init__(self, kind, dp_size, mp_size):
        self.kind = kind
        self.mp_size = mp_size
        chips = dp_size // 2
        self.size = {
            "pair": 2,
            "plane": chips,
            "column": mp_size,
            "cross": chips * mp_size,
            "row": dp_size,
            "all": dp_size * mp_size,
        }[kind]

    def me(self):
        dp, mp = lax.axis_index("dp"), lax.axis_index("mp")
        if self.kind == "pair":
            return lax.rem(dp, 2)
        if self.kind == "plane":
            return lax.div(dp, 2)
        if self.kind == "column":
            return mp
        if self.kind == "cross":
            return lax.div(dp, 2) * self.mp_size + mp
        if self.kind == "row":
            return dp
        return dp * self.mp_size + mp

    def device(self, member):
        dp, mp = lax.axis_index("dp"), lax.axis_index("mp")
        core = lax.rem(dp, 2)
        if self.kind == "pair":
            return (dp - core + member, mp)
        if self.kind == "plane":
            return (member * 2 + core, mp)
        if self.kind == "column":
            return (dp, member)
        if self.kind == "cross":
            return (lax.div(member, self.mp_size) * 2 + core, lax.rem(member, self.mp_size))
        if self.kind == "row":
            return (member, mp)
        return (lax.div(member, self.mp_size), lax.rem(member, self.mp_size))


def repeat(low, high, body):
    if high - low <= 8:
        for step in range(low, high):
            body(step)
    else:
        lax.fori_loop(low, high, lambda step, none: (body(step), none)[1], None)


def exchange(group, operands, results, moves, collective_id):
    count = len(operands)
    size = group.size
    lanes = len(moves)

    def kernel(*refs):
        ins, outs = refs[:count], refs[count : count + len(results)]
        send_sems, recv_sems, own_sems = refs[count + len(results) :]
        me = group.me()
        barrier = pltpu.get_barrier_semaphore()

        def greet(step):
            other = lax.rem(me + step, size)
            pl.semaphore_signal(
                barrier, inc=1, device_id=group.device(other), device_id_type=pl.DeviceIdType.MESH
            )

        repeat(1, size, greet)
        pl.semaphore_wait(barrier, size - 1)

        def remote(move, lane, step, sender, target, device):
            return pltpu.make_async_remote_copy(
                src_ref=move(ins, outs, me, target)[0],
                dst_ref=move(ins, outs, sender, me)[1],
                send_sem=send_sems.at[lane, step],
                recv_sem=recv_sems.at[lane, step],
                device_id=group.device(device),
                device_id_type=pl.DeviceIdType.MESH,
            )

        def launch(step):
            other = lax.rem(me + step, size)
            for lane, move in enumerate(moves):
                remote(move, lane, step, me, other, other).start()

        repeat(1, size, launch)
        own = []
        for lane, move in enumerate(moves):
            source, target = move(ins, outs, me, me)
            own.append(pltpu.make_async_copy(source, target, own_sems.at[lane]))
            own[-1].start()

        def finish(step):
            other = lax.rem(me + step, size)
            sender = lax.rem(me + size - step, size)
            for lane, move in enumerate(moves):
                remote(move, lane, step, sender, other, other).wait()

        repeat(1, size, finish)
        for copy in own:
            copy.wait()

    any_space = pl.BlockSpec(memory_space=pl.ANY)
    return pl.pallas_call(
        kernel,
        out_shape=results,
        in_specs=[any_space] * count,
        out_specs=[any_space] * len(results),
        scratch_shapes=[
            pltpu.SemaphoreType.DMA((lanes, size)),
            pltpu.SemaphoreType.DMA((lanes, size)),
            pltpu.SemaphoreType.DMA((lanes,)),
        ],
        compiler_params=pltpu.CompilerParams(collective_id=collective_id, has_side_effects=True),
    )(*operands)


def shape(dims, dtype=BF16):
    return jax.ShapeDtypeStruct(dims, dtype)


def part(index, width):
    return pl.ds(pl.multiple_of(index * width, width), width)


def allowed_pairs(seg_row, seg_col, length):
    places = lax.broadcasted_iota(jnp.int32, (length, length), 0)
    keys = lax.broadcasted_iota(jnp.int32, (length, length), 1)
    return (seg_col[...] == seg_row[...]) & (keys <= places)


def probabilities(query, key, allowed):
    scores = jnp.where(allowed, mul(query, key, COLS_COLS) * SCALE, MASKED_SCORE)
    exponent = jnp.exp(scores - jnp.max(scores, axis=-1, keepdims=True))
    return exponent / jnp.sum(exponent, axis=-1, keepdims=True)


def attend_kernel(width, joint, seg_row, seg_col, out_weight, attended, partial):
    allowed = allowed_pairs(seg_row, seg_col, joint.shape[0])
    for start in range(0, width, HEAD_DIM):
        head = pl.ds(start, HEAD_DIM)
        query, key, value = (joint[:, pl.ds(c * width + start, HEAD_DIM)] for c in range(3))
        prob = probabilities(query, key, allowed)
        attended[:, head] = mul(prob.astype(BF16), value).astype(BF16)
    partial[...] = mul(attended[...], out_weight[...]).astype(BF16)


def attend_back_kernel(
    width, joint, seg_row, seg_col, out_weight, attended, branch, d_joint, grad_out, d_attended
):
    allowed = allowed_pairs(seg_row, seg_col, joint.shape[0])
    d_attended[...] = mul(branch[...], out_weight[...], COLS_COLS).astype(BF16)
    for start in range(0, width, HEAD_DIM):
        query, key, value = (joint[:, pl.ds(c * width + start, HEAD_DIM)] for c in range(3))
        d_out = d_attended[:, pl.ds(start, HEAD_DIM)]
        prob = probabilities(query, key, allowed)
        d_joint[:, pl.ds(2 * width + start, HEAD_DIM)] = mul(
            prob.astype(BF16), d_out, ROWS_ROWS
        ).astype(BF16)
        d_prob = mul(d_out, value, COLS_COLS)
        row_delta = jnp.sum(d_prob * prob, axis=-1, keepdims=True)
        d_raw = (prob * (d_prob - row_delta) * SCALE).astype(BF16)
        d_joint[:, pl.ds(start, HEAD_DIM)] = mul(d_raw, key).astype(BF16)
        d_joint[:, pl.ds(width + start, HEAD_DIM)] = mul(d_raw, query, ROWS_ROWS).astype(BF16)
    grad_out[...] = mul(attended[...], branch[...], ROWS_ROWS).astype(BF16)


def local(
    dp_size,
    mp_size,
    inputs,
    segment_ids,
    cotangent,
    query_key_value,
    attention_out,
    expand_weight,
    contract_weight,
    norm_params,
    first_query_key_value,
    first_attention_out,
    first_expand_weight,
    first_contract_weight,
    first_norm_params,
    second_query_key_value,
    second_attention_out,
    second_expand_weight,
    second_contract_weight,
    second_norm_params,
):
    params = (query_key_value, attention_out, expand_weight, contract_weight, norm_params)
    firsts = (
        first_query_key_value,
        first_attention_out,
        first_expand_weight,
        first_contract_weight,
        first_norm_params,
    )
    seconds = (
        second_query_key_value,
        second_attention_out,
        second_expand_weight,
        second_contract_weight,
        second_norm_params,
    )
    chips = dp_size // 2
    pair, plane, column, cross, row, everyone = (
        Group(kind, dp_size, mp_size)
        for kind in ("pair", "plane", "column", "cross", "row", "all")
    )
    dp, mp = lax.axis_index("dp"), lax.axis_index("mp")
    core = dp % 2
    length, model = inputs.shape
    width = query_key_value.shape[2]
    shard = query_key_value.shape[1]
    slab = 2 * shard
    hidden_units = expand_weight.shape[1]
    own_units = contract_weight.shape[0]
    units = 2 * own_units
    out_rows = attention_out.shape[0]
    strip = length // mp_size
    tokens = chips * length

    (norm_all,) = exchange(
        row,
        [norm_params],
        [shape((dp_size, 4, shard), F32)],
        [lambda ins, outs, me, other: (ins[0], outs[0].at[me])],
        0,
    )
    norm_weights = jnp.swapaxes(norm_all.astype(BF16).astype(F32), 0, 1).reshape(4, model)

    def shared(column_block):
        def move(ins, outs, me, other):
            return (ins[0].at[column_block], outs[0].at[part(me, shard), pl.ds(column_block * width, width)])

        return move

    joint_weight, expand_pair, contract_pair = exchange(
        pair,
        [query_key_value.astype(BF16), expand_weight.astype(BF16), contract_weight.astype(BF16)],
        [shape((slab, 3 * width)), shape((slab, hidden_units)), shape((units, model))],
        [
            shared(0),
            shared(1),
            shared(2),
            lambda ins, outs, me, other: (ins[1], outs[1].at[part(me, shard), :]),
            lambda ins, outs, me, other: (ins[2], outs[2].at[part(me, own_units), :]),
        ],
        1,
    )
    (output_all,) = exchange(
        row,
        [attention_out.astype(BF16)],
        [shape((dp_size * out_rows, model))],
        [lambda ins, outs, me, other: (ins[0], outs[0].at[part(me, out_rows), :])],
        2,
    )
    (grad_rows,) = exchange(
        plane,
        [cotangent],
        [shape((chips, length, model))],
        [lambda ins, outs, me, other: (ins[0], outs[0].at[me])],
        3,
    )
    grad_rows = grad_rows.reshape(tokens, model)

    values = inputs.astype(F32)
    normed = layer_norm(values, norm_weights[0], norm_weights[1]).astype(BF16)
    (normed_low,) = exchange(
        plane,
        [normed],
        [shape((chips, length, slab))],
        [lambda ins, outs, me, other: (ins[0].at[:, part(other, slab)], outs[0].at[me])],
        4,
    )
    normed_low = normed_low.reshape(tokens, slab)
    joint_part = mul(normed_low, joint_weight).astype(BF16).reshape(chips, length, 3 * width)
    (joint_parts,) = exchange(
        plane,
        [joint_part],
        [shape((chips, length, 3 * width))],
        [lambda ins, outs, me, other: (ins[0].at[other], outs[0].at[me])],
        5,
    )
    joint = jnp.sum(joint_parts.astype(F32), axis=0).astype(BF16)

    seg_row = segment_ids
    seg_col = segment_ids.reshape(length, 1)
    attended, branch_part = pl.pallas_call(
        functools.partial(attend_kernel, width),
        out_shape=[shape((length, width)), shape((length, model))],
        compiler_params=pltpu.CompilerParams(vmem_limit_bytes=48 * 2**20),
    )(joint, seg_row, seg_col, output_all)

    (branch_parts,) = exchange(
        column,
        [branch_part.reshape(mp_size, strip, model)],
        [shape((mp_size, strip, model))],
        [lambda ins, outs, me, other: (ins[0].at[other], outs[0].at[me])],
        6,
    )
    own_values = lax.dynamic_slice_in_dim(values, mp * strip, strip, 0)
    hidden = own_values + jnp.sum(branch_parts.astype(F32), axis=0)
    normed_two, pull_two = jax.vjp(layer_norm, hidden, norm_weights[2], norm_weights[3])
    (second_low,) = exchange(
        cross,
        [normed_two.astype(BF16)],
        [shape((chips * mp_size, strip, slab))],
        [
            lambda ins, outs, me, other: (
                ins[0].at[:, part(lax.div(other, mp_size), slab)],
                outs[0].at[me],
            )
        ],
        7,
    )
    second_low = second_low.reshape(tokens, slab)
    pre_part = mul(second_low, expand_pair).astype(BF16)
    (pre_parts,) = exchange(
        plane,
        [pre_part],
        [shape((chips, tokens, units))],
        [lambda ins, outs, me, other: (ins[0].at[:, part(other, units)], outs[0].at[me])],
        8,
    )
    pre_gelu = jnp.sum(pre_parts.astype(F32), axis=0)
    activated, pull_gelu = jax.vjp(gelu_tanh, pre_gelu)
    activated_low = activated.astype(BF16)
    d_activated = mul(grad_rows, contract_pair, COLS_COLS)
    (d_pre,) = pull_gelu(d_activated)
    (d_pre_all,) = exchange(
        plane,
        [d_pre.astype(BF16)],
        [shape((tokens, hidden_units))],
        [lambda ins, outs, me, other: (ins[0], outs[0].at[:, part(me, units)])],
        9,
    )

    def scatter_rows(partial, collective_id):
        (blocks,) = exchange(
            cross,
            [partial.reshape(chips * mp_size, strip, slab)],
            [shape((chips * mp_size, strip, slab))],
            [lambda ins, outs, me, other: (ins[0].at[other], outs[0].at[me])],
            collective_id,
        )
        total = jnp.sum(blocks.reshape(chips, mp_size, strip, slab).astype(F32), axis=1)
        return jnp.swapaxes(total, 0, 1).reshape(strip, model)

    d_normed_two = scatter_rows(mul(d_pre_all, expand_pair, COLS_COLS).astype(BF16), 10)
    d_hidden_norm, gain_two, shift_two = pull_two(d_normed_two)
    own_grad = lax.dynamic_slice_in_dim(cotangent, mp * strip, strip, 0).astype(F32)
    d_hidden = own_grad + d_hidden_norm

    def gather_rows(block, collective_id):
        (rows,) = exchange(
            column,
            [block],
            [shape((mp_size, strip, model))],
            [lambda ins, outs, me, other: (ins[0], outs[0].at[me])],
            collective_id,
        )
        return rows.reshape(length, model)

    branch_grad = gather_rows(d_hidden.astype(BF16), 11)
    d_joint, grad_output_part, _ = pl.pallas_call(
        functools.partial(attend_back_kernel, width),
        out_shape=[shape((length, 3 * width)), shape((width, model)), shape((length, width))],
        compiler_params=pltpu.CompilerParams(vmem_limit_bytes=48 * 2**20),
    )(joint, seg_row, seg_col, output_all, attended, branch_grad)
    (d_joint_all,) = exchange(
        plane,
        [d_joint],
        [shape((chips, length, 3 * width))],
        [lambda ins, outs, me, other: (ins[0], outs[0].at[me])],
        12,
    )
    d_joint_all = d_joint_all.reshape(tokens, 3 * width)
    d_normed_one = scatter_rows(mul(d_joint_all, joint_weight, COLS_COLS).astype(BF16), 13)
    _, pull_one = jax.vjp(layer_norm, own_values, norm_weights[0], norm_weights[1])
    d_values_norm, gain_one, shift_one = pull_one(d_normed_one)
    input_grad = gather_rows((d_hidden + d_values_norm).astype(BF16), 14).astype(F32)

    out_part = mul(activated_low, contract_pair).astype(BF16).reshape(chips, length, model)
    (out_parts,) = exchange(
        plane,
        [out_part],
        [shape((chips, length, model))],
        [lambda ins, outs, me, other: (ins[0].at[other], outs[0].at[me])],
        15,
    )
    out_rows_sum = jnp.sum(out_parts.astype(F32), axis=0).astype(BF16)
    (out_strips,) = exchange(
        column,
        [out_rows_sum.reshape(mp_size, strip, model)],
        [shape((mp_size, strip, model))],
        [lambda ins, outs, me, other: (ins[0].at[other], outs[0].at[me])],
        16,
    )
    layer_output = gather_rows(
        (hidden + jnp.sum(out_strips.astype(F32), axis=0)).astype(BF16), 17
    )

    (grad_output_parts,) = exchange(
        row,
        [grad_output_part.reshape(dp_size, out_rows, model)],
        [shape((dp_size, out_rows, model))],
        [lambda ins, outs, me, other: (ins[0].at[other], outs[0].at[me])],
        18,
    )
    reduced_output = jnp.sum(grad_output_parts.astype(F32), axis=0)
    own_joint, other_joint = [], []
    grad_joint = mul(normed_low, d_joint_all, ROWS_ROWS)
    grad_expand = mul(second_low, d_pre_all, ROWS_ROWS)
    grad_contract = mul(activated_low, grad_rows, ROWS_ROWS)

    def halves(array, index):
        return lax.dynamic_slice_in_dim(array, index * (array.shape[0] // 2), array.shape[0] // 2, 0)

    pieces = (grad_joint, grad_expand, grad_contract)
    sent = [halves(entry, 1 - core).astype(BF16) for entry in pieces]
    got = exchange_pair(pair, sent, 19)
    reduced_joint, reduced_expand, reduced_contract = (
        halves(entry, core) + other.astype(F32) for entry, other in zip(pieces, got)
    )
    reduced_joint = jnp.swapaxes(reduced_joint.reshape(shard, 3, width), 0, 1)

    zero_row = jnp.zeros((model,), F32)
    norm_rows = jnp.stack([gain_one, shift_one, gain_two, shift_two] + [zero_row] * 4)
    norm_rows = jnp.swapaxes(norm_rows.reshape(8, dp_size, shard), 0, 1)
    (norm_parts,) = exchange(
        everyone,
        [norm_rows],
        [shape((dp_size * mp_size, 8, shard), F32)],
        [
            lambda ins, outs, me, other: (
                ins[0].at[lax.div(other, mp_size)],
                outs[0].at[me],
            )
        ],
        20,
    )
    reduced_norms = jnp.sum(norm_parts, axis=0)[:4]

    grads = (reduced_joint, reduced_output, reduced_expand, reduced_contract, reduced_norms)
    squares = sum((jnp.sum(entry * entry) for entry in grads[:4])) + jnp.sum(
        reduced_norms * reduced_norms
    ) / mp_size
    (square_parts,) = exchange(
        everyone,
        [jnp.full((8, 128), squares, F32)],
        [shape((dp_size * mp_size, 8, 128), F32)],
        [lambda ins, outs, me, other: (ins[0], outs[0].at[me])],
        21,
    )
    gradient_norm = jnp.sqrt(jnp.sum(square_parts[:, 0, 0]))
    clip_factor = jnp.minimum(1.0, MAX_NORM / (gradient_norm + CLIP_EPSILON))
    updates = [
        adam_update(params[k], grads[k], firsts[k], seconds[k], LEARN_RATES[k], clip_factor)
        for k in range(5)
    ]
    copies = [entry[2].astype(BF16) for entry in updates]
    return (
        layer_output,
        input_grad,
        *grads,
        *[entry[0] for entry in updates],
        *[entry[1] for entry in updates],
        *[entry[2] for entry in updates],
        *copies,
        gradient_norm,
    )


def exchange_pair(pair, sent, collective_id):
    moves = [
        lambda ins, outs, me, other, lane=lane: (ins[lane], outs[lane]) for lane in range(len(sent))
    ]
    return swap(pair, sent, moves, collective_id)


def swap(pair, sent, moves, collective_id):
    count = len(sent)

    def kernel(*refs):
        ins, outs = refs[:count], refs[count : 2 * count]
        send_sems, recv_sems = refs[2 * count :]
        other = pair.device(1 - pair.me())
        barrier = pltpu.get_barrier_semaphore()
        pl.semaphore_signal(barrier, inc=1, device_id=other, device_id_type=pl.DeviceIdType.MESH)
        pl.semaphore_wait(barrier, 1)
        copies = [
            pltpu.make_async_remote_copy(
                src_ref=ins[lane],
                dst_ref=outs[lane],
                send_sem=send_sems.at[lane],
                recv_sem=recv_sems.at[lane],
                device_id=other,
                device_id_type=pl.DeviceIdType.MESH,
            )
            for lane in range(count)
        ]
        for copy in copies:
            copy.start()
        for copy in copies:
            copy.wait()

    any_space = pl.BlockSpec(memory_space=pl.ANY)
    return pl.pallas_call(
        kernel,
        out_shape=[shape(entry.shape, entry.dtype) for entry in sent],
        in_specs=[any_space] * count,
        out_specs=[any_space] * count,
        scratch_shapes=[pltpu.SemaphoreType.DMA((count,)), pltpu.SemaphoreType.DMA((count,))],
        compiler_params=pltpu.CompilerParams(collective_id=collective_id, has_side_effects=True),
    )(*sent)


def solution(mesh):
    rows = P("dp", None)
    sets = (
        P(None, "dp", "mp"),
        P(("mp", "dp"), None),
        P("dp", "mp"),
        P(("mp", "dp"), None),
        P(None, "dp"),
    )
    return jax.shard_map(
        functools.partial(local, mesh.shape["dp"], mesh.shape["mp"]),
        mesh=mesh,
        in_specs=(rows, rows, rows) + sets * 3,
        out_specs=(rows, rows) + sets * 5 + (P(),),
        check_vma=False,
    )
```

time: 908 us -> 594 us (0.65)
  waiting for transfers between devices: 681 us -> 0 us
  Pallas kernels: 0 us -> 453 us
  blocking collectives: 49.9 us -> 0 us
  matrix products: 72.7 us -> 28.3 us
  other arithmetic: 51.4 us -> 67.8 us
  between operations: 20 us -> 6.44 us
    pallas_call x0 -> x24, Pallas kernels: none -> 453 us  [the longest x21 443 us: exchange(): pl.pallas_call(kernel, out_shape=results, in_specs=[any_space] * count, o...]
    reduce_scatter x4 -> x0, waiting for transfers between devices: 373 us -> none  [the longest x1 117 us: local(): lax.psum_scatter(grad_contract, 'dp', scatter_dimension=0, tiled=True)]
    all_gather x4 -> x0, waiting for transfers between devices: 164 us -> none  [the longest x1 53.1 us: local(): lax.all_gather(contract_weight.astype(jnp.bfloat16), 'dp', axis=0, tiled=...]
    psum x3 -> x0, waiting for transfers between devices: 144 us -> none  [the longest x1 51.7 us: local(): lax.psum(jnp.dot(activated_low, contract_full, preferred_element_type=jnp...]
    dot_general x18 -> x9, matrix products: 72.7 us -> 28.3 us  [mul(): return lax.dot_general(left, right, dims, preferred_element_type=F32)]
    psum x1 -> x0, blocking collectives: 39.5 us -> none  [local(): gradient_norm = jnp.sqrt(lax.psum(squares, ('dp', 'mp')))]
    reduce_sum x1 -> x11, other arithmetic: 0.61 us -> 17.1 us  [the longest x1 2.92 us: local(): out_rows_sum = jnp.sum(out_parts.astype(F32), axis=0).astype(BF16)]
    all_gather x1 -> x0, blocking collectives: 10.4 us -> none  [local(): lax.all_gather(norm_params.astype(jnp.bfloat16), 'dp', axis=1, tiled=True)]
  transfers between devices with their start and end apart: 12 -> 0, of which waited for: 11 -> 0; matrix products, arithmetic and copies ran while one was open for 9% -> 0% of each run, Pallas kernels for 0% -> 0%
where the time goes in v1:
time: 594 us; the launch traced here: 592 us
  Pallas kernels  453 us (76%)
  other arithmetic  67.8 us (11%)
  local copies, waits for them, and re-layouts  36.6 us (6%)
  matrix products  28.3 us (5%)
  between operations  6.44 us (1%)
    pallas_call x21, Pallas kernels, exchange(): pl.pallas_call(kernel, out_shape=results, in_specs=[any_space] * count, o...  443 us
    unnamed x97, local copies, waits for them, and re-layouts  29.3 us
    dot_general x9, matrix products, mul(): return lax.dot_general(left, right, dims, preferred_element_type=F32)  28.3 us
    convert_element_type x5, other arithmetic, local(): copies = [entry[2].astype(BF16) for entry in updates]  19.4 us

profile of v1, /device:TPU:0, one launch (start us, length us, event | category | flops | bytes accessed | tf_op | source)
XLA Modules:
  0.0 592.4 jit_solution(1524962405663633279)
XLA Ops:
  3.4 6.7 %shard_map.393 = f32[8,4,256]{2,1,0:T(4,128)} custom-call(f32[4,256]{1,0:T(4,128)} %refs_0_.2), custom_call_target="tpu_custom_call" | custom-call | tf_op jit(solution)/shard_map/pallas_call | solution.py:164
  14.6 9.6 %shard_map.394 = bf16[4,128,512]{2,1,0:T(8,128)(2,1)} custom-call(bf16[128,2048]{1,0:T(8,128)(2,1)} %add_convert_fusion.refs_0_), custom_call_target="tpu_custom_call" | custom-call | tf_op jit(solution)/shard_map/pallas_call | solution.py:164
  29.5 3.0 copy.72
  32.5 3.0 copy.73
  37.1 25.8 %shard_map.397.out_weight = bf16[512,2048]{1,0:T(8,128)(2,1)} custom-call(bf16[64,2048]{1,0:T(8,128)(2,1)} %convert_element_type.132.refs_0_), custom_call_target="tpu_custom_call" | custom-call | tf_op jit(solution)/shard_map/pallas_call | solution.py:164
  62.9 25.9 %shard_map.405 = bf16[4,128,2048]{2,1,0:T(8,128)(2,1)} custom-call(bf16[128,2048]{1,0:T(8,128)(2,1)} %refs_0_.3), custom_call_target="tpu_custom_call" | custom-call | tf_op jit(solution)/shard_map/pallas_call | solution.py:164
  88.8 89.2 %shard_map.395 = (bf16[512,1536]{1,0:T(8,128)(2,1)}, bf16[512,2048]{1,0:T(8,128)(2,1)}, bf16[512,2048]{1,0:T(8,128)(2,1)}) custom-call(bf16[3,256,512]{2,1,0:T(8,128)(2,1)} %convert_element_type.128.refs_0_, bf16[256,2048]{1,0:T(8,128)(2,1)} %convert_element_type.129.refs_1_, bf16[256,2048]{1,0:T(8,128)(2,1)} %convert_element_type.130.refs_2_), custom_call_target="tpu_custom_call" | custom-call | tf_op jit(solution)/shard_map/pallas_call | solution.py:164
  178.1 3.5 convolution_convert_fusion
  181.6 21.3 %shard_map.396 = bf16[4,128,1536]{2,1,0:T(8,128)(2,1)} custom-call(bf16[4,128,1536]{2,1,0:T(8,128)(2,1)} %bitcast.87), custom_call_target="tpu_custom_call" | custom-call | tf_op jit(solution)/shard_map/pallas_call | solution.py:164
  204.7 1.8 shard_map.398
  207.3 13.2 %shard_map.399 = bf16[4,32,2048]{2,1,0:T(8,128)(2,1)} custom-call(bf16[4,32,2048]{2,1,0:T(8,128)(2,1)} %bitcast.67), custom_call_target="tpu_custom_call" | custom-call | tf_op jit(solution)/shard_map/pallas_call | solution.py:164
  223.8 17.7 %shard_map.400 = bf16[16,32,512]{2,1,0:T(8,128)(2,1)} custom-call(bf16[32,2048]{1,0:T(8,128)(2,1)} %add_convert_fusion.3.refs_0_), custom_call_target="tpu_custom_call" | custom-call | tf_op jit(solution)/shard_map/pallas_call | solution.py:164
  241.5 4.3 convolution_convert_fusion.2.refs_0_
  245.9 24.0 %shard_map.401 = bf16[4,512,512]{2,1,0:T(8,128)(2,1)} custom-call(bf16[512,2048]{1,0:T(8,128)(2,1)} %convolution_convert_fusion.2.refs_0_), custom_call_target="tpu_custom_call" | custom-call | tf_op jit(solution)/shard_map/pallas_call | solution.py:164
  269.8 2.1 convert_reduce_fusion.1
  272.1 4.6 fusion.9.refs_0_
  276.7 2.7 convolution_convert_fusion.1
  279.4 25.8 %shard_map.402 = bf16[4,128,2048]{2,1,0:T(8,128)(2,1)} custom-call(bf16[4,128,2048]{2,1,0:T(8,128)(2,1)} %bitcast.83), custom_call_target="tpu_custom_call" | custom-call | tf_op jit(solution)/shard_map/pallas_call | solution.py:164
  305.2 2.9 reduce_sum.306
  308.1 12.6 %shard_map.403 = bf16[4,32,2048]{2,1,0:T(8,128)(2,1)} custom-call(bf16[4,32,2048]{2,1,0:T(8,128)(2,1)} %bitcast.84), custom_call_target="tpu_custom_call" | custom-call | tf_op jit(solution)/shard_map/pallas_call | solution.py:164
  320.7 1.8 convert_reduce_fusion.4
  322.5 3.3 fusion.15
  325.9 1.9 copy-done.6
  328.9 25.4 %shard_map.406 = bf16[512,2048]{1,0:T(8,128)(2,1)} custom-call(bf16[512,512]{1,0:T(8,128)(2,1)} %fusion.9.refs_0_), custom_call_target="tpu_custom_call" | custom-call | tf_op jit(solution)/shard_map/pallas_call | solution.py:164
  354.3 4.3 convolution_convert_fusion.4
  358.6 17.4 %shard_map.407 = bf16[16,32,512]{2,1,0:T(8,128)(2,1)} custom-call(bf16[16,32,512]{2,1,0:T(8,128)(2,1)} %bitcast.88), custom_call_target="tpu_custom_call" | custom-call | tf_op jit(solution)/shard_map/pallas_call | solution.py:164
  381.0 11.4 %shard_map.408 = bf16[4,32,2048]{2,1,0:T(8,128)(2,1)} custom-call(bf16[32,2048]{1,0:T(8,128)(2,1)} %fusion.11.refs_0_), custom_call_target="tpu_custom_call" | custom-call | tf_op jit(solution)/shard_map/pallas_call | solution.py:164
  393.4 3.0 shard_map.409
  398.5 25.0 %shard_map.414 = bf16[8,64,2048]{2,1,0:T(8,128)(2,1)} custom-call(bf16[8,64,2048]{2,1,0:T(8,128)(2,1)} %bitcast.65), custom_call_target="tpu_custom_call" | custom-call | tf_op jit(solution)/shard_map/pallas_call | solution.py:164
  423.5 2.0 convert_reduce_fusion
  427.1 15.3 %shard_map.404 = bf16[4,32,2048]{2,1,0:T(8,128)(2,1)} custom-call(bf16[32,2048]{1,0:T(8,128)(2,1)} %get-tuple-element.141.refs_0_), custom_call_target="tpu_custom_call" | custom-call | tf_op jit(solution)/shard_map/pallas_call | solution.py:164
  442.3 21.0 %shard_map.410 = bf16[4,128,1536]{2,1,0:T(8,128)(2,1)} custom-call(bf16[128,1536]{1,0:T(8,128)(2,1)} %copy-done.4), custom_call_target="tpu_custom_call" | custom-call | tf_op jit(solution)/shard_map/pallas_call | solution.py:164
  463.4 3.2 convolution_convert_fusion.3
  466.6 18.1 %shard_map.411 = bf16[16,32,512]{2,1,0:T(8,128)(2,1)} custom-call(bf16[16,32,512]{2,1,0:T(8,128)(2,1)} %bitcast.89), custom_call_target="tpu_custom_call" | custom-call | tf_op jit(solution)/shard_map/pallas_call | solution.py:164
  490.0 12.5 %shard_map.415 = f32[32,8,256]{2,1,0:T(8,128)} custom-call(f32[8,8,256]{2,1,0:T(8,128)} %bitcast.90), custom_call_target="tpu_custom_call" | custom-call | tf_op jit(solution)/shard_map/pallas_call | solution.py:164
  504.7 13.0 %shard_map.412 = bf16[4,32,2048]{2,1,0:T(8,128)(2,1)} custom-call(bf16[32,2048]{1,0:T(8,128)(2,1)} %add_convert_fusion.1.refs_0_), custom_call_target="tpu_custom_call" | custom-call | tf_op jit(solution)/shard_map/pallas_call | solution.py:164
  517.7 2.1 bitcast_convert_fusion
  526.2 5.7 shard_map.413
  531.9 4.5 multiply_reduce_fusion
  536.4 2.4 multiply_reduce_fusion.1
  540.3 2.0 copy.71
  546.5 11.8 %shard_map.416 = f32[32,8,128]{2,1,0:T(8,128)} custom-call(f32[8,128]{1,0:T(8,128)} %broadcast_in_dim.25.refs_0_), custom_call_target="tpu_custom_call" | custom-call | tf_op jit(solution)/shard_map/pallas_call | solution.py:164
  561.2 5.1 fusion.24
  567.9 2.4 copy.80
  573.6 3.2 copy.77
  576.7 2.8 fusion.22
  579.6 6.6 %fusion.20 = (bf16[256,2048]{1,0:T(8,128)(2,1)}, f32[256,2048]{1,0:T(8,128)}, f32[256,2048]{1,0:T(8,128)}, f32[256,2048]{1,0:T(8,128)}) fusion(f32[256,2048]{1,0:T(8,128)S(1)} %copy-done.11, f32[256,2048]{1,0:T(8,128)S(1)} %copy-done.15, f32[]{:T(128)S(6)} %min.3, f32[256,2048]{1,0:T(8,128)} %param.33, f32[256,2048]{1,0:T(8,128)} %param.28), kind=kLoop, calls=%fused_computation.93 | loop fusion | flops 8912896 | bytes 15728644 | tf_op jit(solution)/shard_map/convert_element_type | solution.py:522
  586.3 4.2 fusion.18
  (147 shorter events, 54.4 us)
Async XLA Ops:
  0.7 12.8 %copy-start.17 = (bf16[128,2048]{1,0:T(8,128)(2,1)S(1)}, bf16[128,2048]{1,0:T(8,128)(2,1)}, u32[]{:S(2)}) copy-start(bf16[128,2048]{1,0:T(8,128)(2,1)} %param.18) | copy-start | bytes 1572868
  0.7 23.6 %copy-start.18 = (f32[3,256,512]{2,1,0:T(8,128)S(1)}, f32[3,256,512]{2,1,0:T(8,128)}, u32[]{:S(2)}) copy-start(f32[3,256,512]{2,1,0:T(8,128)} %param.21) | copy-start | bytes 4718596
  24.3 2.2 copy-start.10
  25.4 1.0 copy-start.26
  26.4 2.0 copy-start.12
  88.8 89.2 %copy-start.32 = (bf16[4,128,512]{2,1,0:T(8,128)(2,1)S(1)}, bf16[4,128,512]{2,1,0:T(8,128)(2,1)}, u32[]{:S(2)}) copy-start(bf16[4,128,512]{2,1,0:T(8,128)(2,1)} %shard_map.394) | copy-start | bytes 1572868
  181.6 23.0 %copy-start = (bf16[512,2048]{1,0:T(8,128)(2,1)S(1)}, bf16[512,2048]{1,0:T(8,128)(2,1)}, u32[]{:S(2)}) copy-start(bf16[512,2048]{1,0:T(8,128)(2,1)} %shard_map.397.out_weight) | copy-start | bytes 6291460
  181.6 23.0 %copy-start.5 = (s32[1,128]{1,0:T(1,128)S(1)}, s32[1,128]{1,0:T(1,128)}, u32[]{:S(2)}) copy-start(s32[1,128]{1,0:T(1,128)} %seg_row.3) | copy-start | bytes 1540
  206.5 0.8 copy-start.3
  269.8 2.2 copy-start.9
  272.1 4.6 copy-start.25
  272.1 4.6 copy-start.42
  325.9 1.9 copy-start.6
  392.3 1.0 copy-start.2
  396.4 1.3 copy-start.1
  397.7 0.7 copy-start.4
  425.5 0.8 copy-start.23
  426.3 37.0 %copy-start.43 = (bf16[512,1536]{1,0:T(8,128)(2,1)S(1)}, bf16[512,1536]{1,0:T(8,128)(2,1)}, u32[]{:S(2)}) copy-start(bf16[512,1536]{1,0:T(8,128)(2,1)} %get-tuple-element.38) | copy-start | bytes 4718596
  466.6 19.3 %copy-start.27 = (f32[128,2048]{1,0:T(8,128)S(1)}, f32[128,2048]{1,0:T(8,128)}, u32[]{:S(2)}) copy-start(f32[128,2048]{1,0:T(8,128)} %copy-done.26) | copy-start | bytes 3145732
  485.9 1.0 copy-start.28
  486.9 33.0 %copy-start.16 = (bf16[512,2048]{1,0:T(8,128)(2,1)S(1)}, bf16[512,2048]{1,0:T(8,128)(2,1)}, u32[]{:S(2)}) copy-start(bf16[512,2048]{1,0:T(8,128)(2,1)} %shard_map.406) | copy-start | bytes 6291460
  488.2 31.6 %copy-start.35 = (bf16[16,32,512]{2,1,0:T(8,128)(2,1)S(1)}, bf16[16,32,512]{2,1,0:T(8,128)(2,1)}, u32[]{:S(2)}) copy-start(bf16[16,32,512]{2,1,0:T(8,128)(2,1)} %shard_map.400) | copy-start | bytes 1572868
  504.1 56.5 %copy-start.39 = (f32[4,256]{1,0:T(4,128)}, f32[4,256]{1,0:T(4,128)S(1)}, u32[]{:S(2)}) copy-start(f32[4,256]{1,0:T(4,128)S(1)} %get-tuple-element.182) | copy-start | bytes 12292
  521.1 4.1 copy-start.7
  521.2 2.5 copy-start.19
  521.2 3.0 copy-start.33
  531.9 4.6 copy-start.8
  531.9 4.6 copy-start.36
  536.4 2.4 copy-start.37
  540.2 20.3 %copy-start.38 = (f32[4,256]{1,0:T(4,128)S(1)}, f32[4,256]{1,0:T(4,128)}, u32[]{:S(2)}) copy-start(f32[4,256]{1,0:T(4,128)} %refs_0_.2) | copy-start | bytes 12292
  540.2 20.3 %copy-start.40 = (f32[4,256]{1,0:T(4,128)S(1)}, f32[4,256]{1,0:T(4,128)}, u32[]{:S(2)}) copy-start(f32[4,256]{1,0:T(4,128)} %param.35) | copy-start | bytes 12292
  540.2 20.3 %copy-start.41 = (f32[4,256]{1,0:T(4,128)S(1)}, f32[4,256]{1,0:T(4,128)}, u32[]{:S(2)}) copy-start(f32[4,256]{1,0:T(4,128)} %param.30) | copy-start | bytes 12292
  540.2 20.9 %copy-start.20 = (f32[3,256,512]{1,2,0:T(8,128)S(1)}, f32[3,256,512]{1,2,0:T(8,128)}, u32[]{:S(2)}) copy-start(f32[3,256,512]{1,2,0:T(8,128)} %copy.72) | copy-start | bytes 4718596
  566.3 4.0 copy-start.22
  567.9 4.0 copy-start.21
  573.6 3.2 copy-start.24
  573.6 3.2 copy-start.31
  573.6 6.0 %copy-start.15 = (f32[256,2048]{1,0:T(8,128)S(1)}, f32[256,2048]{1,0:T(8,128)}, u32[]{:S(2)}) copy-start(f32[256,2048]{1,0:T(8,128)} %get-tuple-element.180) | copy-start | bytes 6291460
  576.7 2.8 copy-start.11
  579.6 6.6 %copy-start.13 = (f32[256,2048]{1,0:T(8,128)S(1)}, f32[256,2048]{1,0:T(8,128)}, u32[]{:S(2)}) copy-start(f32[256,2048]{1,0:T(8,128)} %param.24) | copy-start | bytes 6291460
  579.6 6.6 %copy-start.14 = (f32[256,2048]{1,0:T(8,128)S(1)}, f32[256,2048]{1,0:T(8,128)}, u32[]{:S(2)}) copy-start(f32[256,2048]{1,0:T(8,128)} %get-tuple-element.181) | copy-start | bytes 6291460
  579.6 6.6 %copy-start.29 = (f32[256,2048]{1,0:T(8,128)S(1)}, f32[256,2048]{1,0:T(8,128)}, u32[]{:S(2)}) copy-start(f32[256,2048]{1,0:T(8,128)} %param.34) | copy-start | bytes 6291460
  579.6 6.6 %copy-start.30 = (f32[256,2048]{1,0:T(8,128)S(1)}, f32[256,2048]{1,0:T(8,128)}, u32[]{:S(2)}) copy-start(f32[256,2048]{1,0:T(8,128)} %param.29) | copy-start | bytes 6291460
  586.3 4.3 copy-start.34

commit v2 on v1

--- a/solution.py
+++ b/solution.py
@@ -1,5 +1,6 @@
 import functools
 import math
+from types import SimpleNamespace
 
 import jax
 import jax.numpy as jnp
@@ -56,46 +57,56 @@
     return (new_first, new_second, new_weight)
 
 
+PAIR, PLANE, COLUMN, CROSS, ROW, ALL = (
+    "pair",
+    "plane",
+    "column",
+    "cross",
+    "row",
+    "all",
+)
+
+
 class Group:
     def __init__(self, kind, dp_size, mp_size):
         self.kind = kind
         self.mp_size = mp_size
         chips = dp_size // 2
         self.size = {
-            "pair": 2,
-            "plane": chips,
-            "column": mp_size,
-            "cross": chips * mp_size,
-            "row": dp_size,
-            "all": dp_size * mp_size,
+            PAIR: 2,
+            PLANE: chips,
+            COLUMN: mp_size,
+            CROSS: chips * mp_size,
+            ROW: dp_size,
+            ALL: dp_size * mp_size,
         }[kind]
 
     def me(self):
         dp, mp = lax.axis_index("dp"), lax.axis_index("mp")
-        if self.kind == "pair":
+        if self.kind == PAIR:
             return lax.rem(dp, 2)
-        if self.kind == "plane":
+        if self.kind == PLANE:
             return lax.div(dp, 2)
-        if self.kind == "column":
+        if self.kind == COLUMN:
             return mp
-        if self.kind == "cross":
+        if self.kind == CROSS:
             return lax.div(dp, 2) * self.mp_size + mp
-        if self.kind == "row":
+        if self.kind == ROW:
             return dp
         return dp * self.mp_size + mp
 
     def device(self, member):
         dp, mp = lax.axis_index("dp"), lax.axis_index("mp")
         core = lax.rem(dp, 2)
-        if self.kind == "pair":
+        if self.kind == PAIR:
             return (dp - core + member, mp)
-        if self.kind == "plane":
+        if self.kind == PLANE:
             return (member * 2 + core, mp)
-        if self.kind == "column":
+        if self.kind == COLUMN:
             return (dp, member)
-        if self.kind == "cross":
+        if self.kind == CROSS:
             return (lax.div(member, self.mp_size) * 2 + core, lax.rem(member, self.mp_size))
-        if self.kind == "row":
+        if self.kind == ROW:
             return (member, mp)
         return (lax.div(member, self.mp_size), lax.rem(member, self.mp_size))
 
@@ -225,7 +236,7 @@
     grad_out[...] = mul(attended[...], branch[...], ROWS_ROWS).astype(BF16)
 
 
-def local(
+def local_steps(
     dp_size,
     mp_size,
     inputs,
@@ -265,7 +276,7 @@
     chips = dp_size // 2
     pair, plane, column, cross, row, everyone = (
         Group(kind, dp_size, mp_size)
-        for kind in ("pair", "plane", "column", "cross", "row", "all")
+        for kind in (PAIR, PLANE, COLUMN, CROSS, ROW, ALL)
     )
     dp, mp = lax.axis_index("dp"), lax.axis_index("mp")
     core = dp % 2
@@ -576,6 +587,659 @@
     )(*sent)
 
 
+class Lane:
+    def __init__(self, group, me, sems, view):
+        self.group, self.me, self.view = group, me, view
+        self.send_sems, self.recv_sems = sems
+        self.size = group.size
+
+    def copy(self, step):
+        to = lax.rem(self.me + step, self.size)
+        return pltpu.make_async_remote_copy(
+            src_ref=self.view(self.me, to)[0],
+            dst_ref=self.view(self.me, to)[1],
+            send_sem=self.send_sems.at[step],
+            recv_sem=self.recv_sems.at[step],
+            device_id=self.group.device(to),
+            device_id_type=pl.DeviceIdType.MESH,
+        )
+
+    def start(self, step):
+        self.copy(step).start()
+
+    def start_all(self):
+        repeat(1, self.size, self.start)
+
+    def source(self, step):
+        return lax.rem(self.me + self.size - step, self.size)
+
+    def take(self, step):
+        to = lax.rem(self.me + step, self.size)
+        pltpu.make_async_remote_copy(
+            src_ref=self.view(self.me, to)[0],
+            dst_ref=self.view(self.source(step), self.me)[1],
+            send_sem=self.send_sems.at[step],
+            recv_sem=self.recv_sems.at[step],
+            device_id=self.group.device(to),
+            device_id_type=pl.DeviceIdType.MESH,
+        ).wait_recv()
+
+    def take_all(self):
+        repeat(1, self.size, self.take)
+
+    def sent(self, step):
+        self.copy(step).wait_send()
+
+    def sent_all(self):
+        repeat(1, self.size, self.sent)
+
+
+def standardise(values):
+    row_mean = jnp.mean(values, axis=-1, keepdims=True)
+    centered = values - row_mean
+    spread = jnp.mean(centered * centered, axis=-1, keepdims=True)
+    return centered, lax.rsqrt(spread + NORM_EPSILON)
+
+
+def norm_back(grad, values, gain_row):
+    centered, inverse = standardise(values)
+    unit = centered * inverse
+    scaled = grad * gain_row
+    inner = jnp.mean(scaled * unit, axis=-1, keepdims=True)
+    back = inverse * (scaled - jnp.mean(scaled, axis=-1, keepdims=True) - unit * inner)
+    gain_grad = jnp.sum(grad * unit, axis=0, keepdims=True)
+    shift_grad = jnp.sum(grad, axis=0, keepdims=True)
+    return back, gain_grad, shift_grad
+
+
+ROOT = math.sqrt(2.0 / math.pi)
+CUBE = 0.044715
+
+LANES = dict(
+    norms=ROW,
+    normed=PLANE,
+    joint_weight=PAIR,
+    out_own=PAIR,
+    out_plane=PLANE,
+    out_pass=PLANE,
+    joint=PLANE,
+    expand=PAIR,
+    contract=PAIR,
+    cotangent=PLANE,
+    branch=COLUMN,
+    second=CROSS,
+    pre=PLANE,
+    d_pre=PLANE,
+    g_contract=PAIR,
+    d_second=CROSS,
+    out=PLANE,
+    g_expand=PAIR,
+    d_hidden=COLUMN,
+    d_joint=PLANE,
+    g_out=PLANE,
+    g_out_pair=PAIR,
+    out_strip=COLUMN,
+    d_first=CROSS,
+    g_joint=PAIR,
+    out_rows=COLUMN,
+    in_rows=COLUMN,
+    g_norms=CROSS,
+    g_norms_pair=PAIR,
+)
+
+
+def layer(dp_size, mp_size, operands):
+    x, segments, cotangent, joint_w, out_w, expand_w, contract_w, norms = operands
+    chips = dp_size // 2
+    groups = SimpleNamespace(
+        **{kind: Group(kind, dp_size, mp_size) for kind in (PAIR, PLANE, COLUMN, CROSS, ROW)}
+    )
+    length, model = x.shape
+    width, shard = joint_w.shape[2], joint_w.shape[1]
+    slab = 2 * shard
+    hidden = expand_w.shape[1]
+    own_units = contract_w.shape[0]
+    units = 2 * own_units
+    out_rows = out_w.shape[0]
+    strip = length // mp_size
+    tokens = chips * length
+    wide = 3 * width
+
+    outs = dict(
+        layer_output=shape((length, model)),
+        input_grad=shape((length, model), F32),
+        own_joint=shape((3, shard, width), F32),
+        own_out=shape((out_rows, model), F32),
+        own_expand=shape((shard, hidden), F32),
+        own_contract=shape((own_units, model), F32),
+        own_norms=shape((8, shard), F32),
+    )
+    far = dict(
+        far_joint=shape((3, shard, width)),
+        far_out=shape((out_rows, model)),
+        far_expand=shape((chips, shard, units)),
+        far_contract=shape((own_units, model)),
+    )
+    scratch = dict(
+        norm_all=((dp_size, 4, shard), F32),
+        a_mine=((chips, length, slab), BF16),
+        a_all=((chips, length, slab), BF16),
+        wq=((3, slab, width), BF16),
+        wo=((dp_size, out_rows, model), BF16),
+        wu=((chips, slab, units), BF16),
+        wd=((units, model), BF16),
+        j_send=((chips, length, wide), BF16),
+        j_recv=((chips, length, wide), BF16),
+        joint=((length, wide), BF16),
+        dy_all=((chips, length, model), BF16),
+        attended=((length, width), BF16),
+        b_send=((mp_size, strip, model), BF16),
+        b_recv=((mp_size, strip, model), BF16),
+        hid=((strip, model), F32),
+        c_mine=((chips, strip, slab), BF16),
+        c_all=((chips, mp_size, strip, slab), BF16),
+        u_send=((chips, tokens, units), BF16),
+        u_recv=((chips, tokens, units), BF16),
+        u_acc=((tokens, units), F32),
+        dz=((tokens, units), F32),
+        z=((tokens, units), BF16),
+        du_all=((chips, tokens, units), BF16),
+        y_send=((chips, length, model), BF16),
+        y_recv=((chips, length, model), BF16),
+        gc_send=((own_units, model), BF16),
+        dc_send=((chips, mp_size, strip, slab), BF16),
+        dc_recv=((chips, mp_size, strip, slab), BF16),
+        ge_send=((chips, shard, units), BF16),
+        dh=((strip, model), F32),
+        da_mine=((strip, model), BF16),
+        da_rows=((mp_size, strip, model), BF16),
+        dq_mine=((length, wide), BF16),
+        dq_all=((chips, length, wide), BF16),
+        go_send=((chips, 2, out_rows, model), BF16),
+        go_recv=((chips, 2, out_rows, model), BF16),
+        go_pair=((2, out_rows, model), BF16),
+        y2_send=((mp_size, strip, model), BF16),
+        y2_recv=((mp_size, strip, model), BF16),
+        y_mine=((strip, model), BF16),
+        y_rows=((mp_size, strip, model), BF16),
+        df_send=((chips, mp_size, strip, slab), BF16),
+        df_recv=((chips, mp_size, strip, slab), BF16),
+        gj_send=((3, shard, width), BF16),
+        ig_mine=((strip, model), BF16),
+        ig_rows=((mp_size, strip, model), BF16),
+        gn_send=((chips, 8, slab), F32),
+        gn_recv=((chips * mp_size, 8, slab), F32),
+        gn_pair=((8, shard), F32),
+        gn_far=((8, shard), F32),
+    )
+    in_names = dict(
+        x=0, seg_row=1, seg_col=2, cot=3, f_joint=4, f_out=5, f_expand=6, f_contract=7, norm_own=8
+    )
+    names = list(in_names) + list(outs) + list(far) + list(scratch)
+
+    def kernel(*refs):
+        r = SimpleNamespace(**dict(zip(names, refs)))
+        sems = refs[len(names) :]
+        load_sems = sems[0]
+        dp, mp = lax.axis_index("dp"), lax.axis_index("mp")
+        core, chip = lax.rem(dp, 2), lax.div(dp, 2)
+        mine, other = part(core, shard), part(1 - core, shard)
+        cross_me = groups.cross.me()
+
+        def flat(ref, columns=slice(None)):
+            values = ref[(slice(None),) * (len(ref.shape) - 1) + (columns,)]
+            return values.reshape(-1, values.shape[-1])
+
+        views = dict(
+            norms=lambda s, t: (r.norm_own, r.norm_all.at[s]),
+            normed=lambda s, t: (r.a_mine.at[t], r.a_all.at[s]),
+            joint_weight=lambda s, t: (
+                r.wq.at[:, part(s, shard), :],
+                r.wq.at[:, part(s, shard), :],
+            ),
+            out_own=lambda s, t: (r.wo.at[dp - core + s], r.wo.at[dp - core + s]),
+            out_plane=lambda s, t: (r.wo.at[2 * s + core], r.wo.at[2 * s + core]),
+            joint=lambda s, t: (r.j_send.at[t], r.j_recv.at[s]),
+            expand=lambda s, t: (
+                r.wu.at[:, part(s, shard), :],
+                r.wu.at[:, part(s, shard), :],
+            ),
+            contract=lambda s, t: (
+                r.wd.at[part(s, own_units), :],
+                r.wd.at[part(s, own_units), :],
+            ),
+            cotangent=lambda s, t: (r.cot, r.dy_all.at[s]),
+            branch=lambda s, t: (r.b_send.at[t], r.b_recv.at[s]),
+            second=lambda s, t: (
+                r.c_mine.at[lax.div(t, mp_size)],
+                r.c_all.at[lax.div(s, mp_size), lax.rem(s, mp_size)],
+            ),
+            pre=lambda s, t: (r.u_send.at[t], r.u_recv.at[s]),
+            d_pre=lambda s, t: (r.du_all.at[s], r.du_all.at[s]),
+            g_contract=lambda s, t: (r.gc_send, r.far_contract),
+            d_second=lambda s, t: (
+                r.dc_send.at[lax.div(t, mp_size), lax.rem(t, mp_size)],
+                r.dc_recv.at[lax.div(s, mp_size), lax.rem(s, mp_size)],
+            ),
+            out=lambda s, t: (r.y_send.at[t], r.y_recv.at[s]),
+            g_expand=lambda s, t: (r.ge_send, r.far_expand),
+            d_hidden=lambda s, t: (r.da_mine, r.da_rows.at[s]),
+            d_joint=lambda s, t: (r.dq_mine, r.dq_all.at[s]),
+            g_out=lambda s, t: (r.go_send.at[t], r.go_recv.at[s]),
+            g_out_pair=lambda s, t: (r.go_pair.at[t], r.far_out),
+            out_strip=lambda s, t: (r.y2_send.at[t], r.y2_recv.at[s]),
+            d_first=lambda s, t: (
+                r.df_send.at[lax.div(t, mp_size), lax.rem(t, mp_size)],
+                r.df_recv.at[lax.div(s, mp_size), lax.rem(s, mp_size)],
+            ),
+            g_joint=lambda s, t: (r.gj_send, r.far_joint),
+            out_rows=lambda s, t: (r.y_mine, r.y_rows.at[s]),
+            in_rows=lambda s, t: (r.ig_mine, r.ig_rows.at[s]),
+            g_norms=lambda s, t: (r.gn_send.at[lax.div(t, mp_size)], r.gn_recv.at[s]),
+            g_norms_pair=lambda s, t: (r.gn_pair, r.gn_far),
+        )
+        lane = SimpleNamespace()
+        pass_sems = None
+        for index, (name, kind) in enumerate(LANES.items()):
+            pair_sems = (sems[1 + 2 * index], sems[2 + 2 * index])
+            if name in views:
+                group = vars(groups)[kind]
+                setattr(lane, name, Lane(group, group.me(), pair_sems, views[name]))
+            else:
+                pass_sems = pair_sems
+
+        def passing(step, to_me):
+            block = r.wo.at[2 * lane.out_plane.source(step) + (1 - core if to_me else core)]
+            return pltpu.make_async_remote_copy(
+                src_ref=block,
+                dst_ref=block,
+                send_sem=pass_sems[0].at[step],
+                recv_sem=pass_sems[1].at[step],
+                device_id=(dp + 1 - 2 * core, mp),
+                device_id_type=pl.DeviceIdType.MESH,
+            )
+
+        loads = [
+            pltpu.make_async_copy(source, target, load_sems.at[i])
+            for i, (source, target) in enumerate(
+                (
+                    (r.f_joint, r.own_joint),
+                    (r.f_out, r.own_out),
+                    (r.f_expand, r.own_expand),
+                    (r.f_contract, r.own_contract),
+                )
+            )
+        ]
+        for load in loads:
+            load.start()
+
+        barrier = pltpu.get_barrier_semaphore()
+
+        def greet(device):
+            pl.semaphore_signal(
+                barrier, inc=1, device_id=device, device_id_type=pl.DeviceIdType.MESH
+            )
+
+        cross = groups.cross
+        repeat(1, cross.size, lambda s: greet(cross.device(lax.rem(cross_me + s, cross.size))))
+        repeat(0, chips, lambda s: greet((s * 2 + 1 - core, mp)))
+        pl.semaphore_wait(barrier, cross.size - 1 + chips)
+
+        lane.norms.start_all()
+        r.norm_all[dp] = r.norm_own[...]
+        values = r.x[...].astype(F32)
+        centered, inverse = standardise(values)
+        lane.norms.take_all()
+
+        def norm_row(index, block=None):
+            blocks = range(dp_size) if block is None else (block,)
+            rows = [r.norm_all[b, pl.ds(index, 1), :] for b in blocks]
+            whole = rows[0] if len(rows) == 1 else jnp.concatenate(rows, axis=1)
+            return whole.astype(BF16).astype(F32)
+
+        for b in range(dp_size):
+            columns = slice(b * shard, (b + 1) * shard)
+            r.a_mine[b // 2, :, (b % 2) * shard : (b % 2 + 1) * shard] = (
+                centered[:, columns] * inverse * norm_row(0, b) + norm_row(1, b)
+            ).astype(BF16)
+        lane.normed.start_all()
+        r.a_all[chip] = r.a_mine[chip]
+
+        loads[0].wait()
+        for c in range(3):
+            r.wq[c, mine, :] = r.own_joint[c].astype(BF16)
+        lane.joint_weight.start_all()
+        loads[1].wait()
+        r.wo[dp] = r.own_out[...].astype(BF16)
+        lane.out_plane.start_all()
+        lane.out_own.start_all()
+        lane.joint_weight.take_all()
+
+        def joint_part(block):
+            rows = r.a_all[block]
+            for c in range(3):
+                r.j_send[block, :, c * width : (c + 1) * width] = mul(rows, r.wq[c]).astype(BF16)
+
+        def joint_step(step):
+            lane.normed.take(step)
+            joint_part(lane.normed.source(step))
+            lane.joint.start(chips - step)
+
+        repeat(1, chips, joint_step)
+        joint_part(chip)
+
+        loads[2].wait()
+        for c in range(chips):
+            r.wu[c, mine, :] = r.own_expand[:, c * units : (c + 1) * units].astype(BF16)
+        lane.expand.start_all()
+        loads[3].wait()
+        r.wd[part(core, own_units), :] = r.own_contract[...].astype(BF16)
+        lane.contract.start_all()
+        for step in range(1, chips):
+            lane.out_plane.take(step)
+            passing(step, False).start()
+
+        lane.joint.take_all()
+        lane.cotangent.start_all()
+        total = r.j_send[chip].astype(F32)
+        for step in range(1, chips):
+            total = total + r.j_recv[lane.joint.source(step)].astype(F32)
+        r.joint[...] = total.astype(BF16)
+
+        allowed = allowed_pairs(r.seg_row, r.seg_col, length)
+        probs = []
+        for start in range(0, width, HEAD_DIM):
+            query, key, value = (
+                r.joint[:, c * width + start : c * width + start + HEAD_DIM] for c in range(3)
+            )
+            prob = probabilities(query, key, allowed)
+            r.attended[:, start : start + HEAD_DIM] = mul(prob.astype(BF16), value).astype(BF16)
+
+        lane.out_own.take_all()
+        for step in range(1, chips):
+            passing(step, True).wait_recv()
+        branch = mul(r.attended[...], flat(r.wo)).astype(BF16)
+        for m in range(mp_size):
+            r.b_send[m] = branch[m * strip : (m + 1) * strip]
+        lane.branch.start_all()
+        r.dy_all[chip] = r.cot[...]
+        lane.branch.take_all()
+        here = part(mp, strip)
+        total = r.x[here, :].astype(F32) + r.b_send[mp].astype(F32)
+        for step in range(1, mp_size):
+            total = total + r.b_recv[lane.branch.source(step)].astype(F32)
+        r.hid[...] = total
+        centered, inverse = standardise(total)
+        for b in range(dp_size):
+            columns = slice(b * shard, (b + 1) * shard)
+            r.c_mine[b // 2, :, (b % 2) * shard : (b % 2 + 1) * shard] = (
+                centered[:, columns] * inverse * norm_row(2, b) + norm_row(3, b)
+            ).astype(BF16)
+        lane.second.start_all()
+        r.c_all[chip, mp] = r.c_mine[chip]
+        lane.expand.take_all()
+        lane.contract.take_all()
+        lane.cotangent.take_all()
+        r.dz[...] = mul(flat(r.dy_all), r.wd[...], COLS_COLS)
+        lane.second.take_all()
+
+        def pre_step(step):
+            to = lax.rem(chip + step, chips)
+            r.u_send[to] = mul(flat(r.c_all), r.wu[to]).astype(BF16)
+            lane.pre.start(step)
+
+        repeat(1, chips, pre_step)
+        r.u_acc[...] = mul(flat(r.c_all), r.wu[chip])
+        lane.pre.take_all()
+
+        tile = 64
+
+        def gelu_tile(i, none):
+            rows = part(i, tile)
+            pre = r.u_acc[rows, :]
+            for step in range(1, chips):
+                pre = pre + r.u_recv[lane.pre.source(step), rows, :].astype(F32)
+            square = pre * pre
+            curve = jnp.tanh(ROOT * pre * (1.0 + CUBE * square))
+            half = 0.5 * (1.0 + curve)
+            r.z[rows, :] = (pre * half).astype(BF16)
+            slope = half + 0.5 * pre * (1.0 - curve * curve) * (ROOT * (1.0 + 3.0 * CUBE * square))
+            r.du_all[chip, rows, :] = (r.dz[rows, :] * slope).astype(BF16)
+            return none
+
+        lax.fori_loop(0, tokens // tile, gelu_tile, None)
+        lane.d_pre.start_all()
+
+        for c in range(chips):
+            rows = slice(c * length, (c + 1) * length)
+            r.y_send[c] = mul(r.z[rows, :], r.wd[...]).astype(BF16)
+        r.gc_send[...] = mul(r.z[:, part(1 - core, own_units)], flat(r.dy_all), ROWS_ROWS).astype(BF16)
+        lane.g_contract.start_all()
+
+        total = mul(r.du_all[chip], r.wu[chip], COLS_COLS)
+        for step in range(1, chips):
+            lane.d_pre.take(step)
+            source = lane.d_pre.source(step)
+            total = total + mul(r.du_all[source], r.wu[source], COLS_COLS)
+        total = total.astype(BF16)
+        for c in range(chips):
+            for m in range(mp_size):
+                first = c * length + m * strip
+                r.dc_send[c, m] = total[first : first + strip]
+        lane.d_second.start_all()
+        lane.out.start_all()
+        r.own_contract[...] = mul(r.z[:, part(core, own_units)], flat(r.dy_all), ROWS_ROWS)
+        for c in range(chips):
+            r.ge_send[c] = mul(flat(r.c_all, other), r.du_all[c], ROWS_ROWS).astype(BF16)
+        lane.g_expand.start_all()
+        for c in range(chips):
+            r.own_expand[:, c * units : (c + 1) * units] = mul(
+                flat(r.c_all, mine), r.du_all[c], ROWS_ROWS
+            )
+        lane.d_second.take_all()
+
+        def gathered(send, recv):
+            blocks = []
+            for c in range(chips):
+                block = jnp.zeros((strip, slab), F32)
+                for m in range(mp_size):
+                    block = block + recv[c, m].astype(F32)
+                blocks.append(block)
+            return jnp.concatenate(blocks, axis=1)
+
+        r.dc_recv[chip, mp] = r.dc_send[chip, mp]
+        d_normed = gathered(r.dc_send, r.dc_recv)
+        back, gain_two, shift_two = norm_back(d_normed, r.hid[...], norm_row(2))
+        d_hidden = r.cot[here, :].astype(F32) + back
+        r.dh[...] = d_hidden
+        r.da_mine[...] = d_hidden.astype(BF16)
+        lane.d_hidden.start_all()
+        r.da_rows[mp] = r.da_mine[...]
+        lane.d_hidden.take_all()
+        d_attended = mul(flat(r.da_rows), flat(r.wo), COLS_COLS).astype(BF16)
+        for start in range(0, width, HEAD_DIM):
+            query, key, value = (
+                r.joint[:, c * width + start : c * width + start + HEAD_DIM] for c in range(3)
+            )
+            d_out = d_attended[:, start : start + HEAD_DIM]
+            prob = probabilities(query, key, allowed)
+            d_prob = mul(d_out, value, COLS_COLS)
+            row_delta = jnp.sum(d_prob * prob, axis=-1, keepdims=True)
+            d_raw = (prob * (d_prob - row_delta) * SCALE).astype(BF16)
+            r.dq_mine[:, start : start + HEAD_DIM] = mul(d_raw, key).astype(BF16)
+            r.dq_mine[:, width + start : width + start + HEAD_DIM] = mul(
+                d_raw, query, ROWS_ROWS
+            ).astype(BF16)
+            r.dq_mine[:, 2 * width + start : 2 * width + start + HEAD_DIM] = mul(
+                prob.astype(BF16), d_out, ROWS_ROWS
+            ).astype(BF16)
+        lane.d_joint.start_all()
+        r.dq_all[chip] = r.dq_mine[...]
+
+        lane.out.take_all()
+        total = r.y_send[chip].astype(F32)
+        for step in range(1, chips):
+            total = total + r.y_recv[lane.out.source(step)].astype(F32)
+        total = total.astype(BF16)
+        for m in range(mp_size):
+            r.y2_send[m] = total[m * strip : (m + 1) * strip]
+        lane.out_strip.start_all()
+        grad_out = mul(r.attended[...], flat(r.da_rows), ROWS_ROWS).astype(BF16)
+        for c in range(chips):
+            for k in range(2):
+                first = (2 * c + k) * out_rows
+                r.go_send[c, k] = grad_out[first : first + out_rows]
+
+        def first_block(block):
+            rows = r.dq_all[block]
+            total = mul(rows[:, :width], r.wq[0], COLS_COLS)
+            for c in range(1, 3):
+                total = total + mul(rows[:, c * width : (c + 1) * width], r.wq[c], COLS_COLS)
+            total = total.astype(BF16)
+            for m in range(mp_size):
+                r.df_send[block, m] = total[m * strip : (m + 1) * strip]
+
+        first_block(chip)
+        for step in range(1, chips):
+            lane.d_joint.take(step)
+            first_block(lane.d_joint.source(step))
+        lane.d_first.start_all()
+        lane.g_out.start_all()
+        for c in range(3):
+            r.gj_send[c] = mul(
+                flat(r.a_all, other), flat(r.dq_all, slice(c * width, (c + 1) * width)), ROWS_ROWS
+            ).astype(BF16)
+        lane.g_joint.start_all()
+        for c in range(3):
+            r.own_joint[c] = mul(
+                flat(r.a_all, mine), flat(r.dq_all, slice(c * width, (c + 1) * width)), ROWS_ROWS
+            )
+        lane.out_strip.take_all()
+        total = r.hid[...] + r.y2_send[mp].astype(F32)
+        for step in range(1, mp_size):
+            total = total + r.y2_recv[lane.out_strip.source(step)].astype(F32)
+        r.y_mine[...] = total.astype(BF16)
+        lane.out_rows.start_all()
+        r.layer_output[here, :] = r.y_mine[...]
+
+        lane.d_first.take_all()
+        r.df_recv[chip, mp] = r.df_send[chip, mp]
+        d_normed = gathered(r.df_send, r.df_recv)
+        back, gain_one, shift_one = norm_back(d_normed, r.x[here, :].astype(F32), norm_row(0))
+        grad = r.dh[...] + back
+        r.ig_mine[...] = grad.astype(BF16)
+        lane.in_rows.start_all()
+        r.input_grad[here, :] = grad
+        for c in range(chips):
+            columns = slice(c * slab, (c + 1) * slab)
+            for index, row in enumerate((gain_one, shift_one, gain_two, shift_two)):
+                r.gn_send[c, index : index + 1, :] = row[:, columns]
+            r.gn_send[c, 4:8, :] = jnp.zeros((4, slab), F32)
+        lane.g_norms.start_all()
+        r.gn_recv[cross_me] = r.gn_send[chip]
+        lane.g_norms.take_all()
+        summed = r.gn_recv[0]
+        for index in range(1, chips * mp_size):
+            summed = summed + r.gn_recv[index]
+        low, high = summed[:, :shard], summed[:, shard:]
+        first = core == 0
+        r.gn_pair[...] = jnp.where(first, high, low)
+        lane.g_norms_pair.start_all()
+
+        lane.g_out.take_all()
+        for k in range(2):
+            total = r.go_send[chip, k].astype(F32)
+            for step in range(1, chips):
+                total = total + r.go_recv[lane.g_out.source(step), k].astype(F32)
+
+            @pl.when(core == k)
+            def _():
+                r.own_out[...] = total
+
+            r.go_pair[k] = total.astype(BF16)
+        lane.g_out_pair.start_all()
+
+        lane.g_norms_pair.take_all()
+        r.own_norms[...] = jnp.where(first, low, high) + r.gn_far[...]
+
+        def place(rows_lane, rows, output):
+            rows_lane.take_all()
+            for step in range(1, mp_size):
+                source = rows_lane.source(step)
+                output[part(source, strip), :] = rows[source].astype(output.dtype)
+
+        place(lane.out_rows, r.y_rows, r.layer_output)
+        place(lane.in_rows, r.ig_rows, r.input_grad)
+        for entry in (lane.g_contract, lane.g_expand, lane.g_joint, lane.g_out_pair):
+            entry.take_all()
+        for entry in vars(lane).values():
+            entry.sent_all()
+        for step in range(1, chips):
+            passing(step, False).wait_send()
+
+    vmem = pl.BlockSpec(memory_space=pltpu.VMEM)
+    any_space = pl.BlockSpec(memory_space=pl.ANY)
+    sem_shapes = [pltpu.SemaphoreType.DMA((4,))]
+    for kind in LANES.values():
+        sem_shapes += [pltpu.SemaphoreType.DMA((vars(groups)[kind].size,))] * 2
+    results = pl.pallas_call(
+        kernel,
+        out_shape=list(outs.values()) + list(far.values()),
+        in_specs=[vmem] * 4 + [any_space] * 4 + [vmem],
+        out_specs=[vmem] * len(outs) + [any_space] * len(far),
+        scratch_shapes=[pltpu.VMEM(*entry) for entry in scratch.values()] + sem_shapes,
+        compiler_params=pltpu.CompilerParams(
+            collective_id=30, has_side_effects=True, vmem_limit_bytes=VMEM_LIMIT
+        ),
+    )(x, segments, segments.reshape(length, 1), cotangent, joint_w, out_w, expand_w, contract_w, norms)
+    return SimpleNamespace(**dict(zip(list(outs) + list(far), results)))
+
+
+VMEM_LIMIT = 60 * 2**20
+
+
+def local(dp_size, mp_size, *arrays):
+    params, firsts, seconds = arrays[3:8], arrays[8:13], arrays[13:18]
+    everyone = Group(ALL, dp_size, mp_size)
+    r = layer(dp_size, mp_size, arrays[:8])
+    shard, hidden = params[2].shape
+    far_expand = jnp.swapaxes(r.far_expand, 0, 1).reshape(shard, hidden)
+    grads = (
+        r.own_joint + r.far_joint.astype(F32),
+        r.own_out + r.far_out.astype(F32),
+        r.own_expand + far_expand.astype(F32),
+        r.own_contract + r.far_contract.astype(F32),
+        r.own_norms[:4],
+    )
+    squares = sum((jnp.sum(entry * entry) for entry in grads[:4])) + jnp.sum(
+        grads[4] * grads[4]
+    ) / mp_size
+    (square_parts,) = exchange(
+        everyone,
+        [jnp.full((8, 128), squares, F32)],
+        [shape((dp_size * mp_size, 8, 128), F32)],
+        [lambda ins, outs, me, other: (ins[0], outs[0].at[me])],
+        21,
+    )
+    gradient_norm = jnp.sqrt(jnp.sum(square_parts[:, 0, 0]))
+    clip_factor = jnp.minimum(1.0, MAX_NORM / (gradient_norm + CLIP_EPSILON))
+    updates = [
+        adam_update(params[k], grads[k], firsts[k], seconds[k], LEARN_RATES[k], clip_factor)
+        for k in range(5)
+    ]
+    copies = [entry[2].astype(BF16) for entry in updates]
+    return (
+        r.layer_output,
+        r.input_grad,
+        *grads,
+        *[entry[0] for entry in updates],
+        *[entry[1] for entry in updates],
+        *[entry[2] for entry in updates],
+        *copies,
+        gradient_norm,
+    )
+
+
 def solution(mesh):
     rows = P("dp", None)
     sets = (
@@ -585,8 +1249,9 @@
         P(("mp", "dp"), None),
         P(None, "dp"),
     )
+    form = local if mesh.shape["dp"] <= 8 else local_steps
     return jax.shard_map(
-        functools.partial(local, mesh.shape["dp"], mesh.shape["mp"]),
+        functools.partial(form, mesh.shape["dp"], mesh.shape["mp"]),
         mesh=mesh,
         in_specs=(rows, rows, rows) + sets * 3,
         out_specs=(rows, rows) + sets * 5 + (P(),),

time: 594 us -> 279 us (0.47)
  Pallas kernels: 453 us -> 236 us
  other arithmetic: 67.8 us -> 29.6 us
  local copies, waits for them, and re-layouts: 36.6 us -> 7.69 us
  matrix products: 28.3 us -> 0 us
    pallas_call x21 -> x1, Pallas kernels: 443 us -> 10.9 us  [exchange(): pl.pallas_call(kernel, out_shape=results, in_specs=[any_space] * count, o...]
    pallas_call x3 -> x1, Pallas kernels: 10.5 us -> 225 us  [layer(): pl.pallas_call(kernel, out_shape=list(outs.values()) + list(far.values())...]
    dot_general x9 -> x0, matrix products: 28.3 us -> none  [mul(): return lax.dot_general(left, right, dims, preferred_element_type=F32)]
    unnamed x97 -> x46, local copies, waits for them, and re-layouts: 29.3 us -> 5.49 us
    reduce_sum x21 -> x1, other arithmetic: 23.4 us -> 1.31 us  [local(): jnp.sum(grads[4] * grads[4]) / mp_size]
    convert_element_type x10 -> x0, other arithmetic: 12.6 us -> none  [the longest x1 2.12 us: local(): gather_rows((d_hidden + d_values_norm).astype(BF16), 14).astype(F32)]
where the time goes in v2:
time: 279 us
  Pallas kernels  236 us (85%)
  other arithmetic  29.6 us (11%)
  local copies, waits for them, and re-layouts  7.69 us (3%)
  between operations  6.01 us (2%)
    pallas_call x1, Pallas kernels, layer(): pl.pallas_call(kernel, out_shape=list(outs.values()) + list(far.values())...  225 us
    convert_element_type x5, other arithmetic, local(): copies = [entry[2].astype(BF16) for entry in updates]  17.7 us
    pallas_call x1, Pallas kernels, exchange(): pl.pallas_call(kernel, out_shape=results, in_specs=[any_space] * count, o...  10.9 us
    reduce_sum x3, other arithmetic, local(): jnp.sum(entry * entry)  8.77 us

profile of v2, /device:TPU:0, one launch (start us, length us, event | category | flops | bytes accessed | tf_op | source)
XLA Modules:
  0.0 278.9 jit_solution(17889590320929844893)
XLA Ops:
  0.7 1.4 copy.46.refs_2_
  2.1 224.8 %shard_map.393 = (bf16[128,2048]{1,0:T(8,128)(2,1)}, f32[128,2048]{1,0:T(8,128)}, f32[3,256,512]{2,1,0:T(8,128)}, f32[64,2048]{1,0:T(8,128)}, f32[256,2048]{1,0:...) custom-call(bf16[128,2048]{1,0:T(8,128)(2,1)} %refs_0_.1, ...), custom_call_target="tpu_custom_call" | custom-call | tf_op jit(solution)/shard_map/pallas_call | solution.py:1185
  226.8 1.3 multiply_reduce_fusion.4
  228.8 1.9 multiply_reduce_fusion.3
  230.6 3.9 %multiply_reduce_fusion.2 = (f32[]{:T(128)}, f32[3,256,512]{2,1,0:T(8,128)}) fusion(f32[3,256,512]{2,1,0:T(8,128)} %get-tuple-element.41, bf16[3,256,512]{2,1,0:T(8,128)(2,1)} %get-tuple-element.42), kind=kLoop, calls=%fused_computation.16 | loop fusion | flops 1572863 | bytes 3932164 | tf_op jit(solution)/shard_map/reduce_sum | solution.py:1214
  235.9 0.0 copy-done.15
  235.9 0.0 copy-start.14
  235.9 0.3 convert_bitcast_fusion
  236.2 0.0 copy-start.12
  236.2 0.0 copy-start.13
  236.2 0.2 copy.48
  236.4 0.7 copy-done.14
  237.1 0.8 copy-done.12
  237.9 0.6 copy-done.13
  238.5 3.0 %multiply_reduce_fusion = (f32[]{:T(128)}, f32[256,2048]{1,0:T(8,128)S(1)}, f32[]{:T(128)}, f32[256,2048]{1,0:T(8,128)}) fusion(f32[256,2048]{1,0:T(8,128)S(1)} %copy-done.13, bf16[256,2048]{1,0:T(8,128)(2,1)S(1)} %copy-done.14, f32[256,2048]{1,0:T(8,128)S(1)} %copy-done.12, f32[256,2048]{1,0:T(8,128)S(1)} %bitcast.5), kind=kLoop, calls=%fused_computation.10 | loop fusion | flops 3670014 | bytes 11534344 | tf_op jit(solution)/shard_map/reduce_sum | solution.py:1214
  242.9 0.6 broadcast_in_dim.3.refs_0_
  243.4 10.9 %shard_map.394 = f32[32,8,128]{2,1,0:T(8,128)} custom-call(f32[8,128]{1,0:T(8,128)} %broadcast_in_dim.3.refs_0_), custom_call_target="tpu_custom_call" | custom-call | tf_op jit(solution)/shard_map/pallas_call | solution.py:175
  254.3 1.5 slice_reduce_fusion
  256.6 0.0 copy-done.19
  256.6 0.0 copy-done.18
  256.7 0.0 copy-done.20
  256.7 0.0 copy-done.21
  256.7 0.0 copy-start.4
  256.7 0.0 copy-start.5
  256.7 0.6 fusion.5
  257.3 0.0 copy-done.11
  257.3 0.0 copy-done.10
  257.3 3.0 %fusion.11 = (bf16[64,2048]{1,0:T(8,128)(2,1)}, f32[64,2048]{1,0:T(8,128)}, f32[64,2048]{1,0:T(8,128)}, f32[64,2048]{1,0:T(8,128)}) fusion(f32[64,2048]{1,0:T(8,128)S(1)} %copy-done.10, f32[64,2048]{1,0:T(8,128)S(1)} %get-tuple-element.113, f32[]{:T(128)S(6)} %min_shard_map.3, f32[64,2048]{1,0:T(8,128)} %param.32, f32[64,2048]{1,0:T(8,128)} %param.27), kind=kLoop, calls=%fused_computation.33 | loop fusion | flops 2228224 | bytes 3932164 | tf_op jit(solution)/shard_map/convert_element_type | solution.py:1230
  260.3 0.0 copy-done.4
  260.3 0.0 copy-done.5
  260.3 0.0 copy-start.3
  260.3 0.0 copy-start.6
  260.4 0.0 copy-start.7
  260.4 5.4 %fusion.13 = (bf16[3,256,512]{2,1,0:T(8,128)(2,1)}, f32[3,256,512]{2,1,0:T(8,128)}, f32[3,256,512]{2,1,0:T(8,128)}, f32[3,256,512]{2,1,0:T(8,128)}) fusion(f32[3,256,512]{2,1,0:T(8,128)S(1)} %copy-done.4, f32[3,256,512]{2,1,0:T(8,128)S(1)} %copy-done.5, f32[]{:T(128)S(6)} %min_shard_map.3, f32[3,256,512]{2,1,0:T(8,128)} %param.31, f32[3,256,512]{2,1,0:T(8,128)} %param.26), kind=kLoop, calls=%fused_computation.34 | loop fusion | flops 6684672 | bytes 11796484 | tf_op jit(solution)/shard_map/convert_element_type | solution.py:1230
  265.7 0.0 copy-done
  265.7 0.0 copy-done.3
  265.8 0.0 copy-done.6
  265.8 0.7 copy-done.7
  266.5 4.5 %fusion.9 = (bf16[256,2048]{1,0:T(8,128)(2,1)}, f32[256,2048]{1,0:T(8,128)}, f32[256,2048]{1,0:T(8,128)}, f32[256,2048]{1,0:T(8,128)}) fusion(f32[256,2048]{1,0:T(8,128)S(1)} %copy-done, f32[256,2048]{1,0:T(8,128)S(1)} %copy-done.3, f32[]{:T(128)S(6)} %min_shard_map.3, f32[256,2048]{1,0:T(8,128)S(1)} %copy-done.6, f32[256,2048]{1,0:T(8,128)S(1)} %copy-done.7), kind=kLoop, calls=%fused_computation.32 | loop fusion | flops 8912896 | bytes 15728644 | tf_op jit(solution)/shard_map/convert_element_type | solution.py:1230
  270.9 0.0 copy-done.2
  270.9 0.0 copy-done.1
  270.9 0.0 copy-done.8
  270.9 0.9 copy-done.9
  271.8 4.2 %fusion.7 = (bf16[256,2048]{1,0:T(8,128)(2,1)}, f32[256,2048]{1,0:T(8,128)}, f32[256,2048]{1,0:T(8,128)}, f32[256,2048]{1,0:T(8,128)}) fusion(f32[256,2048]{1,0:T(8,128)S(1)} %copy-done.1, f32[256,2048]{1,0:T(8,128)S(1)} %get-tuple-element.115, f32[]{:T(128)S(6)} %min_shard_map.3, f32[256,2048]{1,0:T(8,128)S(1)} %copy-done.8, f32[256,2048]{1,0:T(8,128)S(1)} %copy-done.9), kind=kLoop, calls=%fused_computation.31 | loop fusion | flops 8912896 | bytes 15728644 | tf_op jit(solution)/shard_map/convert_element_type | solution.py:1230
  276.0 0.0 copy-done.17
  276.1 0.8 copy.51
  276.8 0.0 copy-done.16
  276.8 1.0 copy.52
  (14 shorter events, 0.0 us)
Async XLA Ops:
  228.1 28.5 %copy-start.19 = (f32[4,256]{1,0:T(4,128)}, f32[4,256]{1,0:T(4,128)S(1)}, u32[]{:S(2)}) copy-start(f32[4,256]{1,0:T(4,128)S(1)} %get-tuple-element.116) | copy-start | bytes 12292
  230.6 26.7 %copy-start.11 = (f32[64,2048]{1,0:T(8,128)}, f32[64,2048]{1,0:T(8,128)S(1)}, u32[]{:S(2)}) copy-start(f32[64,2048]{1,0:T(8,128)S(1)} %get-tuple-element.113) | copy-start | bytes 1572868
  230.6 5.2 %copy-start.15 = (bf16[4,256,512]{2,1,0:T(8,128)(2,1)S(1)}, bf16[4,256,512]{2,1,0:T(8,128)(2,1)}, u32[]{:S(2)}) copy-start(bf16[4,256,512]{2,1,0:T(8,128)(2,1)} %get-tuple-element.46) | copy-start | bytes 3145732
  235.9 1.2 copy-start.14
  236.2 1.7 copy-start.12
  236.2 2.3 copy-start.13
  238.5 18.1 %copy-start.18 = (f32[4,256]{1,0:T(4,128)S(1)}, f32[4,256]{1,0:T(4,128)}, u32[]{:S(2)}) copy-start(f32[4,256]{1,0:T(4,128)} %refs_8_.1) | copy-start | bytes 12292
  238.5 18.1 %copy-start.20 = (f32[4,256]{1,0:T(4,128)S(1)}, f32[4,256]{1,0:T(4,128)}, u32[]{:S(2)}) copy-start(f32[4,256]{1,0:T(4,128)} %param.35) | copy-start | bytes 12292
  238.5 18.1 %copy-start.21 = (f32[4,256]{1,0:T(4,128)S(1)}, f32[4,256]{1,0:T(4,128)}, u32[]{:S(2)}) copy-start(f32[4,256]{1,0:T(4,128)} %param.30) | copy-start | bytes 12292
  238.5 18.8 %copy-start.10 = (f32[64,2048]{1,0:T(8,128)S(1)}, f32[64,2048]{1,0:T(8,128)}, u32[]{:S(2)}) copy-start(f32[64,2048]{1,0:T(8,128)} %refs_5_.1) | copy-start | bytes 1572868
  241.5 29.4 %copy-start.2 = (f32[256,2048]{1,0:T(8,128)}, f32[256,2048]{1,0:T(8,128)S(1)}, u32[]{:S(2)}) copy-start(f32[256,2048]{1,0:T(8,128)S(1)} %get-tuple-element.115) | copy-start | bytes 6291460
  256.7 3.6 %copy-start.4 = (f32[3,256,512]{2,1,0:T(8,128)S(1)}, f32[3,256,512]{2,1,0:T(8,128)}, u32[]{:S(2)}) copy-start(f32[3,256,512]{2,1,0:T(8,128)} %refs_4_.1) | copy-start | bytes 4718596
  256.7 3.6 %copy-start.5 = (f32[3,256,512]{2,1,0:T(8,128)S(1)}, f32[3,256,512]{2,1,0:T(8,128)}, u32[]{:S(2)}) copy-start(f32[3,256,512]{2,1,0:T(8,128)} %get-tuple-element.112) | copy-start | bytes 4718596
  260.3 5.4 %copy-start = (f32[256,2048]{1,0:T(8,128)S(1)}, f32[256,2048]{1,0:T(8,128)}, u32[]{:S(2)}) copy-start(f32[256,2048]{1,0:T(8,128)} %refs_6_.1) | copy-start | bytes 6291460
  260.3 5.4 %copy-start.3 = (f32[256,2048]{1,0:T(8,128)S(1)}, f32[256,2048]{1,0:T(8,128)}, u32[]{:S(2)}) copy-start(f32[256,2048]{1,0:T(8,128)} %get-tuple-element.114) | copy-start | bytes 6291460
  260.3 5.4 %copy-start.6 = (f32[256,2048]{1,0:T(8,128)S(1)}, f32[256,2048]{1,0:T(8,128)}, u32[]{:S(2)}) copy-start(f32[256,2048]{1,0:T(8,128)} %param.33) | copy-start | bytes 6291460
  260.4 6.1 %copy-start.7 = (f32[256,2048]{1,0:T(8,128)S(1)}, f32[256,2048]{1,0:T(8,128)}, u32[]{:S(2)}) copy-start(f32[256,2048]{1,0:T(8,128)} %param.28) | copy-start | bytes 6291460
  266.4 4.5 %copy-start.1 = (f32[256,2048]{1,0:T(8,128)S(1)}, f32[256,2048]{1,0:T(8,128)}, u32[]{:S(2)}) copy-start(f32[256,2048]{1,0:T(8,128)} %refs_7_.1) | copy-start | bytes 6291460
  266.4 4.5 %copy-start.8 = (f32[256,2048]{1,0:T(8,128)S(1)}, f32[256,2048]{1,0:T(8,128)}, u32[]{:S(2)}) copy-start(f32[256,2048]{1,0:T(8,128)} %param.34) | copy-start | bytes 6291460
  266.4 5.3 %copy-start.9 = (f32[256,2048]{1,0:T(8,128)S(1)}, f32[256,2048]{1,0:T(8,128)}, u32[]{:S(2)}) copy-start(f32[256,2048]{1,0:T(8,128)} %param.29) | copy-start | bytes 6291460
  271.8 4.3 %copy-start.17 = (bf16[128,2048]{1,0:T(8,128)(2,1)S(1)}, bf16[128,2048]{1,0:T(8,128)(2,1)}, u32[]{:S(2)}) copy-start(bf16[128,2048]{1,0:T(8,128)(2,1)} %get-tuple-element.110) | copy-start | bytes 1572868
  271.8 5.0 %copy-start.16 = (f32[128,2048]{1,0:T(8,128)S(1)}, f32[128,2048]{1,0:T(8,128)}, u32[]{:S(2)}) copy-start(f32[128,2048]{1,0:T(8,128)} %get-tuple-element.111) | copy-start | bytes 3145732

commit v3 on v2

--- a/solution.py
+++ b/solution.py
@@ -57,14 +57,7 @@
     return (new_first, new_second, new_weight)
 
 
-PAIR, PLANE, COLUMN, CROSS, ROW, ALL = (
-    "pair",
-    "plane",
-    "column",
-    "cross",
-    "row",
-    "all",
-)
+PAIR, PLANE, COLUMN, CROSS, ROW, ALL = ("pair", "plane", "column", "cross", "row", "all")
 
 
 class Group:
@@ -661,7 +654,6 @@
     joint_weight=PAIR,
     out_own=PAIR,
     out_plane=PLANE,
-    out_pass=PLANE,
     joint=PLANE,
     expand=PAIR,
     contract=PAIR,
@@ -685,7 +677,10 @@
     in_rows=COLUMN,
     g_norms=CROSS,
     g_norms_pair=PAIR,
+    squares=CROSS,
+    squares_pair=PAIR,
 )
+PIECED = ("joint", "d_joint")
 
 
 def layer(dp_size, mp_size, operands):
@@ -704,6 +699,8 @@
     strip = length // mp_size
     tokens = chips * length
     wide = 3 * width
+    pieces = max(1, width // (2 * HEAD_DIM))
+    piece = width // pieces
 
     outs = dict(
         layer_output=shape((length, model)),
@@ -713,8 +710,7 @@
         own_expand=shape((shard, hidden), F32),
         own_contract=shape((own_units, model), F32),
         own_norms=shape((8, shard), F32),
-    )
-    far = dict(
+        square_sum=shape((8, 128), F32),
         far_joint=shape((3, shard, width)),
         far_out=shape((out_rows, model)),
         far_expand=shape((chips, shard, units)),
@@ -728,9 +724,9 @@
         wo=((dp_size, out_rows, model), BF16),
         wu=((chips, slab, units), BF16),
         wd=((units, model), BF16),
-        j_send=((chips, length, wide), BF16),
-        j_recv=((chips, length, wide), BF16),
-        joint=((length, wide), BF16),
+        j_send=((pieces, chips, length, 3 * piece), BF16),
+        j_recv=((pieces, chips, length, 3 * piece), BF16),
+        joint=((pieces, length, 3 * piece), BF16),
         dy_all=((chips, length, model), BF16),
         attended=((length, width), BF16),
         b_send=((mp_size, strip, model), BF16),
@@ -753,8 +749,8 @@
         dh=((strip, model), F32),
         da_mine=((strip, model), BF16),
         da_rows=((mp_size, strip, model), BF16),
-        dq_mine=((length, wide), BF16),
-        dq_all=((chips, length, wide), BF16),
+        dq_mine=((pieces, length, 3 * piece), BF16),
+        dq_all=((pieces, chips, length, 3 * piece), BF16),
         go_send=((chips, 2, out_rows, model), BF16),
         go_recv=((chips, 2, out_rows, model), BF16),
         go_pair=((2, out_rows, model), BF16),
@@ -771,11 +767,15 @@
         gn_recv=((chips * mp_size, 8, slab), F32),
         gn_pair=((8, shard), F32),
         gn_far=((8, shard), F32),
+        sq_mine=((8, 128), F32),
+        sq_recv=((chips * mp_size, 8, 128), F32),
+        sq_pair=((8, 128), F32),
+        sq_far=((8, 128), F32),
     )
     in_names = dict(
-        x=0, seg_row=1, seg_col=2, cot=3, f_joint=4, f_out=5, f_expand=6, f_contract=7, norm_own=8
-    )
-    names = list(in_names) + list(outs) + list(far) + list(scratch)
+        x=0, seg_row=1, cot=2, f_joint=3, f_out=4, f_expand=5, f_contract=6, norm_own=7
+    )
+    names = list(in_names) + list(outs) + list(scratch)
 
     def kernel(*refs):
         r = SimpleNamespace(**dict(zip(names, refs)))
@@ -799,7 +799,9 @@
             ),
             out_own=lambda s, t: (r.wo.at[dp - core + s], r.wo.at[dp - core + s]),
             out_plane=lambda s, t: (r.wo.at[2 * s + core], r.wo.at[2 * s + core]),
-            joint=lambda s, t: (r.j_send.at[t], r.j_recv.at[s]),
+            joint=[
+                lambda s, t, p=p: (r.j_send.at[p, t], r.j_recv.at[p, s]) for p in range(pieces)
+            ],
             expand=lambda s, t: (
                 r.wu.at[:, part(s, shard), :],
                 r.wu.at[:, part(s, shard), :],
@@ -824,7 +826,9 @@
             out=lambda s, t: (r.y_send.at[t], r.y_recv.at[s]),
             g_expand=lambda s, t: (r.ge_send, r.far_expand),
             d_hidden=lambda s, t: (r.da_mine, r.da_rows.at[s]),
-            d_joint=lambda s, t: (r.dq_mine, r.dq_all.at[s]),
+            d_joint=[
+                lambda s, t, p=p: (r.dq_mine.at[p], r.dq_all.at[p, s]) for p in range(pieces)
+            ],
             g_out=lambda s, t: (r.go_send.at[t], r.go_recv.at[s]),
             g_out_pair=lambda s, t: (r.go_pair.at[t], r.far_out),
             out_strip=lambda s, t: (r.y2_send.at[t], r.y2_recv.at[s]),
@@ -837,16 +841,21 @@
             in_rows=lambda s, t: (r.ig_mine, r.ig_rows.at[s]),
             g_norms=lambda s, t: (r.gn_send.at[lax.div(t, mp_size)], r.gn_recv.at[s]),
             g_norms_pair=lambda s, t: (r.gn_pair, r.gn_far),
+            squares=lambda s, t: (r.sq_mine, r.sq_recv.at[s]),
+            squares_pair=lambda s, t: (r.sq_pair, r.sq_far),
         )
         lane = SimpleNamespace()
-        pass_sems = None
-        for index, (name, kind) in enumerate(LANES.items()):
-            pair_sems = (sems[1 + 2 * index], sems[2 + 2 * index])
-            if name in views:
-                group = vars(groups)[kind]
-                setattr(lane, name, Lane(group, group.me(), pair_sems, views[name]))
-            else:
-                pass_sems = pair_sems
+        every_lane = []
+        used = iter(sems[1:])
+        for name, kind in LANES.items():
+            group = vars(groups)[kind]
+            lanes = [
+                Lane(group, group.me(), (next(used), next(used)), view)
+                for view in (views[name] if name in PIECED else [views[name]])
+            ]
+            every_lane += lanes
+            setattr(lane, name, lanes if name in PIECED else lanes[0])
+        pass_sems = (next(used), next(used))
 
         def passing(step, to_me):
             block = r.wo.at[2 * lane.out_plane.source(step) + (1 - core if to_me else core)]
@@ -870,7 +879,7 @@
                 )
             )
         ]
-        for load in loads:
+        for load in (loads[1], loads[0], loads[2], loads[3]):
             load.start()
 
         barrier = pltpu.get_barrier_semaphore()
@@ -883,12 +892,26 @@
         cross = groups.cross
         repeat(1, cross.size, lambda s: greet(cross.device(lax.rem(cross_me + s, cross.size))))
         repeat(0, chips, lambda s: greet((s * 2 + 1 - core, mp)))
-        pl.semaphore_wait(barrier, cross.size - 1 + chips)
-
-        lane.norms.start_all()
+
         r.norm_all[dp] = r.norm_own[...]
+        loads[1].wait()
+        r.wo[dp] = r.own_out[...].astype(BF16)
         values = r.x[...].astype(F32)
         centered, inverse = standardise(values)
+        unit = centered * inverse
+        loads[0].wait()
+        for c in range(3):
+            r.wq[c, mine, :] = r.own_joint[c].astype(BF16)
+        ids = jnp.broadcast_to(r.seg_row[...].astype(F32), (length, length))
+        places = lax.broadcasted_iota(jnp.int32, (length, length), 0)
+        keys = lax.broadcasted_iota(jnp.int32, (length, length), 1)
+        allowed = (ids == ids.T) & (keys <= places)
+        pl.semaphore_wait(barrier, cross.size - 1 + chips)
+
+        lane.norms.start_all()
+        lane.joint_weight.start_all()
+        lane.out_plane.start_all()
+        lane.out_own.start_all()
         lane.norms.take_all()
 
         def norm_row(index, block=None):
@@ -900,33 +923,27 @@
         for b in range(dp_size):
             columns = slice(b * shard, (b + 1) * shard)
             r.a_mine[b // 2, :, (b % 2) * shard : (b % 2 + 1) * shard] = (
-                centered[:, columns] * inverse * norm_row(0, b) + norm_row(1, b)
+                unit[:, columns] * norm_row(0, b) + norm_row(1, b)
             ).astype(BF16)
         lane.normed.start_all()
         r.a_all[chip] = r.a_mine[chip]
 
-        loads[0].wait()
-        for c in range(3):
-            r.wq[c, mine, :] = r.own_joint[c].astype(BF16)
-        lane.joint_weight.start_all()
-        loads[1].wait()
-        r.wo[dp] = r.own_out[...].astype(BF16)
-        lane.out_plane.start_all()
-        lane.out_own.start_all()
         lane.joint_weight.take_all()
 
-        def joint_part(block):
+        def joint_part(p, block):
             rows = r.a_all[block]
             for c in range(3):
-                r.j_send[block, :, c * width : (c + 1) * width] = mul(rows, r.wq[c]).astype(BF16)
-
-        def joint_step(step):
-            lane.normed.take(step)
-            joint_part(lane.normed.source(step))
-            lane.joint.start(chips - step)
-
-        repeat(1, chips, joint_step)
-        joint_part(chip)
+                r.j_send[p, block, :, c * piece : (c + 1) * piece] = mul(
+                    rows, r.wq[c, :, p * piece : (p + 1) * piece]
+                ).astype(BF16)
+
+        for p in range(pieces):
+            for step in range(1, chips):
+                if p == 0:
+                    lane.normed.take(step)
+                joint_part(p, lane.normed.source(step))
+                lane.joint[p].start(chips - step)
+            joint_part(p, chip)
 
         loads[2].wait()
         for c in range(chips):
@@ -939,21 +956,24 @@
             lane.out_plane.take(step)
             passing(step, False).start()
 
-        lane.joint.take_all()
-        lane.cotangent.start_all()
-        total = r.j_send[chip].astype(F32)
-        for step in range(1, chips):
-            total = total + r.j_recv[lane.joint.source(step)].astype(F32)
-        r.joint[...] = total.astype(BF16)
-
-        allowed = allowed_pairs(r.seg_row, r.seg_col, length)
-        probs = []
-        for start in range(0, width, HEAD_DIM):
-            query, key, value = (
-                r.joint[:, c * width + start : c * width + start + HEAD_DIM] for c in range(3)
+        def query_key_value(start):
+            p, first = start // piece, start % piece
+            return (
+                r.joint[p, :, c * piece + first : c * piece + first + HEAD_DIM] for c in range(3)
             )
-            prob = probabilities(query, key, allowed)
-            r.attended[:, start : start + HEAD_DIM] = mul(prob.astype(BF16), value).astype(BF16)
+
+        for p in range(pieces):
+            lane.joint[p].take_all()
+            total = r.j_send[p, chip].astype(F32)
+            for step in range(1, chips):
+                total = total + r.j_recv[p, lane.joint[p].source(step)].astype(F32)
+            r.joint[p] = total.astype(BF16)
+            if p == pieces - 1:
+                lane.cotangent.start_all()
+            for start in range(p * piece, (p + 1) * piece, HEAD_DIM):
+                query, key, value = query_key_value(start)
+                prob = probabilities(query, key, allowed)
+                r.attended[:, start : start + HEAD_DIM] = mul(prob.astype(BF16), value).astype(BF16)
 
         lane.out_own.take_all()
         for step in range(1, chips):
@@ -978,9 +998,6 @@
         lane.second.start_all()
         r.c_all[chip, mp] = r.c_mine[chip]
         lane.expand.take_all()
-        lane.contract.take_all()
-        lane.cotangent.take_all()
-        r.dz[...] = mul(flat(r.dy_all), r.wd[...], COLS_COLS)
         lane.second.take_all()
 
         def pre_step(step):
@@ -990,6 +1007,9 @@
 
         repeat(1, chips, pre_step)
         r.u_acc[...] = mul(flat(r.c_all), r.wu[chip])
+        lane.contract.take_all()
+        lane.cotangent.take_all()
+        r.dz[...] = mul(flat(r.dy_all), r.wd[...], COLS_COLS)
         lane.pre.take_all()
 
         tile = 64
@@ -1057,24 +1077,24 @@
         r.da_rows[mp] = r.da_mine[...]
         lane.d_hidden.take_all()
         d_attended = mul(flat(r.da_rows), flat(r.wo), COLS_COLS).astype(BF16)
-        for start in range(0, width, HEAD_DIM):
-            query, key, value = (
-                r.joint[:, c * width + start : c * width + start + HEAD_DIM] for c in range(3)
-            )
-            d_out = d_attended[:, start : start + HEAD_DIM]
-            prob = probabilities(query, key, allowed)
-            d_prob = mul(d_out, value, COLS_COLS)
-            row_delta = jnp.sum(d_prob * prob, axis=-1, keepdims=True)
-            d_raw = (prob * (d_prob - row_delta) * SCALE).astype(BF16)
-            r.dq_mine[:, start : start + HEAD_DIM] = mul(d_raw, key).astype(BF16)
-            r.dq_mine[:, width + start : width + start + HEAD_DIM] = mul(
-                d_raw, query, ROWS_ROWS
-            ).astype(BF16)
-            r.dq_mine[:, 2 * width + start : 2 * width + start + HEAD_DIM] = mul(
-                prob.astype(BF16), d_out, ROWS_ROWS
-            ).astype(BF16)
-        lane.d_joint.start_all()
-        r.dq_all[chip] = r.dq_mine[...]
+        for p in range(pieces):
+            for start in range(p * piece, (p + 1) * piece, HEAD_DIM):
+                query, key, value = query_key_value(start)
+                d_out = d_attended[:, start : start + HEAD_DIM]
+                prob = probabilities(query, key, allowed)
+                d_prob = mul(d_out, value, COLS_COLS)
+                row_delta = jnp.sum(d_prob * prob, axis=-1, keepdims=True)
+                d_raw = (prob * (d_prob - row_delta) * SCALE).astype(BF16)
+                thirds = (
+                    mul(d_raw, key),
+                    mul(d_raw, query, ROWS_ROWS),
+                    mul(prob.astype(BF16), d_out, ROWS_ROWS),
+                )
+                for c in range(3):
+                    first = c * piece + start % piece
+                    r.dq_mine[p, :, first : first + HEAD_DIM] = thirds[c].astype(BF16)
+            lane.d_joint[p].start_all()
+            r.dq_all[p, chip] = r.dq_mine[p]
 
         lane.out.take_all()
         total = r.y_send[chip].astype(F32)
@@ -1091,29 +1111,45 @@
                 r.go_send[c, k] = grad_out[first : first + out_rows]
 
         def first_block(block):
-            rows = r.dq_all[block]
-            total = mul(rows[:, :width], r.wq[0], COLS_COLS)
-            for c in range(1, 3):
-                total = total + mul(rows[:, c * width : (c + 1) * width], r.wq[c], COLS_COLS)
+            total = jnp.zeros((length, slab), F32)
+            for p in range(pieces):
+                for c in range(3):
+                    total = total + mul(
+                        r.dq_all[p, block, :, c * piece : (c + 1) * piece],
+                        r.wq[c, :, p * piece : (p + 1) * piece],
+                        COLS_COLS,
+                    )
             total = total.astype(BF16)
             for m in range(mp_size):
                 r.df_send[block, m] = total[m * strip : (m + 1) * strip]
 
+        def first_send(block, others):
+            for j in others:
+                to = block * mp_size + lax.rem(mp + j, mp_size)
+                lane.d_first.start(lax.rem(to + cross.size - cross_me, cross.size))
+
         first_block(chip)
+        first_send(chip, range(1, mp_size))
         for step in range(1, chips):
-            lane.d_joint.take(step)
-            first_block(lane.d_joint.source(step))
-        lane.d_first.start_all()
+            for p in range(pieces):
+                lane.d_joint[p].take(step)
+            first_block(lane.d_joint[0].source(step))
+            first_send(lane.d_joint[0].source(step), range(mp_size))
         lane.g_out.start_all()
+
+        def joint_grad(c, columns, target):
+            for p in range(pieces):
+                target[c, :, p * piece : (p + 1) * piece] = mul(
+                    flat(r.a_all, columns),
+                    r.dq_all[p, :, :, c * piece : (c + 1) * piece].reshape(tokens, piece),
+                    ROWS_ROWS,
+                ).astype(target.dtype)
+
         for c in range(3):
-            r.gj_send[c] = mul(
-                flat(r.a_all, other), flat(r.dq_all, slice(c * width, (c + 1) * width)), ROWS_ROWS
-            ).astype(BF16)
+            joint_grad(c, other, r.gj_send)
         lane.g_joint.start_all()
         for c in range(3):
-            r.own_joint[c] = mul(
-                flat(r.a_all, mine), flat(r.dq_all, slice(c * width, (c + 1) * width)), ROWS_ROWS
-            )
+            joint_grad(c, mine, r.own_joint)
         lane.out_strip.take_all()
         total = r.hid[...] + r.y2_send[mp].astype(F32)
         for step in range(1, mp_size):
@@ -1137,6 +1173,38 @@
             r.gn_send[c, 4:8, :] = jnp.zeros((4, slab), F32)
         lane.g_norms.start_all()
         r.gn_recv[cross_me] = r.gn_send[chip]
+
+        def square(own, distant):
+            whole = own + distant.astype(F32)
+            return jnp.sum(whole * whole, axis=0, keepdims=True)
+
+        def folded(row):
+            return sum(row[:, i : i + 128] for i in range(0, row.shape[1], 128))
+
+        lane.g_contract.take_all()
+        squares = folded(square(r.own_contract[...], r.far_contract[...]))
+        lane.g_expand.take_all()
+        for c in range(chips):
+            squares = squares + folded(
+                square(r.own_expand[:, c * units : (c + 1) * units], r.far_expand[c])
+            )
+        lane.g_joint.take_all()
+        for c in range(3):
+            squares = squares + folded(square(r.own_joint[c], r.far_joint[c]))
+
+        lane.g_out.take_all()
+        for k in range(2):
+            total = r.go_send[chip, k].astype(F32)
+            for step in range(1, chips):
+                total = total + r.go_recv[lane.g_out.source(step), k].astype(F32)
+
+            @pl.when(core == k)
+            def _():
+                r.own_out[...] = total
+
+            r.go_pair[k] = total.astype(BF16)
+        lane.g_out_pair.start_all()
+
         lane.g_norms.take_all()
         summed = r.gn_recv[0]
         for index in range(1, chips * mp_size):
@@ -1145,22 +1213,16 @@
         first = core == 0
         r.gn_pair[...] = jnp.where(first, high, low)
         lane.g_norms_pair.start_all()
-
-        lane.g_out.take_all()
-        for k in range(2):
-            total = r.go_send[chip, k].astype(F32)
-            for step in range(1, chips):
-                total = total + r.go_recv[lane.g_out.source(step), k].astype(F32)
-
-            @pl.when(core == k)
-            def _():
-                r.own_out[...] = total
-
-            r.go_pair[k] = total.astype(BF16)
-        lane.g_out_pair.start_all()
-
+        lane.g_out_pair.take_all()
+        squares = squares + folded(square(r.own_out[...], r.far_out[...]))
         lane.g_norms_pair.take_all()
-        r.own_norms[...] = jnp.where(first, low, high) + r.gn_far[...]
+        own_norms = jnp.where(first, low, high) + r.gn_far[...]
+        r.own_norms[...] = own_norms
+        own_norms = jnp.sum(own_norms * own_norms, axis=0, keepdims=True) * (1.0 / mp_size)
+        squares = squares + folded(own_norms)
+        r.sq_mine[...] = jnp.broadcast_to(jnp.sum(squares), (8, 128))
+        lane.squares.start_all()
+        r.sq_recv[cross_me] = r.sq_mine[...]
 
         def place(rows_lane, rows, output):
             rows_lane.take_all()
@@ -1170,9 +1232,15 @@
 
         place(lane.out_rows, r.y_rows, r.layer_output)
         place(lane.in_rows, r.ig_rows, r.input_grad)
-        for entry in (lane.g_contract, lane.g_expand, lane.g_joint, lane.g_out_pair):
-            entry.take_all()
-        for entry in vars(lane).values():
+        lane.squares.take_all()
+        total = r.sq_recv[0]
+        for index in range(1, chips * mp_size):
+            total = total + r.sq_recv[index]
+        r.sq_pair[...] = total
+        lane.squares_pair.start_all()
+        lane.squares_pair.take_all()
+        r.square_sum[...] = total + r.sq_far[...]
+        for entry in every_lane:
             entry.sent_all()
         for step in range(1, chips):
             passing(step, False).wait_send()
@@ -1180,19 +1248,21 @@
     vmem = pl.BlockSpec(memory_space=pltpu.VMEM)
     any_space = pl.BlockSpec(memory_space=pl.ANY)
     sem_shapes = [pltpu.SemaphoreType.DMA((4,))]
-    for kind in LANES.values():
-        sem_shapes += [pltpu.SemaphoreType.DMA((vars(groups)[kind].size,))] * 2
+    for name, kind in LANES.items():
+        count = 2 * pieces if name in PIECED else 2
+        sem_shapes += [pltpu.SemaphoreType.DMA((vars(groups)[kind].size,))] * count
+    sem_shapes += [pltpu.SemaphoreType.DMA((chips,))] * 2
     results = pl.pallas_call(
         kernel,
-        out_shape=list(outs.values()) + list(far.values()),
-        in_specs=[vmem] * 4 + [any_space] * 4 + [vmem],
-        out_specs=[vmem] * len(outs) + [any_space] * len(far),
+        out_shape=list(outs.values()),
+        in_specs=[vmem] * 3 + [any_space] * 4 + [vmem],
+        out_specs=[vmem] * len(outs),
         scratch_shapes=[pltpu.VMEM(*entry) for entry in scratch.values()] + sem_shapes,
         compiler_params=pltpu.CompilerParams(
             collective_id=30, has_side_effects=True, vmem_limit_bytes=VMEM_LIMIT
         ),
-    )(x, segments, segments.reshape(length, 1), cotangent, joint_w, out_w, expand_w, contract_w, norms)
-    return SimpleNamespace(**dict(zip(list(outs) + list(far), results)))
+    )(x, segments, cotangent, joint_w, out_w, expand_w, contract_w, norms)
+    return SimpleNamespace(**dict(zip(outs, results)))
 
 
 VMEM_LIMIT = 60 * 2**20
@@ -1200,7 +1270,6 @@
 
 def local(dp_size, mp_size, *arrays):
     params, firsts, seconds = arrays[3:8], arrays[8:13], arrays[13:18]
-    everyone = Group(ALL, dp_size, mp_size)
     r = layer(dp_size, mp_size, arrays[:8])
     shard, hidden = params[2].shape
     far_expand = jnp.swapaxes(r.far_expand, 0, 1).reshape(shard, hidden)
@@ -1211,17 +1280,7 @@
         r.own_contract + r.far_contract.astype(F32),
         r.own_norms[:4],
     )
-    squares = sum((jnp.sum(entry * entry) for entry in grads[:4])) + jnp.sum(
-        grads[4] * grads[4]
-    ) / mp_size
-    (square_parts,) = exchange(
-        everyone,
-        [jnp.full((8, 128), squares, F32)],
-        [shape((dp_size * mp_size, 8, 128), F32)],
-        [lambda ins, outs, me, other: (ins[0], outs[0].at[me])],
-        21,
-    )
-    gradient_norm = jnp.sqrt(jnp.sum(square_parts[:, 0, 0]))
+    gradient_norm = jnp.sqrt(r.square_sum[0, 0])
     clip_factor = jnp.minimum(1.0, MAX_NORM / (gradient_norm + CLIP_EPSILON))
     updates = [
         adam_update(params[k], grads[k], firsts[k], seconds[k], LEARN_RATES[k], clip_factor)

time: 279 us -> 251 us (0.90)
  Pallas kernels: 236 us -> 223 us
  other arithmetic: 29.6 us -> 17.7 us
  between operations: 6.01 us -> 2.74 us
    pallas_call x2 -> x1, Pallas kernels: 236 us -> 223 us  [layer(): pl.pallas_call(kernel, out_shape=list(outs.values()), in_specs=[vmem] * 3...]
    reduce_sum x5 -> x0, other arithmetic: 11.6 us -> none  [the longest x3 8.77 us: local(): jnp.sum(entry * entry)]
    convert_element_type x5 -> x4, other arithmetic: 17.7 us -> 16 us  [local(): copies = [entry[2].astype(BF16) for entry in updates]]
    unnamed x46 -> x44, local copies, waits for them, and re-layouts: 5.49 us -> 5.59 us
where the time goes in v3:
time: 251 us
  Pallas kernels  223 us (89%)
  other arithmetic  17.7 us (7%)
  local copies, waits for them, and re-layouts  6.95 us (3%)
  between operations  2.74 us (1%)
    pallas_call x1, Pallas kernels, layer(): pl.pallas_call(kernel, out_shape=list(outs.values()), in_specs=[vmem] * 3...  223 us
    convert_element_type x4, other arithmetic, local(): copies = [entry[2].astype(BF16) for entry in updates]  16 us
    unnamed x44, local copies, waits for them, and re-layouts  5.59 us

profile of v3, /device:TPU:0, one launch (start us, length us, event | category | flops | bytes accessed | tf_op | source)
XLA Modules:
  0.0 250.7 jit_solution(6633769892339608344)
XLA Ops:
  0.7 0.0 copy-start.4
  0.7 223.4 %shard_map.393 = (bf16[128,2048]{1,0:T(8,128)(2,1)}, f32[128,2048]{1,0:T(8,128)}, f32[3,256,512]{2,1,0:T(8,128)}, f32[64,2048]{1,0:T(8,128)}, f32[256,2048]{1,0:...) custom-call(bf16[128,2048]{1,0:T(8,128)(2,1)} %refs_0_.1, ...), custom_call_target="tpu_custom_call" | custom-call | tf_op jit(solution)/shard_map/pallas_call | solution.py:1255
  224.1 1.2 slice.7
  226.0 0.0 copy-start.3
  226.0 0.0 copy-start.9
  226.0 1.6 convert_bitcast_fusion
  227.7 0.0 copy-start
  227.7 0.0 copy-start.1
  227.7 0.2 copy.47
  227.9 0.0 copy-done.4
  227.9 0.0 copy-done.3
  227.9 0.3 copy-done.9
  228.2 1.2 copy-done
  229.4 0.6 copy-done.1
  230.0 0.0 copy-start.5
  230.0 0.0 copy-start.12
  230.0 0.0 copy-start.13
  230.0 0.0 copy-start.14
  230.0 0.0 copy-start.16
  230.0 0.0 copy-start.8
  230.0 0.0 copy-start.11
  230.0 10.2 %fusion.7 = (bf16[256,2048]{1,0:T(8,128)(2,1)}, f32[256,2048]{1,0:T(8,128)}, f32[256,2048]{1,0:T(8,128)}, f32[256,2048]{1,0:T(8,128)}, f32[256,2048]{1,0:T(8,128...) fusion(f32[256,2048]{1,0:T(8,128)S(1)} %copy-done.1, ...), kind=kLoop, calls=%fused_computation.25 | loop fusion | flops 19398656 | bytes 38797316 | tf_op jit(solution)/shard_map/convert_element_type | solution.py:1289
  240.3 0.0 copy-done.5
  240.3 0.0 copy-done.12
  240.3 0.0 copy-done.13
  240.3 0.0 copy-done.14
  240.3 0.0 copy-done.16
  240.3 0.0 copy-start.2
  240.3 0.0 copy-start.6
  240.3 0.0 copy-start.7
  240.3 1.6 fusion.11
  241.9 0.0 copy-done.8
  241.9 0.0 copy-done.11
  241.9 0.5 copy-done.2
  242.4 0.7 copy-done.6
  243.0 0.5 copy-done.7
  243.5 0.0 copy-start.15
  243.5 0.0 copy-start.10
  243.6 3.6 %fusion.13 = (bf16[3,256,512]{2,1,0:T(8,128)(2,1)}, f32[3,256,512]{2,1,0:T(8,128)}, f32[3,256,512]{2,1,0:T(8,128)}, f32[3,256,512]{2,1,0:T(8,128)}, f32[3,256,512]{2,1,0:T(8,128)}) fusion(f32[3,256,512]{2,1,0:T(8,128)S(1)} %copy-done.2, f32[]{:T(128)S(6)} %min_shard_map.3, f32[3,256,512]{2,1,0:T(8,128)S(1)} %copy-done.6, f32[3,256,512]{2,1,0:T(8,128)S(1)} %copy-done.7, ...), kind=kLoop, calls=%fused_computation.28 | loop fusion | flops 7471104 | bytes 14155780 | tf_op jit(solution)/shard_map/convert_element_type | solution.py:1289
  247.2 0.0 copy-done.17
  247.2 0.0 copy-done.18
  247.2 0.0 copy-done.19
  247.2 0.0 copy-done.20
  247.2 0.6 fusion.5
  247.8 0.0 copy-done.15
  247.8 0.8 copy.50
  248.6 0.0 copy-done.10
  248.6 1.0 copy.51
  (4 shorter events, 0.0 us)
Async XLA Ops:
  0.7 227.2 %copy-start.4 = (f32[256,2048]{1,0:T(8,128)S(1)}, f32[256,2048]{1,0:T(8,128)}, u32[]{:S(2)}) copy-start(f32[256,2048]{1,0:T(8,128)} %param.29) | copy-start | bytes 6291460
  226.0 1.9 copy-start.3
  226.0 2.2 copy-start.9
  227.7 1.7 copy-start
  227.7 2.3 copy-start.1
  230.0 10.3 %copy-start.5 = (f32[64,2048]{1,0:T(8,128)S(1)}, f32[64,2048]{1,0:T(8,128)}, u32[]{:S(2)}) copy-start(f32[64,2048]{1,0:T(8,128)} %refs_4_.1) | copy-start | bytes 1572868
  230.0 10.3 %copy-start.12 = (f32[64,2048]{1,0:T(8,128)S(1)}, f32[64,2048]{1,0:T(8,128)}, u32[]{:S(2)}) copy-start(f32[64,2048]{1,0:T(8,128)} %param.32) | copy-start | bytes 1572868
  230.0 10.3 %copy-start.13 = (f32[64,2048]{1,0:T(8,128)S(1)}, f32[64,2048]{1,0:T(8,128)}, u32[]{:S(2)}) copy-start(f32[64,2048]{1,0:T(8,128)} %param.27) | copy-start | bytes 1572868
  230.0 10.3 %copy-start.14 = (f32[64,2048]{1,0:T(8,128)S(1)}, f32[64,2048]{1,0:T(8,128)}, u32[]{:S(2)}) copy-start(f32[64,2048]{1,0:T(8,128)} %get-tuple-element.44) | copy-start | bytes 1572868
  230.0 10.3 %copy-start.16 = (bf16[64,2048]{1,0:T(8,128)(2,1)S(1)}, bf16[64,2048]{1,0:T(8,128)(2,1)}, u32[]{:S(2)}) copy-start(bf16[64,2048]{1,0:T(8,128)(2,1)} %get-tuple-element.45) | copy-start | bytes 786436
  230.0 11.9 %copy-start.8 = (f32[3,256,512]{2,1,0:T(8,128)S(1)}, f32[3,256,512]{2,1,0:T(8,128)}, u32[]{:S(2)}) copy-start(f32[3,256,512]{2,1,0:T(8,128)} %get-tuple-element.42) | copy-start | bytes 4718596
  230.0 11.9 %copy-start.11 = (bf16[3,256,512]{2,1,0:T(8,128)(2,1)S(1)}, bf16[3,256,512]{2,1,0:T(8,128)(2,1)}, u32[]{:S(2)}) copy-start(bf16[3,256,512]{2,1,0:T(8,128)(2,1)} %get-tuple-element.43) | copy-start | bytes 2359300
  240.3 2.1 copy-start.2
  240.3 2.7 %copy-start.6 = (f32[3,256,512]{2,1,0:T(8,128)S(1)}, f32[3,256,512]{2,1,0:T(8,128)}, u32[]{:S(2)}) copy-start(f32[3,256,512]{2,1,0:T(8,128)} %param.31) | copy-start | bytes 4718596
  240.3 3.2 %copy-start.7 = (f32[3,256,512]{2,1,0:T(8,128)S(1)}, f32[3,256,512]{2,1,0:T(8,128)}, u32[]{:S(2)}) copy-start(f32[3,256,512]{2,1,0:T(8,128)} %param.26) | copy-start | bytes 4718596
  243.5 3.7 %copy-start.17 = (f32[4,256]{1,0:T(4,128)S(1)}, f32[4,256]{1,0:T(4,128)}, u32[]{:S(2)}) copy-start(f32[4,256]{1,0:T(4,128)} %refs_7_.1) | copy-start | bytes 12292
  243.5 3.7 %copy-start.18 = (f32[4,256]{1,0:T(4,128)S(1)}, f32[4,256]{1,0:T(4,128)}, u32[]{:S(2)}) copy-start(f32[4,256]{1,0:T(4,128)} %param.35) | copy-start | bytes 12292
  243.5 3.7 %copy-start.19 = (f32[4,256]{1,0:T(4,128)S(1)}, f32[4,256]{1,0:T(4,128)}, u32[]{:S(2)}) copy-start(f32[4,256]{1,0:T(4,128)} %param.30) | copy-start | bytes 12292
  243.5 3.7 %copy-start.20 = (f32[8,256]{1,0:T(8,128)S(1)}, f32[8,256]{1,0:T(8,128)}, u32[]{:S(2)}) copy-start(f32[8,256]{1,0:T(8,128)} %get-tuple-element.50) | copy-start | bytes 24580
  243.5 4.3 %copy-start.15 = (bf16[128,2048]{1,0:T(8,128)(2,1)S(1)}, bf16[128,2048]{1,0:T(8,128)(2,1)}, u32[]{:S(2)}) copy-start(bf16[128,2048]{1,0:T(8,128)(2,1)} %get-tuple-element.110) | copy-start | bytes 1572868
  243.5 5.1 %copy-start.10 = (f32[128,2048]{1,0:T(8,128)S(1)}, f32[128,2048]{1,0:T(8,128)}, u32[]{:S(2)}) copy-start(f32[128,2048]{1,0:T(8,128)} %get-tuple-element.111) | copy-start | bytes 3145732

commit v4 on v3

--- a/solution.py
+++ b/solution.py
@@ -627,6 +627,99 @@
         repeat(1, self.size, self.sent)
 
 
+class Hop:
+    def __init__(self, dp, mp):
+        core, self.me = lax.rem(dp, 2), lax.div(dp, 2)
+        x_next = self.me + 1 - 2 * lax.rem(self.me, 2)
+        self.chips = (x_next, lax.rem(self.me + 2, 4))
+        self.far = 3 - self.me
+        self.devices = tuple((chip * 2 + core, mp) for chip in self.chips)
+
+    def copy(self, source, target, sems, index, way):
+        return pltpu.make_async_remote_copy(
+            src_ref=source,
+            dst_ref=target,
+            send_sem=sems[0].at[index],
+            recv_sem=sems[1].at[index],
+            device_id=self.devices[way],
+            device_id_type=pl.DeviceIdType.MESH,
+        )
+
+
+class PlaneGather:
+    def __init__(self, hop, sems, own, block, half):
+        self.hop, self.sems, self.own, self.block, self.half = hop, sems, own, block, half
+
+    def first(self, way):
+        return self.hop.copy(self.own, self.block(self.hop.me), self.sems, way, way)
+
+    def second(self, way):
+        piece = self.half(self.block(self.hop.chips[way]), way)
+        return self.hop.copy(piece, piece, self.sems, 2 + way, 1 - way)
+
+    def start(self):
+        for way in range(2):
+            self.first(way).start()
+
+    def near(self, way):
+        near = self.block(self.hop.chips[way])
+        self.hop.copy(near, near, self.sems, way, way).wait_recv()
+
+    def forward(self):
+        for way in range(2):
+            self.near(way)
+            self.second(way).start()
+
+    def finish(self):
+        for way in range(2):
+            piece = self.half(self.block(self.hop.far), way)
+            self.hop.copy(piece, piece, self.sems, 2 + way, 1 - way).wait_recv()
+
+    def sent_all(self):
+        for way in range(2):
+            self.first(way).wait_send()
+            self.second(way).wait_send()
+
+
+class PlaneReduce:
+    def __init__(self, hop, sems, parts, inbox, middle):
+        self.hop, self.sems = hop, sems
+        self.parts, self.inbox, self.middle = parts, inbox, middle
+
+    def copy(self, stage, way):
+        hop = self.hop
+        chip = (hop.far, hop.chips[way])[stage] if stage < 2 else None
+        source = self.parts.at[chip, way] if stage < 2 else self.middle.at[way]
+        along = way if stage < 2 else 1 - way
+        return hop.copy(source, self.inbox.at[stage, way], self.sems, 2 * stage + way, along)
+
+    def start(self, stage):
+        for way in range(2):
+            self.copy(stage, way).start()
+
+    def forward(self):
+        for way in range(2):
+            self.copy(0, way).wait_recv()
+            onward = self.hop.chips[1 - way]
+            total = self.parts[onward, way].astype(F32) + self.inbox[0, way].astype(F32)
+            self.middle[way] = total.astype(BF16)
+            self.copy(2, way).start()
+
+    def take(self, way):
+        self.copy(1, way).wait_recv()
+        self.copy(2, way).wait_recv()
+
+    def total(self, way, rows=slice(None)):
+        own = self.parts[self.hop.me, way, rows].astype(F32)
+        near = self.inbox[1, way, rows].astype(F32)
+        return own + near + self.inbox[2, way, rows].astype(F32)
+
+    def sent_all(self):
+        for stage in range(3):
+            for way in range(2):
+                self.copy(stage, way).wait_send()
+
+
 def standardise(values):
     row_mean = jnp.mean(values, axis=-1, keepdims=True)
     centered = values - row_mean
@@ -653,22 +746,14 @@
     normed=PLANE,
     joint_weight=PAIR,
     out_own=PAIR,
-    out_plane=PLANE,
-    joint=PLANE,
     expand=PAIR,
     contract=PAIR,
-    cotangent=PLANE,
     branch=COLUMN,
     second=CROSS,
-    pre=PLANE,
-    d_pre=PLANE,
     g_contract=PAIR,
     d_second=CROSS,
-    out=PLANE,
     g_expand=PAIR,
     d_hidden=COLUMN,
-    d_joint=PLANE,
-    g_out=PLANE,
     g_out_pair=PAIR,
     out_strip=COLUMN,
     d_first=CROSS,
@@ -680,7 +765,6 @@
     squares=CROSS,
     squares_pair=PAIR,
 )
-PIECED = ("joint", "d_joint")
 
 
 def layer(dp_size, mp_size, operands):
@@ -713,7 +797,7 @@
         square_sum=shape((8, 128), F32),
         far_joint=shape((3, shard, width)),
         far_out=shape((out_rows, model)),
-        far_expand=shape((chips, shard, units)),
+        far_expand=shape((shard, hidden)),
         far_contract=shape((own_units, model)),
     )
     scratch = dict(
@@ -724,8 +808,9 @@
         wo=((dp_size, out_rows, model), BF16),
         wu=((chips, slab, units), BF16),
         wd=((units, model), BF16),
-        j_send=((pieces, chips, length, 3 * piece), BF16),
-        j_recv=((pieces, chips, length, 3 * piece), BF16),
+        j_send=((pieces, chips, 2, length // 2, 3 * piece), BF16),
+        j_recv=((pieces, 3, 2, length // 2, 3 * piece), BF16),
+        j_mid=((pieces, 2, length // 2, 3 * piece), BF16),
         joint=((pieces, length, 3 * piece), BF16),
         dy_all=((chips, length, model), BF16),
         attended=((length, width), BF16),
@@ -734,25 +819,27 @@
         hid=((strip, model), F32),
         c_mine=((chips, strip, slab), BF16),
         c_all=((chips, mp_size, strip, slab), BF16),
-        u_send=((chips, tokens, units), BF16),
-        u_recv=((chips, tokens, units), BF16),
-        u_acc=((tokens, units), F32),
+        u_send=((chips, 2, tokens // 2, units), BF16),
+        u_recv=((3, 2, tokens // 2, units), BF16),
+        u_mid=((2, tokens // 2, units), BF16),
         dz=((tokens, units), F32),
         z=((tokens, units), BF16),
         du_all=((chips, tokens, units), BF16),
-        y_send=((chips, length, model), BF16),
-        y_recv=((chips, length, model), BF16),
+        y_send=((chips, 2, length // 2, model), BF16),
+        y_recv=((3, 2, length // 2, model), BF16),
+        y_mid=((2, length // 2, model), BF16),
         gc_send=((own_units, model), BF16),
         dc_send=((chips, mp_size, strip, slab), BF16),
         dc_recv=((chips, mp_size, strip, slab), BF16),
-        ge_send=((chips, shard, units), BF16),
+        ge_send=((shard, hidden), BF16),
         dh=((strip, model), F32),
         da_mine=((strip, model), BF16),
         da_rows=((mp_size, strip, model), BF16),
         dq_mine=((pieces, length, 3 * piece), BF16),
         dq_all=((pieces, chips, length, 3 * piece), BF16),
         go_send=((chips, 2, out_rows, model), BF16),
-        go_recv=((chips, 2, out_rows, model), BF16),
+        go_recv=((3, 2, out_rows, model), BF16),
+        go_mid=((2, out_rows, model), BF16),
         go_pair=((2, out_rows, model), BF16),
         y2_send=((mp_size, strip, model), BF16),
         y2_recv=((mp_size, strip, model), BF16),
@@ -798,10 +885,6 @@
                 r.wq.at[:, part(s, shard), :],
             ),
             out_own=lambda s, t: (r.wo.at[dp - core + s], r.wo.at[dp - core + s]),
-            out_plane=lambda s, t: (r.wo.at[2 * s + core], r.wo.at[2 * s + core]),
-            joint=[
-                lambda s, t, p=p: (r.j_send.at[p, t], r.j_recv.at[p, s]) for p in range(pieces)
-            ],
             expand=lambda s, t: (
                 r.wu.at[:, part(s, shard), :],
                 r.wu.at[:, part(s, shard), :],
@@ -810,26 +893,18 @@
                 r.wd.at[part(s, own_units), :],
                 r.wd.at[part(s, own_units), :],
             ),
-            cotangent=lambda s, t: (r.cot, r.dy_all.at[s]),
             branch=lambda s, t: (r.b_send.at[t], r.b_recv.at[s]),
             second=lambda s, t: (
                 r.c_mine.at[lax.div(t, mp_size)],
                 r.c_all.at[lax.div(s, mp_size), lax.rem(s, mp_size)],
             ),
-            pre=lambda s, t: (r.u_send.at[t], r.u_recv.at[s]),
-            d_pre=lambda s, t: (r.du_all.at[s], r.du_all.at[s]),
             g_contract=lambda s, t: (r.gc_send, r.far_contract),
             d_second=lambda s, t: (
                 r.dc_send.at[lax.div(t, mp_size), lax.rem(t, mp_size)],
                 r.dc_recv.at[lax.div(s, mp_size), lax.rem(s, mp_size)],
             ),
-            out=lambda s, t: (r.y_send.at[t], r.y_recv.at[s]),
             g_expand=lambda s, t: (r.ge_send, r.far_expand),
             d_hidden=lambda s, t: (r.da_mine, r.da_rows.at[s]),
-            d_joint=[
-                lambda s, t, p=p: (r.dq_mine.at[p], r.dq_all.at[p, s]) for p in range(pieces)
-            ],
-            g_out=lambda s, t: (r.go_send.at[t], r.go_recv.at[s]),
             g_out_pair=lambda s, t: (r.go_pair.at[t], r.far_out),
             out_strip=lambda s, t: (r.y2_send.at[t], r.y2_recv.at[s]),
             d_first=lambda s, t: (
@@ -847,23 +922,49 @@
         lane = SimpleNamespace()
         every_lane = []
         used = iter(sems[1:])
+
+        def pair_of():
+            return (next(used), next(used))
+
         for name, kind in LANES.items():
             group = vars(groups)[kind]
-            lanes = [
-                Lane(group, group.me(), (next(used), next(used)), view)
-                for view in (views[name] if name in PIECED else [views[name]])
-            ]
-            every_lane += lanes
-            setattr(lane, name, lanes if name in PIECED else lanes[0])
-        pass_sems = (next(used), next(used))
-
-        def passing(step, to_me):
-            block = r.wo.at[2 * lane.out_plane.source(step) + (1 - core if to_me else core)]
+            setattr(lane, name, Lane(group, group.me(), pair_of(), views[name]))
+            every_lane.append(vars(lane)[name])
+        hop = Hop(dp, mp)
+
+        def gather(own, block, half):
+            every_lane.append(PlaneGather(hop, pair_of(), own, block, half))
+            return every_lane[-1]
+
+        def reduce(parts, inbox, middle):
+            every_lane.append(PlaneReduce(hop, pair_of(), parts, inbox, middle))
+            return every_lane[-1]
+
+        def row_half(ref, way):
+            rows = ref.shape[0] // 2
+            return ref.at[pl.ds(way * rows, rows), :]
+
+        out_plane = gather(r.wo.at[dp], lambda c: r.wo.at[2 * c + core], row_half)
+        cot_plane = gather(r.cot, lambda c: r.dy_all.at[c], row_half)
+        d_pre = gather(r.du_all.at[chip], lambda c: r.du_all.at[c], row_half)
+        d_joint = [
+            gather(r.dq_mine.at[p], lambda c, p=p: r.dq_all.at[p, c], row_half)
+            for p in range(pieces)
+        ]
+        joint = [reduce(r.j_send.at[p], r.j_recv.at[p], r.j_mid.at[p]) for p in range(pieces)]
+        pre_sum = reduce(r.u_send, r.u_recv, r.u_mid)
+        out_sum = reduce(r.y_send, r.y_recv, r.y_mid)
+        g_out_sum = reduce(r.go_send, r.go_recv, r.go_mid)
+        pass_sems = pair_of()
+
+        def passing(index, to_me):
+            source = (*hop.chips, hop.far)[index]
+            block = r.wo.at[2 * source + (1 - core if to_me else core)]
             return pltpu.make_async_remote_copy(
                 src_ref=block,
                 dst_ref=block,
-                send_sem=pass_sems[0].at[step],
-                recv_sem=pass_sems[1].at[step],
+                send_sem=pass_sems[0].at[index],
+                recv_sem=pass_sems[1].at[index],
                 device_id=(dp + 1 - 2 * core, mp),
                 device_id_type=pl.DeviceIdType.MESH,
             )
@@ -910,7 +1011,7 @@
 
         lane.norms.start_all()
         lane.joint_weight.start_all()
-        lane.out_plane.start_all()
+        out_plane.start()
         lane.out_own.start_all()
         lane.norms.take_all()
 
@@ -930,20 +1031,37 @@
 
         lane.joint_weight.take_all()
 
+        half_rows = length // 2
+
         def joint_part(p, block):
             rows = r.a_all[block]
             for c in range(3):
-                r.j_send[p, block, :, c * piece : (c + 1) * piece] = mul(
-                    rows, r.wq[c, :, p * piece : (p + 1) * piece]
-                ).astype(BF16)
+                columns = slice(c * piece, (c + 1) * piece)
+                third = mul(rows, r.wq[c, :, p * piece : (p + 1) * piece]).astype(BF16)
+                for way in range(2):
+                    r.j_send[p, block, way, :, columns] = third[
+                        way * half_rows : (way + 1) * half_rows
+                    ]
+
+        def chip_step(block):
+            return lax.rem(chip + chips - block, chips)
 
         for p in range(pieces):
-            for step in range(1, chips):
+            for way in range(2):
                 if p == 0:
-                    lane.normed.take(step)
-                joint_part(p, lane.normed.source(step))
-                lane.joint[p].start(chips - step)
+                    lane.normed.take(chip_step(hop.chips[way]))
+                joint_part(p, hop.chips[way])
+            joint[p].start(1)
+            if p == 0:
+                lane.normed.take(chip_step(hop.far))
+            joint_part(p, hop.far)
+            joint[p].start(0)
             joint_part(p, chip)
+        out_plane.forward()
+        for index in range(2):
+            passing(index, False).start()
+        for p in range(pieces):
+            joint[p].forward()
 
         loads[2].wait()
         for c in range(chips):
@@ -952,10 +1070,6 @@
         loads[3].wait()
         r.wd[part(core, own_units), :] = r.own_contract[...].astype(BF16)
         lane.contract.start_all()
-        for step in range(1, chips):
-            lane.out_plane.take(step)
-            passing(step, False).start()
-
         def query_key_value(start):
             p, first = start // piece, start % piece
             return (
@@ -963,26 +1077,29 @@
             )
 
         for p in range(pieces):
-            lane.joint[p].take_all()
-            total = r.j_send[p, chip].astype(F32)
-            for step in range(1, chips):
-                total = total + r.j_recv[p, lane.joint[p].source(step)].astype(F32)
-            r.joint[p] = total.astype(BF16)
+            for way in range(2):
+                joint[p].take(way)
+                r.joint[p, way * half_rows : (way + 1) * half_rows, :] = (
+                    joint[p].total(way).astype(BF16)
+                )
             if p == pieces - 1:
-                lane.cotangent.start_all()
+                cot_plane.start()
             for start in range(p * piece, (p + 1) * piece, HEAD_DIM):
                 query, key, value = query_key_value(start)
                 prob = probabilities(query, key, allowed)
                 r.attended[:, start : start + HEAD_DIM] = mul(prob.astype(BF16), value).astype(BF16)
 
         lane.out_own.take_all()
-        for step in range(1, chips):
-            passing(step, True).wait_recv()
+        out_plane.finish()
+        passing(2, False).start()
+        for index in range(3):
+            passing(index, True).wait_recv()
         branch = mul(r.attended[...], flat(r.wo)).astype(BF16)
         for m in range(mp_size):
             r.b_send[m] = branch[m * strip : (m + 1) * strip]
         lane.branch.start_all()
         r.dy_all[chip] = r.cot[...]
+        cot_plane.forward()
         lane.branch.take_all()
         here = part(mp, strip)
         total = r.x[here, :].astype(F32) + r.b_send[mp].astype(F32)
@@ -1000,62 +1117,81 @@
         lane.expand.take_all()
         lane.second.take_all()
 
-        def pre_step(step):
-            to = lax.rem(chip + step, chips)
-            r.u_send[to] = mul(flat(r.c_all), r.wu[to]).astype(BF16)
-            lane.pre.start(step)
-
-        repeat(1, chips, pre_step)
-        r.u_acc[...] = mul(flat(r.c_all), r.wu[chip])
+        half_tokens = tokens // 2
+
+        def pre_part(to):
+            part_sum = mul(flat(r.c_all), r.wu[to]).astype(BF16)
+            for way in range(2):
+                r.u_send[to, way] = part_sum[way * half_tokens : (way + 1) * half_tokens]
+
+        pre_part(hop.far)
+        pre_sum.start(0)
+        for way in range(2):
+            pre_part(hop.chips[way])
+        pre_sum.start(1)
+        pre_part(chip)
+        pre_sum.forward()
         lane.contract.take_all()
-        lane.cotangent.take_all()
+        cot_plane.finish()
         r.dz[...] = mul(flat(r.dy_all), r.wd[...], COLS_COLS)
-        lane.pre.take_all()
-
         tile = 64
 
-        def gelu_tile(i, none):
-            rows = part(i, tile)
-            pre = r.u_acc[rows, :]
-            for step in range(1, chips):
-                pre = pre + r.u_recv[lane.pre.source(step), rows, :].astype(F32)
-            square = pre * pre
-            curve = jnp.tanh(ROOT * pre * (1.0 + CUBE * square))
-            half = 0.5 * (1.0 + curve)
-            r.z[rows, :] = (pre * half).astype(BF16)
-            slope = half + 0.5 * pre * (1.0 - curve * curve) * (ROOT * (1.0 + 3.0 * CUBE * square))
-            r.du_all[chip, rows, :] = (r.dz[rows, :] * slope).astype(BF16)
-            return none
-
-        lax.fori_loop(0, tokens // tile, gelu_tile, None)
-        lane.d_pre.start_all()
-
-        for c in range(chips):
-            rows = slice(c * length, (c + 1) * length)
-            r.y_send[c] = mul(r.z[rows, :], r.wd[...]).astype(BF16)
+        for way in range(2):
+            pre_sum.take(way)
+
+            def gelu_tile(i, none, way=way):
+                rows = part(i, tile)
+                pre = pre_sum.total(way, rows)
+                square = pre * pre
+                curve = jnp.tanh(ROOT * pre * (1.0 + CUBE * square))
+                half = 0.5 * (1.0 + curve)
+                slope = half + 0.5 * pre * (1.0 - curve * curve) * (
+                    ROOT * (1.0 + 3.0 * CUBE * square)
+                )
+                rows = part(i + way * (half_tokens // tile), tile)
+                r.z[rows, :] = (pre * half).astype(BF16)
+                r.du_all[chip, rows, :] = (r.dz[rows, :] * slope).astype(BF16)
+                return none
+
+            lax.fori_loop(0, half_tokens // tile, gelu_tile, None)
+        d_pre.start()
+
+        def out_part(c):
+            rows = r.z[c * length : (c + 1) * length, :]
+            part_sum = mul(rows, r.wd[...]).astype(BF16)
+            for way in range(2):
+                r.y_send[c, way] = part_sum[way * half_rows : (way + 1) * half_rows]
+
+        out_part(0)
+        out_part(1)
+        total = mul(r.du_all[chip], r.wu[chip], COLS_COLS)
+        d_pre.forward()
+        out_part(2)
+        out_part(3)
         r.gc_send[...] = mul(r.z[:, part(1 - core, own_units)], flat(r.dy_all), ROWS_ROWS).astype(BF16)
         lane.g_contract.start_all()
 
-        total = mul(r.du_all[chip], r.wu[chip], COLS_COLS)
-        for step in range(1, chips):
-            lane.d_pre.take(step)
-            source = lane.d_pre.source(step)
-            total = total + mul(r.du_all[source], r.wu[source], COLS_COLS)
+        for way in range(2):
+            total = total + mul(r.du_all[hop.chips[way]], r.wu[hop.chips[way]], COLS_COLS)
+        d_pre.finish()
+        total = total + mul(r.du_all[hop.far], r.wu[hop.far], COLS_COLS)
         total = total.astype(BF16)
         for c in range(chips):
             for m in range(mp_size):
                 first = c * length + m * strip
                 r.dc_send[c, m] = total[first : first + strip]
         lane.d_second.start_all()
-        lane.out.start_all()
+        out_sum.start(0)
+        out_sum.start(1)
         r.own_contract[...] = mul(r.z[:, part(core, own_units)], flat(r.dy_all), ROWS_ROWS)
         for c in range(chips):
-            r.ge_send[c] = mul(flat(r.c_all, other), r.du_all[c], ROWS_ROWS).astype(BF16)
+            r.ge_send[:, c * units : (c + 1) * units] = mul(flat(r.c_all, other), r.du_all[c], ROWS_ROWS).astype(BF16)
         lane.g_expand.start_all()
         for c in range(chips):
             r.own_expand[:, c * units : (c + 1) * units] = mul(
                 flat(r.c_all, mine), r.du_all[c], ROWS_ROWS
             )
+        out_sum.forward()
         lane.d_second.take_all()
 
         def gathered(send, recv):
@@ -1076,6 +1212,13 @@
         lane.d_hidden.start_all()
         r.da_rows[mp] = r.da_mine[...]
         lane.d_hidden.take_all()
+        grad_out = mul(r.attended[...], flat(r.da_rows), ROWS_ROWS).astype(BF16)
+        for c in range(chips):
+            for k in range(2):
+                first = (2 * c + k) * out_rows
+                r.go_send[c, k] = grad_out[first : first + out_rows]
+        g_out_sum.start(0)
+        g_out_sum.start(1)
         d_attended = mul(flat(r.da_rows), flat(r.wo), COLS_COLS).astype(BF16)
         for p in range(pieces):
             for start in range(p * piece, (p + 1) * piece, HEAD_DIM):
@@ -1093,22 +1236,18 @@
                 for c in range(3):
                     first = c * piece + start % piece
                     r.dq_mine[p, :, first : first + HEAD_DIM] = thirds[c].astype(BF16)
-            lane.d_joint[p].start_all()
+            d_joint[p].start()
             r.dq_all[p, chip] = r.dq_mine[p]
 
-        lane.out.take_all()
-        total = r.y_send[chip].astype(F32)
-        for step in range(1, chips):
-            total = total + r.y_recv[lane.out.source(step)].astype(F32)
-        total = total.astype(BF16)
-        for m in range(mp_size):
-            r.y2_send[m] = total[m * strip : (m + 1) * strip]
+        g_out_sum.forward()
+        for way in range(2):
+            out_sum.take(way)
+            total = out_sum.total(way).astype(BF16)
+            for m in range(mp_size // 2):
+                r.y2_send[way * (mp_size // 2) + m] = total[m * strip : (m + 1) * strip]
         lane.out_strip.start_all()
-        grad_out = mul(r.attended[...], flat(r.da_rows), ROWS_ROWS).astype(BF16)
-        for c in range(chips):
-            for k in range(2):
-                first = (2 * c + k) * out_rows
-                r.go_send[c, k] = grad_out[first : first + out_rows]
+        for p in range(pieces):
+            d_joint[p].forward()
 
         def first_block(block):
             total = jnp.zeros((length, slab), F32)
@@ -1130,12 +1269,13 @@
 
         first_block(chip)
         first_send(chip, range(1, mp_size))
-        for step in range(1, chips):
-            for p in range(pieces):
-                lane.d_joint[p].take(step)
-            first_block(lane.d_joint[0].source(step))
-            first_send(lane.d_joint[0].source(step), range(mp_size))
-        lane.g_out.start_all()
+        for way in range(2):
+            first_block(hop.chips[way])
+            first_send(hop.chips[way], range(mp_size))
+        for p in range(pieces):
+            d_joint[p].finish()
+        first_block(hop.far)
+        first_send(hop.far, range(mp_size))
 
         def joint_grad(c, columns, target):
             for p in range(pieces):
@@ -1184,19 +1324,14 @@
         lane.g_contract.take_all()
         squares = folded(square(r.own_contract[...], r.far_contract[...]))
         lane.g_expand.take_all()
-        for c in range(chips):
-            squares = squares + folded(
-                square(r.own_expand[:, c * units : (c + 1) * units], r.far_expand[c])
-            )
+        squares = squares + folded(square(r.own_expand[...], r.far_expand[...]))
         lane.g_joint.take_all()
         for c in range(3):
             squares = squares + folded(square(r.own_joint[c], r.far_joint[c]))
 
-        lane.g_out.take_all()
         for k in range(2):
-            total = r.go_send[chip, k].astype(F32)
-            for step in range(1, chips):
-                total = total + r.go_recv[lane.g_out.source(step), k].astype(F32)
+            g_out_sum.take(k)
+            total = g_out_sum.total(k)
 
             @pl.when(core == k)
             def _():
@@ -1242,16 +1377,17 @@
         r.square_sum[...] = total + r.sq_far[...]
         for entry in every_lane:
             entry.sent_all()
-        for step in range(1, chips):
-            passing(step, False).wait_send()
+        for index in range(3):
+            passing(index, False).wait_send()
 
     vmem = pl.BlockSpec(memory_space=pltpu.VMEM)
     any_space = pl.BlockSpec(memory_space=pl.ANY)
     sem_shapes = [pltpu.SemaphoreType.DMA((4,))]
-    for name, kind in LANES.items():
-        count = 2 * pieces if name in PIECED else 2
-        sem_shapes += [pltpu.SemaphoreType.DMA((vars(groups)[kind].size,))] * count
-    sem_shapes += [pltpu.SemaphoreType.DMA((chips,))] * 2
+    for kind in LANES.values():
+        sem_shapes += [pltpu.SemaphoreType.DMA((vars(groups)[kind].size,))] * 2
+    sem_shapes += [pltpu.SemaphoreType.DMA((4,))] * 2 * (3 + pieces)
+    sem_shapes += [pltpu.SemaphoreType.DMA((6,))] * 2 * (3 + pieces)
+    sem_shapes += [pltpu.SemaphoreType.DMA((3,))] * 2
     results = pl.pallas_call(
         kernel,
         out_shape=list(outs.values()),
@@ -1271,12 +1407,10 @@
 def local(dp_size, mp_size, *arrays):
     params, firsts, seconds = arrays[3:8], arrays[8:13], arrays[13:18]
     r = layer(dp_size, mp_size, arrays[:8])
-    shard, hidden = params[2].shape
-    far_expand = jnp.swapaxes(r.far_expand, 0, 1).reshape(shard, hidden)
     grads = (
         r.own_joint + r.far_joint.astype(F32),
         r.own_out + r.far_out.astype(F32),
-        r.own_expand + far_expand.astype(F32),
+        r.own_expand + r.far_expand.astype(F32),
         r.own_contract + r.far_contract.astype(F32),
         r.own_norms[:4],
     )
@@ -1308,7 +1442,7 @@
         P(("mp", "dp"), None),
         P(None, "dp"),
     )
-    form = local if mesh.shape["dp"] <= 8 else local_steps
+    form = local if mesh.shape["dp"] == 8 else local_steps
     return jax.shard_map(
         functools.partial(form, mesh.shape["dp"], mesh.shape["mp"]),
         mesh=mesh,

time: 251 us -> 231 us (0.920)
  Pallas kernels: 223 us -> 206 us
    pallas_call x1, Pallas kernels: 223 us -> 206 us  [layer(): pl.pallas_call(kernel, out_shape=list(outs.values()), in_specs=[vmem] * 3...]
    unnamed x44 -> x36, local copies, waits for them, and re-layouts: 5.59 us -> 3.45 us
where the time goes in v4:
time: 231 us
  Pallas kernels  206 us (89%)
  other arithmetic  18.2 us (8%)
  local copies, waits for them, and re-layouts  4.64 us (2%)
  between operations  2.72 us (1%)
    pallas_call x1, Pallas kernels, layer(): pl.pallas_call(kernel, out_shape=list(outs.values()), in_specs=[vmem] * 3...  206 us
    convert_element_type x4, other arithmetic, local(): copies = [entry[2].astype(BF16) for entry in updates]  18.2 us

profile of v4, /device:TPU:0, one launch (start us, length us, event | category | flops | bytes accessed | tf_op | source)
XLA Modules:
  0.0 231.1 jit_solution(5810467161656131423)
XLA Ops:
  0.7 0.0 copy-start
  0.7 205.5 %shard_map.393 = (bf16[128,2048]{1,0:T(8,128)(2,1)}, f32[128,2048]{1,0:T(8,128)}, f32[3,256,512]{2,1,0:T(8,128)}, f32[64,2048]{1,0:T(8,128)}, f32[256,2048]{1,0:...) custom-call(bf16[128,2048]{1,0:T(8,128)(2,1)} %refs_0_.1, ...), custom_call_target="tpu_custom_call" | custom-call | tf_op jit(solution)/shard_map/pallas_call | solution.py:1391
  206.2 1.2 slice.7
  208.1 0.0 copy-done
  208.1 0.0 copy-start.2
  208.1 0.0 copy-start.8
  208.2 0.0 copy-start.9
  208.2 0.0 copy-start.10
  208.2 0.0 copy-start.12
  208.2 0.0 copy-start.5
  208.2 0.0 copy-start.7
  208.2 12.4 %fusion.7 = (bf16[256,2048]{1,0:T(8,128)(2,1)}, f32[256,2048]{1,0:T(8,128)}, f32[256,2048]{1,0:T(8,128)}, f32[256,2048]{1,0:T(8,128)}, f32[256,2048]{1,0:T(8,128...) fusion(f32[256,2048]{1,0:T(8,128)} %refs_6_.1, ...), kind=kLoop, calls=%fused_computation.25 | loop fusion | flops 19922944 | bytes 37748740 | tf_op jit(solution)/shard_map/convert_element_type | solution.py:1423
  220.6 0.0 copy-done.2
  220.6 0.0 copy-done.8
  220.6 0.0 copy-done.9
  220.6 0.0 copy-done.10
  220.6 0.0 copy-done.12
  220.7 0.0 copy-start.1
  220.7 0.0 copy-start.3
  220.7 0.0 copy-start.4
  220.7 1.6 fusion.11
  222.2 0.0 copy-done.5
  222.2 0.0 copy-done.7
  222.3 0.5 copy-done.1
  222.7 0.7 copy-done.3
  223.4 0.5 copy-done.4
  223.9 0.0 copy-start.13
  223.9 0.0 copy-start.14
  223.9 0.0 copy-start.15
  223.9 0.0 copy-start.16
  223.9 0.0 copy-start.11
  223.9 0.0 copy-start.6
  223.9 3.6 %fusion.13 = (bf16[3,256,512]{2,1,0:T(8,128)(2,1)}, f32[3,256,512]{2,1,0:T(8,128)}, f32[3,256,512]{2,1,0:T(8,128)}, f32[3,256,512]{2,1,0:T(8,128)}, f32[3,256,512]{2,1,0:T(8,128)}) fusion(f32[3,256,512]{2,1,0:T(8,128)S(1)} %copy-done.1, f32[]{:T(128)S(6)} %min_shard_map.3, f32[3,256,512]{2,1,0:T(8,128)S(1)} %copy-done.3, f32[3,256,512]{2,1,0:T(8,128)S(1)} %copy-done.4, ...), kind=kLoop, calls=%fused_computation.28 | loop fusion | flops 7471104 | bytes 14155780 | tf_op jit(solution)/shard_map/convert_element_type | solution.py:1423
  227.5 0.0 copy-done.13
  227.5 0.0 copy-done.14
  227.5 0.0 copy-done.15
  227.5 0.0 copy-done.16
  227.6 0.6 fusion.5
  228.2 0.0 copy-done.11
  228.2 0.8 copy.48
  229.0 0.0 copy-done.6
  229.0 1.0 copy.49
Async XLA Ops:
  0.7 207.5 %copy-start = (f32[256,2048]{1,0:T(8,128)S(1)}, f32[256,2048]{1,0:T(8,128)}, u32[]{:S(2)}) copy-start(f32[256,2048]{1,0:T(8,128)} %refs_5_.1) | copy-start | bytes 6291460
  208.1 12.5 %copy-start.2 = (f32[64,2048]{1,0:T(8,128)S(1)}, f32[64,2048]{1,0:T(8,128)}, u32[]{:S(2)}) copy-start(f32[64,2048]{1,0:T(8,128)} %refs_4_.1) | copy-start | bytes 1572868
  208.1 12.5 %copy-start.8 = (f32[64,2048]{1,0:T(8,128)S(1)}, f32[64,2048]{1,0:T(8,128)}, u32[]{:S(2)}) copy-start(f32[64,2048]{1,0:T(8,128)} %param.32) | copy-start | bytes 1572868
  208.2 12.5 %copy-start.9 = (f32[64,2048]{1,0:T(8,128)S(1)}, f32[64,2048]{1,0:T(8,128)}, u32[]{:S(2)}) copy-start(f32[64,2048]{1,0:T(8,128)} %param.27) | copy-start | bytes 1572868
  208.2 12.5 %copy-start.10 = (f32[64,2048]{1,0:T(8,128)S(1)}, f32[64,2048]{1,0:T(8,128)}, u32[]{:S(2)}) copy-start(f32[64,2048]{1,0:T(8,128)} %get-tuple-element.44) | copy-start | bytes 1572868
  208.2 12.5 %copy-start.12 = (bf16[64,2048]{1,0:T(8,128)(2,1)S(1)}, bf16[64,2048]{1,0:T(8,128)(2,1)}, u32[]{:S(2)}) copy-start(bf16[64,2048]{1,0:T(8,128)(2,1)} %get-tuple-element.45) | copy-start | bytes 786436
  208.2 14.1 %copy-start.5 = (f32[3,256,512]{2,1,0:T(8,128)S(1)}, f32[3,256,512]{2,1,0:T(8,128)}, u32[]{:S(2)}) copy-start(f32[3,256,512]{2,1,0:T(8,128)} %get-tuple-element.42) | copy-start | bytes 4718596
  208.2 14.0 %copy-start.7 = (bf16[3,256,512]{2,1,0:T(8,128)(2,1)S(1)}, bf16[3,256,512]{2,1,0:T(8,128)(2,1)}, u32[]{:S(2)}) copy-start(bf16[3,256,512]{2,1,0:T(8,128)(2,1)} %get-tuple-element.43) | copy-start | bytes 2359300
  220.7 2.1 copy-start.1
  220.7 2.7 %copy-start.3 = (f32[3,256,512]{2,1,0:T(8,128)S(1)}, f32[3,256,512]{2,1,0:T(8,128)}, u32[]{:S(2)}) copy-start(f32[3,256,512]{2,1,0:T(8,128)} %param.31) | copy-start | bytes 4718596
  220.7 3.2 %copy-start.4 = (f32[3,256,512]{2,1,0:T(8,128)S(1)}, f32[3,256,512]{2,1,0:T(8,128)}, u32[]{:S(2)}) copy-start(f32[3,256,512]{2,1,0:T(8,128)} %param.26) | copy-start | bytes 4718596
  223.9 3.7 %copy-start.13 = (f32[4,256]{1,0:T(4,128)S(1)}, f32[4,256]{1,0:T(4,128)}, u32[]{:S(2)}) copy-start(f32[4,256]{1,0:T(4,128)} %refs_7_.1) | copy-start | bytes 12292
  223.9 3.7 %copy-start.14 = (f32[4,256]{1,0:T(4,128)S(1)}, f32[4,256]{1,0:T(4,128)}, u32[]{:S(2)}) copy-start(f32[4,256]{1,0:T(4,128)} %param.35) | copy-start | bytes 12292
  223.9 3.7 %copy-start.15 = (f32[4,256]{1,0:T(4,128)S(1)}, f32[4,256]{1,0:T(4,128)}, u32[]{:S(2)}) copy-start(f32[4,256]{1,0:T(4,128)} %param.30) | copy-start | bytes 12292
  223.9 3.7 %copy-start.16 = (f32[8,256]{1,0:T(8,128)S(1)}, f32[8,256]{1,0:T(8,128)}, u32[]{:S(2)}) copy-start(f32[8,256]{1,0:T(8,128)} %get-tuple-element.50) | copy-start | bytes 24580
  223.9 4.3 %copy-start.11 = (bf16[128,2048]{1,0:T(8,128)(2,1)S(1)}, bf16[128,2048]{1,0:T(8,128)(2,1)}, u32[]{:S(2)}) copy-start(bf16[128,2048]{1,0:T(8,128)(2,1)} %get-tuple-element.110) | copy-start | bytes 1572868
  223.9 5.1 %copy-start.6 = (f32[128,2048]{1,0:T(8,128)S(1)}, f32[128,2048]{1,0:T(8,128)}, u32[]{:S(2)}) copy-start(f32[128,2048]{1,0:T(8,128)} %get-tuple-element.111) | copy-start | bytes 3145732

commit v5 on v4

--- a/solution.py
+++ b/solution.py
@@ -766,6 +766,8 @@
     squares_pair=PAIR,
 )
 
+HALVED = dict(branch=2, second=2, d_second=2, d_hidden=2)
+
 
 def layer(dp_size, mp_size, operands):
     x, segments, cotangent, joint_w, out_w, expand_w, contract_w, norms = operands
@@ -782,25 +784,37 @@
     out_rows = out_w.shape[0]
     strip = length // mp_size
     tokens = chips * length
-    wide = 3 * width
+    half_strip = strip // 2
+    half_rows = length // 2
+    half_tokens = tokens // 2
     pieces = max(1, width // (2 * HEAD_DIM))
     piece = width // pieces
 
     outs = dict(
         layer_output=shape((length, model)),
         input_grad=shape((length, model), F32),
-        own_joint=shape((3, shard, width), F32),
-        own_out=shape((out_rows, model), F32),
-        own_expand=shape((shard, hidden), F32),
-        own_contract=shape((own_units, model), F32),
-        own_norms=shape((8, shard), F32),
+        own_norms=shape((4, shard), F32),
         square_sum=shape((8, 128), F32),
-        far_joint=shape((3, shard, width)),
-        far_out=shape((out_rows, model)),
-        far_expand=shape((shard, hidden)),
-        far_contract=shape((own_units, model)),
+    )
+    homes = dict(
+        home_joint=shape((3, shard, width), F32),
+        home_out=shape((out_rows, model), F32),
+        home_expand=shape((shard, hidden), F32),
+        home_contract=shape((own_units, model), F32),
+        home_far_joint=shape((3, shard, width)),
+        home_far_out=shape((out_rows, model)),
+        home_far_expand=shape((shard, hidden)),
+        home_far_contract=shape((own_units, model)),
     )
     scratch = dict(
+        own_joint=((3, shard, width), F32),
+        own_out=((out_rows, model), F32),
+        own_expand=((shard, hidden), F32),
+        own_contract=((own_units, model), F32),
+        far_joint=((3, shard, width), BF16),
+        far_out=((out_rows, model), BF16),
+        far_expand=((shard, hidden), BF16),
+        far_contract=((own_units, model), BF16),
         norm_all=((dp_size, 4, shard), F32),
         a_mine=((chips, length, slab), BF16),
         a_all=((chips, length, slab), BF16),
@@ -812,29 +826,30 @@
         j_recv=((pieces, 3, 2, length // 2, 3 * piece), BF16),
         j_mid=((pieces, 2, length // 2, 3 * piece), BF16),
         joint=((pieces, length, 3 * piece), BF16),
-        dy_all=((chips, length, model), BF16),
+        dy_mine=((2, half_rows, model), BF16),
+        dy_all=((chips, 2, half_rows, model), BF16),
         attended=((length, width), BF16),
-        b_send=((mp_size, strip, model), BF16),
-        b_recv=((mp_size, strip, model), BF16),
-        hid=((strip, model), F32),
-        c_mine=((chips, strip, slab), BF16),
-        c_all=((chips, mp_size, strip, slab), BF16),
-        u_send=((chips, 2, tokens // 2, units), BF16),
-        u_recv=((3, 2, tokens // 2, units), BF16),
-        u_mid=((2, tokens // 2, units), BF16),
-        dz=((tokens, units), F32),
-        z=((tokens, units), BF16),
-        du_all=((chips, tokens, units), BF16),
+        b_send=((2, mp_size, half_strip, model), BF16),
+        b_recv=((2, mp_size, half_strip, model), BF16),
+        hid=((2, half_strip, model), F32),
+        c_mine=((2, chips, half_strip, slab), BF16),
+        c_all=((2, chips, mp_size, half_strip, slab), BF16),
+        u_send=((2, chips, 2, tokens // 4, units), BF16),
+        u_recv=((2, 3, 2, tokens // 4, units), BF16),
+        u_mid=((2, 2, tokens // 4, units), BF16),
+        dz=((2, half_tokens, units), F32),
+        z=((2, half_tokens, units), BF16),
+        du_all=((2, chips, half_tokens, units), BF16),
         y_send=((chips, 2, length // 2, model), BF16),
         y_recv=((3, 2, length // 2, model), BF16),
         y_mid=((2, length // 2, model), BF16),
         gc_send=((own_units, model), BF16),
-        dc_send=((chips, mp_size, strip, slab), BF16),
-        dc_recv=((chips, mp_size, strip, slab), BF16),
+        dc_send=((2, chips, mp_size, half_strip, slab), BF16),
+        dc_recv=((2, chips, mp_size, half_strip, slab), BF16),
         ge_send=((shard, hidden), BF16),
-        dh=((strip, model), F32),
-        da_mine=((strip, model), BF16),
-        da_rows=((mp_size, strip, model), BF16),
+        dh=((2, half_strip, model), F32),
+        da_mine=((2, half_strip, model), BF16),
+        da_rows=((mp_size, 2, half_strip, model), BF16),
         dq_mine=((pieces, length, 3 * piece), BF16),
         dq_all=((pieces, chips, length, 3 * piece), BF16),
         go_send=((chips, 2, out_rows, model), BF16),
@@ -850,8 +865,8 @@
         gj_send=((3, shard, width), BF16),
         ig_mine=((strip, model), BF16),
         ig_rows=((mp_size, strip, model), BF16),
-        gn_send=((chips, 8, slab), F32),
-        gn_recv=((chips * mp_size, 8, slab), F32),
+        gn_send=((chips, 8, shard), F32),
+        gn_recv=((chips * mp_size, 8, shard), F32),
         gn_pair=((8, shard), F32),
         gn_far=((8, shard), F32),
         sq_mine=((8, 128), F32),
@@ -862,12 +877,12 @@
     in_names = dict(
         x=0, seg_row=1, cot=2, f_joint=3, f_out=4, f_expand=5, f_contract=6, norm_own=7
     )
-    names = list(in_names) + list(outs) + list(scratch)
+    names = list(in_names) + list(outs) + list(homes) + list(scratch)
 
     def kernel(*refs):
         r = SimpleNamespace(**dict(zip(names, refs)))
         sems = refs[len(names) :]
-        load_sems = sems[0]
+        load_sems, home_sems = sems[:2]
         dp, mp = lax.axis_index("dp"), lax.axis_index("mp")
         core, chip = lax.rem(dp, 2), lax.div(dp, 2)
         mine, other = part(core, shard), part(1 - core, shard)
@@ -893,18 +908,28 @@
                 r.wd.at[part(s, own_units), :],
                 r.wd.at[part(s, own_units), :],
             ),
-            branch=lambda s, t: (r.b_send.at[t], r.b_recv.at[s]),
-            second=lambda s, t: (
-                r.c_mine.at[lax.div(t, mp_size)],
-                r.c_all.at[lax.div(s, mp_size), lax.rem(s, mp_size)],
-            ),
+            branch=[
+                lambda s, t, h=h: (r.b_send.at[h, t], r.b_recv.at[h, s]) for h in range(2)
+            ],
+            second=[
+                lambda s, t, h=h: (
+                    r.c_mine.at[h, lax.div(t, mp_size)],
+                    r.c_all.at[h, lax.div(s, mp_size), lax.rem(s, mp_size)],
+                )
+                for h in range(2)
+            ],
             g_contract=lambda s, t: (r.gc_send, r.far_contract),
-            d_second=lambda s, t: (
-                r.dc_send.at[lax.div(t, mp_size), lax.rem(t, mp_size)],
-                r.dc_recv.at[lax.div(s, mp_size), lax.rem(s, mp_size)],
-            ),
+            d_second=[
+                lambda s, t, h=h: (
+                    r.dc_send.at[h, lax.div(t, mp_size), lax.rem(t, mp_size)],
+                    r.dc_recv.at[h, lax.div(s, mp_size), lax.rem(s, mp_size)],
+                )
+                for h in range(2)
+            ],
             g_expand=lambda s, t: (r.ge_send, r.far_expand),
-            d_hidden=lambda s, t: (r.da_mine, r.da_rows.at[s]),
+            d_hidden=[
+                lambda s, t, h=h: (r.da_mine.at[h], r.da_rows.at[s, h]) for h in range(2)
+            ],
             g_out_pair=lambda s, t: (r.go_pair.at[t], r.far_out),
             out_strip=lambda s, t: (r.y2_send.at[t], r.y2_recv.at[s]),
             d_first=lambda s, t: (
@@ -921,15 +946,20 @@
         )
         lane = SimpleNamespace()
         every_lane = []
-        used = iter(sems[1:])
+        used = iter(sems[2:])
 
         def pair_of():
             return (next(used), next(used))
 
         for name, kind in LANES.items():
             group = vars(groups)[kind]
-            setattr(lane, name, Lane(group, group.me(), pair_of(), views[name]))
-            every_lane.append(vars(lane)[name])
+            several = name in HALVED
+            lanes = [
+                Lane(group, group.me(), pair_of(), view)
+                for view in (views[name] if several else [views[name]])
+            ]
+            every_lane += lanes
+            setattr(lane, name, lanes if several else lanes[0])
         hop = Hop(dp, mp)
 
         def gather(own, block, half):
@@ -945,14 +975,17 @@
             return ref.at[pl.ds(way * rows, rows), :]
 
         out_plane = gather(r.wo.at[dp], lambda c: r.wo.at[2 * c + core], row_half)
-        cot_plane = gather(r.cot, lambda c: r.dy_all.at[c], row_half)
-        d_pre = gather(r.du_all.at[chip], lambda c: r.du_all.at[c], row_half)
+        cot_plane = gather(r.dy_mine, lambda c: r.dy_all.at[c], lambda ref, way: ref.at[way])
+        d_pre = [
+            gather(r.du_all.at[h, chip], lambda c, h=h: r.du_all.at[h, c], row_half)
+            for h in range(2)
+        ]
         d_joint = [
             gather(r.dq_mine.at[p], lambda c, p=p: r.dq_all.at[p, c], row_half)
             for p in range(pieces)
         ]
         joint = [reduce(r.j_send.at[p], r.j_recv.at[p], r.j_mid.at[p]) for p in range(pieces)]
-        pre_sum = reduce(r.u_send, r.u_recv, r.u_mid)
+        pre_sum = [reduce(r.u_send.at[h], r.u_recv.at[h], r.u_mid.at[h]) for h in range(2)]
         out_sum = reduce(r.y_send, r.y_recv, r.y_mid)
         g_out_sum = reduce(r.go_send, r.go_recv, r.go_mid)
         pass_sems = pair_of()
@@ -982,6 +1015,12 @@
         ]
         for load in (loads[1], loads[0], loads[2], loads[3]):
             load.start()
+
+        leaving = []
+
+        def send_home(index, source, target):
+            leaving.append(pltpu.make_async_copy(source, target, home_sems.at[index]))
+            leaving[-1].start()
 
         barrier = pltpu.get_barrier_semaphore()
 
@@ -1031,8 +1070,6 @@
 
         lane.joint_weight.take_all()
 
-        half_rows = length // 2
-
         def joint_part(p, block):
             rows = r.a_all[block]
             for c in range(3):
@@ -1057,6 +1094,12 @@
             joint_part(p, hop.far)
             joint[p].start(0)
             joint_part(p, chip)
+        for h in range(2):
+            for m in range(mp_size):
+                first = m * strip + h * half_strip
+                r.dy_mine[h, m * half_strip : (m + 1) * half_strip, :] = r.cot[
+                    first : first + half_strip, :
+                ]
         out_plane.forward()
         for index in range(2):
             passing(index, False).start()
@@ -1095,130 +1138,150 @@
         for index in range(3):
             passing(index, True).wait_recv()
         branch = mul(r.attended[...], flat(r.wo)).astype(BF16)
-        for m in range(mp_size):
-            r.b_send[m] = branch[m * strip : (m + 1) * strip]
-        lane.branch.start_all()
-        r.dy_all[chip] = r.cot[...]
+        for h in range(2):
+            for m in range(mp_size):
+                first = m * strip + h * half_strip
+                r.b_send[h, m] = branch[first : first + half_strip]
+            lane.branch[h].start_all()
+        r.dy_all[chip] = r.dy_mine[...]
         cot_plane.forward()
-        lane.branch.take_all()
-        here = part(mp, strip)
-        total = r.x[here, :].astype(F32) + r.b_send[mp].astype(F32)
-        for step in range(1, mp_size):
-            total = total + r.b_recv[lane.branch.source(step)].astype(F32)
-        r.hid[...] = total
-        centered, inverse = standardise(total)
-        for b in range(dp_size):
-            columns = slice(b * shard, (b + 1) * shard)
-            r.c_mine[b // 2, :, (b % 2) * shard : (b % 2 + 1) * shard] = (
-                centered[:, columns] * inverse * norm_row(2, b) + norm_row(3, b)
-            ).astype(BF16)
-        lane.second.start_all()
-        r.c_all[chip, mp] = r.c_mine[chip]
+
+        def here(h):
+            return pl.ds(pl.multiple_of(mp * strip + h * half_strip, half_strip), half_strip)
+
+        for h in range(2):
+            lane.branch[h].take_all()
+            total = r.x[here(h), :].astype(F32) + r.b_send[h, mp].astype(F32)
+            for step in range(1, mp_size):
+                total = total + r.b_recv[h, lane.branch[h].source(step)].astype(F32)
+            r.hid[h] = total
+            centered, inverse = standardise(total)
+            for b in range(dp_size):
+                columns = slice(b * shard, (b + 1) * shard)
+                r.c_mine[h, b // 2, :, (b % 2) * shard : (b % 2 + 1) * shard] = (
+                    centered[:, columns] * inverse * norm_row(2, b) + norm_row(3, b)
+                ).astype(BF16)
+            lane.second[h].start_all()
+            r.c_all[h, chip, mp] = r.c_mine[h, chip]
         lane.expand.take_all()
-        lane.second.take_all()
-
-        half_tokens = tokens // 2
-
-        def pre_part(to):
-            part_sum = mul(flat(r.c_all), r.wu[to]).astype(BF16)
+
+        def dy_half(h):
+            return r.dy_all[:, h].reshape(half_tokens, model)
+
+        quarter = half_tokens // 2
+
+        def pre_part(h, to):
+            part_sum = mul(flat(r.c_all.at[h]), r.wu[to]).astype(BF16)
             for way in range(2):
-                r.u_send[to, way] = part_sum[way * half_tokens : (way + 1) * half_tokens]
-
-        pre_part(hop.far)
-        pre_sum.start(0)
-        for way in range(2):
-            pre_part(hop.chips[way])
-        pre_sum.start(1)
-        pre_part(chip)
-        pre_sum.forward()
-        lane.contract.take_all()
-        cot_plane.finish()
-        r.dz[...] = mul(flat(r.dy_all), r.wd[...], COLS_COLS)
+                r.u_send[h, to, way] = part_sum[way * quarter : (way + 1) * quarter]
+
+        for h in range(2):
+            lane.second[h].take_all()
+            pre_part(h, hop.far)
+            pre_sum[h].start(0)
+            for way in range(2):
+                pre_part(h, hop.chips[way])
+            pre_sum[h].start(1)
+            pre_part(h, chip)
+            if h == 0:
+                lane.contract.take_all()
+                cot_plane.finish()
+            r.dz[h] = mul(dy_half(h), r.wd[...], COLS_COLS)
+            pre_sum[h].forward()
         tile = 64
 
-        for way in range(2):
-            pre_sum.take(way)
-
-            def gelu_tile(i, none, way=way):
-                rows = part(i, tile)
-                pre = pre_sum.total(way, rows)
-                square = pre * pre
-                curve = jnp.tanh(ROOT * pre * (1.0 + CUBE * square))
-                half = 0.5 * (1.0 + curve)
-                slope = half + 0.5 * pre * (1.0 - curve * curve) * (
-                    ROOT * (1.0 + 3.0 * CUBE * square)
-                )
-                rows = part(i + way * (half_tokens // tile), tile)
-                r.z[rows, :] = (pre * half).astype(BF16)
-                r.du_all[chip, rows, :] = (r.dz[rows, :] * slope).astype(BF16)
-                return none
-
-            lax.fori_loop(0, half_tokens // tile, gelu_tile, None)
-        d_pre.start()
-
-        def out_part(c):
-            rows = r.z[c * length : (c + 1) * length, :]
-            part_sum = mul(rows, r.wd[...]).astype(BF16)
+        for h in range(2):
             for way in range(2):
-                r.y_send[c, way] = part_sum[way * half_rows : (way + 1) * half_rows]
-
-        out_part(0)
-        out_part(1)
-        total = mul(r.du_all[chip], r.wu[chip], COLS_COLS)
-        d_pre.forward()
-        out_part(2)
-        out_part(3)
-        r.gc_send[...] = mul(r.z[:, part(1 - core, own_units)], flat(r.dy_all), ROWS_ROWS).astype(BF16)
-        lane.g_contract.start_all()
-
-        for way in range(2):
-            total = total + mul(r.du_all[hop.chips[way]], r.wu[hop.chips[way]], COLS_COLS)
-        d_pre.finish()
-        total = total + mul(r.du_all[hop.far], r.wu[hop.far], COLS_COLS)
-        total = total.astype(BF16)
-        for c in range(chips):
-            for m in range(mp_size):
-                first = c * length + m * strip
-                r.dc_send[c, m] = total[first : first + strip]
-        lane.d_second.start_all()
+                pre_sum[h].take(way)
+
+                def gelu_tile(i, none, h=h, way=way):
+                    rows = part(i, tile)
+                    pre = pre_sum[h].total(way, rows)
+                    square = pre * pre
+                    curve = jnp.tanh(ROOT * pre * (1.0 + CUBE * square))
+                    half = 0.5 * (1.0 + curve)
+                    slope = half + 0.5 * pre * (1.0 - curve * curve) * (
+                        ROOT * (1.0 + 3.0 * CUBE * square)
+                    )
+                    rows = part(i + way * (quarter // tile), tile)
+                    r.z[h, rows, :] = (pre * half).astype(BF16)
+                    r.du_all[h, chip, rows, :] = (r.dz[h, rows, :] * slope).astype(BF16)
+                    return none
+
+                lax.fori_loop(0, quarter // tile, gelu_tile, None)
+            d_pre[h].start()
+
+        def out_part(h):
+            part_sum = mul(r.z[h], r.wd[...]).astype(BF16)
+            for c in range(chips):
+                r.y_send[c, h] = part_sum[c * half_rows : (c + 1) * half_rows]
+
+        def second_part(h, source):
+            return mul(r.du_all[h, source], r.wu[source], COLS_COLS)
+
+        d_pre[0].forward()
+        for h in range(2):
+            out_part(h)
+            total = second_part(h, chip)
+            for way in range(2):
+                total = total + second_part(h, hop.chips[way])
+            if h == 0:
+                d_pre[1].forward()
+            d_pre[h].finish()
+            total = (total + second_part(h, hop.far)).astype(BF16)
+            for c in range(chips):
+                for m in range(mp_size):
+                    first = (c * mp_size + m) * half_strip
+                    r.dc_send[h, c, m] = total[first : first + half_strip]
+            lane.d_second[h].start_all()
         out_sum.start(0)
         out_sum.start(1)
-        r.own_contract[...] = mul(r.z[:, part(core, own_units)], flat(r.dy_all), ROWS_ROWS)
-        for c in range(chips):
-            r.ge_send[:, c * units : (c + 1) * units] = mul(flat(r.c_all, other), r.du_all[c], ROWS_ROWS).astype(BF16)
-        lane.g_expand.start_all()
-        for c in range(chips):
-            r.own_expand[:, c * units : (c + 1) * units] = mul(
-                flat(r.c_all, mine), r.du_all[c], ROWS_ROWS
-            )
-        out_sum.forward()
-        lane.d_second.take_all()
-
-        def gathered(send, recv):
+
+        def contract_grad(columns):
+            return sum(mul(r.z[h, :, columns], dy_half(h), ROWS_ROWS) for h in range(2))
+
+        def gathered(recv, rows):
             blocks = []
             for c in range(chips):
-                block = jnp.zeros((strip, slab), F32)
+                block = jnp.zeros((rows, slab), F32)
                 for m in range(mp_size):
                     block = block + recv[c, m].astype(F32)
                 blocks.append(block)
             return jnp.concatenate(blocks, axis=1)
 
-        r.dc_recv[chip, mp] = r.dc_send[chip, mp]
-        d_normed = gathered(r.dc_send, r.dc_recv)
-        back, gain_two, shift_two = norm_back(d_normed, r.hid[...], norm_row(2))
-        d_hidden = r.cot[here, :].astype(F32) + back
-        r.dh[...] = d_hidden
-        r.da_mine[...] = d_hidden.astype(BF16)
-        lane.d_hidden.start_all()
-        r.da_rows[mp] = r.da_mine[...]
-        lane.d_hidden.take_all()
-        grad_out = mul(r.attended[...], flat(r.da_rows), ROWS_ROWS).astype(BF16)
+        r.gc_send[...] = contract_grad(part(1 - core, own_units)).astype(BF16)
+        lane.g_contract.start_all()
+        gain_two, shift_two = 0.0, 0.0
+        for h in range(2):
+            lane.d_second[h].take_all()
+            r.dc_recv[h, chip, mp] = r.dc_send[h, chip, mp]
+            d_normed = gathered(r.dc_recv.at[h], half_strip)
+            back, gain, shift = norm_back(d_normed, r.hid[h], norm_row(2))
+            gain_two, shift_two = gain_two + gain, shift_two + shift
+            d_hidden = r.cot[here(h), :].astype(F32) + back
+            r.dh[h] = d_hidden
+            r.da_mine[h] = d_hidden.astype(BF16)
+            lane.d_hidden[h].start_all()
+            r.da_rows[mp, h] = r.da_mine[h]
+        out_sum.forward()
         for c in range(chips):
-            for k in range(2):
-                first = (2 * c + k) * out_rows
-                r.go_send[c, k] = grad_out[first : first + out_rows]
-        g_out_sum.start(0)
-        g_out_sum.start(1)
+            r.ge_send[:, c * units : (c + 1) * units] = mul(
+                flat(r.c_all, other), flat(r.du_all.at[:, c]), ROWS_ROWS
+            ).astype(BF16)
+        lane.g_expand.start_all()
+        r.own_contract[...] = contract_grad(part(core, own_units))
+        send_home(3, r.own_contract, r.home_contract)
+        for h in range(2):
+            lane.d_hidden[h].take_all()
+
+        for way in range(2):
+            out_sum.take(way)
+            total = out_sum.total(way).astype(BF16)
+            for m in range(mp_size):
+                r.y2_send[m, way * half_strip : (way + 1) * half_strip, :] = total[
+                    m * half_strip : (m + 1) * half_strip
+                ]
+        lane.out_strip.start_all()
         d_attended = mul(flat(r.da_rows), flat(r.wo), COLS_COLS).astype(BF16)
         for p in range(pieces):
             for start in range(p * piece, (p + 1) * piece, HEAD_DIM):
@@ -1239,15 +1302,25 @@
             d_joint[p].start()
             r.dq_all[p, chip] = r.dq_mine[p]
 
-        g_out_sum.forward()
-        for way in range(2):
-            out_sum.take(way)
-            total = out_sum.total(way).astype(BF16)
-            for m in range(mp_size // 2):
-                r.y2_send[way * (mp_size // 2) + m] = total[m * strip : (m + 1) * strip]
-        lane.out_strip.start_all()
+        grad_out = mul(r.attended[...], flat(r.da_rows), ROWS_ROWS).astype(BF16)
+        for c in range(chips):
+            for k in range(2):
+                first = (2 * c + k) * out_rows
+                r.go_send[c, k] = grad_out[first : first + out_rows]
         for p in range(pieces):
             d_joint[p].forward()
+        lane.out_strip.take_all()
+        total = r.hid[...].reshape(strip, model) + r.y2_send[mp].astype(F32)
+        for step in range(1, mp_size):
+            total = total + r.y2_recv[lane.out_strip.source(step)].astype(F32)
+        r.y_mine[...] = total.astype(BF16)
+        lane.out_rows.start_all()
+        r.layer_output[part(mp, strip), :] = r.y_mine[...]
+        for c in range(chips):
+            r.own_expand[:, c * units : (c + 1) * units] = mul(
+                flat(r.c_all, mine), flat(r.du_all.at[:, c]), ROWS_ROWS
+            )
+        send_home(2, r.own_expand, r.home_expand)
 
         def first_block(block):
             total = jnp.zeros((length, slab), F32)
@@ -1276,6 +1349,8 @@
             d_joint[p].finish()
         first_block(hop.far)
         first_send(hop.far, range(mp_size))
+        g_out_sum.start(0)
+        g_out_sum.start(1)
 
         def joint_grad(c, columns, target):
             for p in range(pieces):
@@ -1290,27 +1365,21 @@
         lane.g_joint.start_all()
         for c in range(3):
             joint_grad(c, mine, r.own_joint)
-        lane.out_strip.take_all()
-        total = r.hid[...] + r.y2_send[mp].astype(F32)
-        for step in range(1, mp_size):
-            total = total + r.y2_recv[lane.out_strip.source(step)].astype(F32)
-        r.y_mine[...] = total.astype(BF16)
-        lane.out_rows.start_all()
-        r.layer_output[here, :] = r.y_mine[...]
+        send_home(0, r.own_joint, r.home_joint)
+        g_out_sum.forward()
 
         lane.d_first.take_all()
         r.df_recv[chip, mp] = r.df_send[chip, mp]
-        d_normed = gathered(r.df_send, r.df_recv)
-        back, gain_one, shift_one = norm_back(d_normed, r.x[here, :].astype(F32), norm_row(0))
-        grad = r.dh[...] + back
+        d_normed = gathered(r.df_recv, strip)
+        back, gain_one, shift_one = norm_back(d_normed, r.x[part(mp, strip), :].astype(F32), norm_row(0))
+        grad = r.dh[...].reshape(strip, model) + back
         r.ig_mine[...] = grad.astype(BF16)
         lane.in_rows.start_all()
-        r.input_grad[here, :] = grad
-        for c in range(chips):
-            columns = slice(c * slab, (c + 1) * slab)
-            for index, row in enumerate((gain_one, shift_one, gain_two, shift_two)):
-                r.gn_send[c, index : index + 1, :] = row[:, columns]
-            r.gn_send[c, 4:8, :] = jnp.zeros((4, slab), F32)
+        r.input_grad[part(mp, strip), :] = grad
+        for index, row in enumerate((gain_one, shift_one, gain_two, shift_two)):
+            for b in range(dp_size):
+                place = (b % 2) * 4 + index
+                r.gn_send[b // 2, place : place + 1, :] = row[:, b * shard : (b + 1) * shard]
         lane.g_norms.start_all()
         r.gn_recv[cross_me] = r.gn_send[chip]
 
@@ -1322,10 +1391,13 @@
             return sum(row[:, i : i + 128] for i in range(0, row.shape[1], 128))
 
         lane.g_contract.take_all()
+        send_home(7, r.far_contract, r.home_far_contract)
         squares = folded(square(r.own_contract[...], r.far_contract[...]))
         lane.g_expand.take_all()
+        send_home(6, r.far_expand, r.home_far_expand)
         squares = squares + folded(square(r.own_expand[...], r.far_expand[...]))
         lane.g_joint.take_all()
+        send_home(4, r.far_joint, r.home_far_joint)
         for c in range(3):
             squares = squares + folded(square(r.own_joint[c], r.far_joint[c]))
 
@@ -1339,19 +1411,20 @@
 
             r.go_pair[k] = total.astype(BF16)
         lane.g_out_pair.start_all()
+        send_home(1, r.own_out, r.home_out)
 
         lane.g_norms.take_all()
         summed = r.gn_recv[0]
         for index in range(1, chips * mp_size):
             summed = summed + r.gn_recv[index]
-        low, high = summed[:, :shard], summed[:, shard:]
-        first = core == 0
-        r.gn_pair[...] = jnp.where(first, high, low)
+        r.gn_pair[...] = summed
         lane.g_norms_pair.start_all()
         lane.g_out_pair.take_all()
+        send_home(5, r.far_out, r.home_far_out)
         squares = squares + folded(square(r.own_out[...], r.far_out[...]))
         lane.g_norms_pair.take_all()
-        own_norms = jnp.where(first, low, high) + r.gn_far[...]
+        summed = summed + r.gn_far[...]
+        own_norms = jnp.where(core == 0, summed[:4], summed[4:])
         r.own_norms[...] = own_norms
         own_norms = jnp.sum(own_norms * own_norms, axis=0, keepdims=True) * (1.0 / mp_size)
         squares = squares + folded(own_norms)
@@ -1379,26 +1452,29 @@
             entry.sent_all()
         for index in range(3):
             passing(index, False).wait_send()
+        for entry in leaving:
+            entry.wait()
 
     vmem = pl.BlockSpec(memory_space=pltpu.VMEM)
     any_space = pl.BlockSpec(memory_space=pl.ANY)
-    sem_shapes = [pltpu.SemaphoreType.DMA((4,))]
-    for kind in LANES.values():
-        sem_shapes += [pltpu.SemaphoreType.DMA((vars(groups)[kind].size,))] * 2
-    sem_shapes += [pltpu.SemaphoreType.DMA((4,))] * 2 * (3 + pieces)
-    sem_shapes += [pltpu.SemaphoreType.DMA((6,))] * 2 * (3 + pieces)
+    sem_shapes = [pltpu.SemaphoreType.DMA((4,)), pltpu.SemaphoreType.DMA((8,))]
+    for name, kind in LANES.items():
+        count = 2 * HALVED.get(name, 1)
+        sem_shapes += [pltpu.SemaphoreType.DMA((vars(groups)[kind].size,))] * count
+    sem_shapes += [pltpu.SemaphoreType.DMA((4,))] * 2 * (4 + pieces)
+    sem_shapes += [pltpu.SemaphoreType.DMA((6,))] * 2 * (4 + pieces)
     sem_shapes += [pltpu.SemaphoreType.DMA((3,))] * 2
     results = pl.pallas_call(
         kernel,
-        out_shape=list(outs.values()),
+        out_shape=list(outs.values()) + list(homes.values()),
         in_specs=[vmem] * 3 + [any_space] * 4 + [vmem],
-        out_specs=[vmem] * len(outs),
+        out_specs=[vmem] * len(outs) + [any_space] * len(homes),
         scratch_shapes=[pltpu.VMEM(*entry) for entry in scratch.values()] + sem_shapes,
         compiler_params=pltpu.CompilerParams(
             collective_id=30, has_side_effects=True, vmem_limit_bytes=VMEM_LIMIT
         ),
     )(x, segments, cotangent, joint_w, out_w, expand_w, contract_w, norms)
-    return SimpleNamespace(**dict(zip(outs, results)))
+    return SimpleNamespace(**dict(zip(list(outs) + list(homes), results)))
 
 
 VMEM_LIMIT = 60 * 2**20
@@ -1408,11 +1484,11 @@
     params, firsts, seconds = arrays[3:8], arrays[8:13], arrays[13:18]
     r = layer(dp_size, mp_size, arrays[:8])
     grads = (
-        r.own_joint + r.far_joint.astype(F32),
-        r.own_out + r.far_out.astype(F32),
-        r.own_expand + r.far_expand.astype(F32),
-        r.own_contract + r.far_contract.astype(F32),
-        r.own_norms[:4],
+        r.home_joint + r.home_far_joint.astype(F32),
+        r.home_out + r.home_far_out.astype(F32),
+        r.home_expand + r.home_far_expand.astype(F32),
+        r.home_contract + r.home_far_contract.astype(F32),
+        r.own_norms,
     )
     gradient_norm = jnp.sqrt(r.square_sum[0, 0])
     clip_factor = jnp.minimum(1.0, MAX_NORM / (gradient_norm + CLIP_EPSILON))

time: 231 us -> 214 us (0.926)
  Pallas kernels: 206 us -> 188 us
    pallas_call x1, Pallas kernels: 206 us -> 188 us  [layer(): pl.pallas_call(kernel, out_shape=list(outs.values()) + list(homes.values(...]
where the time goes in v5:
time: 214 us
  Pallas kernels  188 us (88%)
  other arithmetic  18.2 us (9%)
  local copies, waits for them, and re-layouts  5.23 us (2%)
  between operations  2.72 us (1%)
    pallas_call x1, Pallas kernels, layer(): pl.pallas_call(kernel, out_shape=list(outs.values()) + list(homes.values(...  188 us
    convert_element_type x4, other arithmetic, local(): copies = [entry[2].astype(BF16) for entry in updates]  18.2 us

profile of v5, /device:TPU:0, one launch (start us, length us, event | category | flops | bytes accessed | tf_op | source)
XLA Modules:
  0.0 213.8 jit_solution(13377772071782009228)
XLA Ops:
  0.7 0.0 copy-start
  0.7 187.7 %shard_map.393 = (bf16[128,2048]{1,0:T(8,128)(2,1)}, f32[128,2048]{1,0:T(8,128)}, f32[4,256]{1,0:T(4,128)}, f32[8,128]{1,0:T(8,128)}, f32[3,256,512]{2,1,0:T(8,1...) custom-call(bf16[128,2048]{1,0:T(8,128)(2,1)} %refs_0_.1, ...), custom_call_target="tpu_custom_call" | custom-call | tf_op jit(solution)/shard_map/pallas_call | solution.py:1467
  188.4 1.2 slice.3
  190.3 0.0 copy-done
  190.3 0.0 copy-start.2
  190.3 0.0 copy-start.8
  190.3 0.0 copy-start.9
  190.3 0.0 copy-start.10
  190.3 0.0 copy-start.12
  190.4 0.0 copy-start.5
  190.4 0.0 copy-start.7
  190.4 12.4 %fusion.7 = (bf16[256,2048]{1,0:T(8,128)(2,1)}, f32[256,2048]{1,0:T(8,128)}, f32[256,2048]{1,0:T(8,128)}, f32[256,2048]{1,0:T(8,128)}, f32[256,2048]{1,0:T(8,128...) fusion(f32[256,2048]{1,0:T(8,128)} %refs_6_.1, ...), kind=kLoop, calls=%fused_computation.25 | loop fusion | flops 19922944 | bytes 37748740 | tf_op jit(solution)/shard_map/convert_element_type | solution.py:1499
  202.8 0.0 copy-done.2
  202.8 0.0 copy-done.8
  202.8 0.0 copy-done.9
  202.8 0.0 copy-done.10
  202.8 0.0 copy-done.12
  202.8 0.0 copy-start.1
  202.8 0.0 copy-start.3
  202.8 0.0 copy-start.4
  202.8 1.6 fusion.11
  204.4 0.0 copy-done.5
  204.4 0.0 copy-done.7
  204.4 0.5 copy-done.1
  204.9 0.7 copy-done.3
  205.5 0.5 copy-done.4
  206.0 0.0 copy-start.13
  206.0 0.0 copy-start.14
  206.0 0.0 copy-start.15
  206.0 0.0 copy-start.16
  206.0 0.0 copy-start.11
  206.0 0.0 copy-start.6
  206.1 3.6 %fusion.13 = (bf16[3,256,512]{2,1,0:T(8,128)(2,1)}, f32[3,256,512]{2,1,0:T(8,128)}, f32[3,256,512]{2,1,0:T(8,128)}, f32[3,256,512]{2,1,0:T(8,128)}, f32[3,256,512]{2,1,0:T(8,128)}) fusion(f32[3,256,512]{2,1,0:T(8,128)S(1)} %copy-done.1, f32[]{:T(128)S(6)} %min_shard_map.3, f32[3,256,512]{2,1,0:T(8,128)S(1)} %copy-done.3, f32[3,256,512]{2,1,0:T(8,128)S(1)} %copy-done.4, ...), kind=kLoop, calls=%fused_computation.28 | loop fusion | flops 7471104 | bytes 14155780 | tf_op jit(solution)/shard_map/convert_element_type | solution.py:1499
  209.7 0.0 copy-done.13
  209.7 0.0 copy-done.14
  209.7 0.0 copy-done.15
  209.7 0.0 copy-done.16
  209.7 0.6 fusion.5
  210.3 0.0 copy-done.11
  210.3 0.8 copy.49
  211.1 0.0 copy-done.6
  211.1 1.0 copy.50
  212.1 0.6 copy.51
Async XLA Ops:
  0.7 189.6 %copy-start = (f32[256,2048]{1,0:T(8,128)S(1)}, f32[256,2048]{1,0:T(8,128)}, u32[]{:S(2)}) copy-start(f32[256,2048]{1,0:T(8,128)} %refs_5_.1) | copy-start | bytes 6291460
  190.3 12.5 %copy-start.2 = (f32[64,2048]{1,0:T(8,128)S(1)}, f32[64,2048]{1,0:T(8,128)}, u32[]{:S(2)}) copy-start(f32[64,2048]{1,0:T(8,128)} %refs_4_.1) | copy-start | bytes 1572868
  190.3 12.5 %copy-start.8 = (f32[64,2048]{1,0:T(8,128)S(1)}, f32[64,2048]{1,0:T(8,128)}, u32[]{:S(2)}) copy-start(f32[64,2048]{1,0:T(8,128)} %param.32) | copy-start | bytes 1572868
  190.3 12.5 %copy-start.9 = (f32[64,2048]{1,0:T(8,128)S(1)}, f32[64,2048]{1,0:T(8,128)}, u32[]{:S(2)}) copy-start(f32[64,2048]{1,0:T(8,128)} %param.27) | copy-start | bytes 1572868
  190.3 12.5 %copy-start.10 = (f32[64,2048]{1,0:T(8,128)S(1)}, f32[64,2048]{1,0:T(8,128)}, u32[]{:S(2)}) copy-start(f32[64,2048]{1,0:T(8,128)} %get-tuple-element.44) | copy-start | bytes 1572868
  190.3 12.5 %copy-start.12 = (bf16[64,2048]{1,0:T(8,128)(2,1)S(1)}, bf16[64,2048]{1,0:T(8,128)(2,1)}, u32[]{:S(2)}) copy-start(bf16[64,2048]{1,0:T(8,128)(2,1)} %get-tuple-element.45) | copy-start | bytes 786436
  190.4 14.1 %copy-start.5 = (f32[3,256,512]{2,1,0:T(8,128)S(1)}, f32[3,256,512]{2,1,0:T(8,128)}, u32[]{:S(2)}) copy-start(f32[3,256,512]{2,1,0:T(8,128)} %get-tuple-element.42) | copy-start | bytes 4718596
  190.4 14.0 %copy-start.7 = (bf16[3,256,512]{2,1,0:T(8,128)(2,1)S(1)}, bf16[3,256,512]{2,1,0:T(8,128)(2,1)}, u32[]{:S(2)}) copy-start(bf16[3,256,512]{2,1,0:T(8,128)(2,1)} %get-tuple-element.43) | copy-start | bytes 2359300
  202.8 2.1 copy-start.1
  202.8 2.7 %copy-start.3 = (f32[3,256,512]{2,1,0:T(8,128)S(1)}, f32[3,256,512]{2,1,0:T(8,128)}, u32[]{:S(2)}) copy-start(f32[3,256,512]{2,1,0:T(8,128)} %param.31) | copy-start | bytes 4718596
  202.8 3.2 %copy-start.4 = (f32[3,256,512]{2,1,0:T(8,128)S(1)}, f32[3,256,512]{2,1,0:T(8,128)}, u32[]{:S(2)}) copy-start(f32[3,256,512]{2,1,0:T(8,128)} %param.26) | copy-start | bytes 4718596
  206.0 3.7 %copy-start.13 = (f32[4,256]{1,0:T(4,128)S(1)}, f32[4,256]{1,0:T(4,128)}, u32[]{:S(2)}) copy-start(f32[4,256]{1,0:T(4,128)} %refs_7_.1) | copy-start | bytes 12292
  206.0 3.7 %copy-start.14 = (f32[4,256]{1,0:T(4,128)S(1)}, f32[4,256]{1,0:T(4,128)}, u32[]{:S(2)}) copy-start(f32[4,256]{1,0:T(4,128)} %get-tuple-element.115) | copy-start | bytes 12292
  206.0 3.7 %copy-start.15 = (f32[4,256]{1,0:T(4,128)S(1)}, f32[4,256]{1,0:T(4,128)}, u32[]{:S(2)}) copy-start(f32[4,256]{1,0:T(4,128)} %param.35) | copy-start | bytes 12292
  206.0 3.7 %copy-start.16 = (f32[4,256]{1,0:T(4,128)S(1)}, f32[4,256]{1,0:T(4,128)}, u32[]{:S(2)}) copy-start(f32[4,256]{1,0:T(4,128)} %param.30) | copy-start | bytes 12292
  206.0 4.3 %copy-start.11 = (bf16[128,2048]{1,0:T(8,128)(2,1)S(1)}, bf16[128,2048]{1,0:T(8,128)(2,1)}, u32[]{:S(2)}) copy-start(bf16[128,2048]{1,0:T(8,128)(2,1)} %get-tuple-element.109) | copy-start | bytes 1572868
  206.0 5.1 %copy-start.6 = (f32[128,2048]{1,0:T(8,128)S(1)}, f32[128,2048]{1,0:T(8,128)}, u32[]{:S(2)}) copy-start(f32[128,2048]{1,0:T(8,128)} %get-tuple-element.110) | copy-start | bytes 3145732

commit v6 on v5

--- a/solution.py
+++ b/solution.py
@@ -581,22 +581,25 @@
 
 
 class Lane:
-    def __init__(self, group, me, sems, view):
-        self.group, self.me, self.view = group, me, view
-        self.send_sems, self.recv_sems = sems
+    def __init__(self, group, me, sems, view, bulk=None):
+        self.group, self.me, self.view, self.bulk = group, me, view, bulk
+        self.sems = sems
         self.size = group.size
 
-    def copy(self, step):
-        to = lax.rem(self.me + step, self.size)
+    def remote(self, source, target, step):
+        index = step - 1 if self.bulk is None else 0
         return pltpu.make_async_remote_copy(
-            src_ref=self.view(self.me, to)[0],
-            dst_ref=self.view(self.me, to)[1],
-            send_sem=self.send_sems.at[step],
-            recv_sem=self.recv_sems.at[step],
-            device_id=self.group.device(to),
+            src_ref=source,
+            dst_ref=target,
+            send_sem=self.sems[0].at[index],
+            recv_sem=self.sems[1].at[index],
+            device_id=self.group.device(lax.rem(self.me + step, self.size)),
             device_id_type=pl.DeviceIdType.MESH,
         )
 
+    def copy(self, step):
+        return self.remote(*self.view(self.me, lax.rem(self.me + step, self.size)), step)
+
     def start(self, step):
         self.copy(step).start()
 
@@ -608,23 +611,20 @@
 
     def take(self, step):
         to = lax.rem(self.me + step, self.size)
-        pltpu.make_async_remote_copy(
-            src_ref=self.view(self.me, to)[0],
-            dst_ref=self.view(self.source(step), self.me)[1],
-            send_sem=self.send_sems.at[step],
-            recv_sem=self.recv_sems.at[step],
-            device_id=self.group.device(to),
-            device_id_type=pl.DeviceIdType.MESH,
-        ).wait_recv()
+        source, target = self.view(self.me, to)[0], self.view(self.source(step), self.me)[1]
+        self.remote(source, target, step).wait_recv()
 
     def take_all(self):
-        repeat(1, self.size, self.take)
-
-    def sent(self, step):
-        self.copy(step).wait_send()
+        if self.bulk is None:
+            repeat(1, self.size, self.take)
+        else:
+            self.remote(self.bulk, self.bulk, 1).wait_recv()
 
     def sent_all(self):
-        repeat(1, self.size, self.sent)
+        if self.bulk is None:
+            repeat(1, self.size, lambda step: self.copy(step).wait_send())
+        else:
+            self.remote(self.bulk, self.bulk, 1).wait_send()
 
 
 class Hop:
@@ -766,6 +766,7 @@
     squares_pair=PAIR,
 )
 
+STEPWISE = dict(normed=True)
 HALVED = dict(branch=2, second=2, d_second=2, d_hidden=2)
 
 
@@ -794,7 +795,7 @@
         layer_output=shape((length, model)),
         input_grad=shape((length, model), F32),
         own_norms=shape((4, shard), F32),
-        square_sum=shape((8, 128), F32),
+        square_sum=shape((1, 1), F32),
     )
     homes = dict(
         home_joint=shape((3, shard, width), F32),
@@ -832,6 +833,7 @@
         b_send=((2, mp_size, half_strip, model), BF16),
         b_recv=((2, mp_size, half_strip, model), BF16),
         hid=((2, half_strip, model), F32),
+        bulk=(((chips * mp_size - 1) * strip, slab), BF16),
         c_mine=((2, chips, half_strip, slab), BF16),
         c_all=((2, chips, mp_size, half_strip, slab), BF16),
         u_send=((2, chips, 2, tokens // 4, units), BF16),
@@ -944,6 +946,21 @@
             squares=lambda s, t: (r.sq_mine, r.sq_recv.at[s]),
             squares_pair=lambda s, t: (r.sq_pair, r.sq_far),
         )
+        others = chips * mp_size - 1
+        column_blocks = pl.ds(0, mp_size - 1)
+        bulks = dict(
+            norms=r.norm_all.at[pl.ds(0, dp_size - 1)],
+            branch=[r.b_recv.at[h, column_blocks] for h in range(2)],
+            second=[r.bulk.at[pl.ds(0, others * half_strip), :]] * 2,
+            d_second=[r.bulk.at[pl.ds(0, others * half_strip), :]] * 2,
+            d_hidden=[r.da_rows.at[column_blocks, h] for h in range(2)],
+            out_strip=r.y2_recv.at[column_blocks],
+            d_first=r.bulk,
+            out_rows=r.y_rows.at[column_blocks],
+            in_rows=r.ig_rows.at[column_blocks],
+            g_norms=r.gn_recv.at[pl.ds(0, others)],
+            squares=r.sq_recv.at[pl.ds(0, others)],
+        )
         lane = SimpleNamespace()
         every_lane = []
         used = iter(sems[2:])
@@ -954,9 +971,12 @@
         for name, kind in LANES.items():
             group = vars(groups)[kind]
             several = name in HALVED
+            bulk = bulks.get(name, None)
             lanes = [
-                Lane(group, group.me(), pair_of(), view)
-                for view in (views[name] if several else [views[name]])
+                Lane(group, group.me(), pair_of(), view, one)
+                for view, one in (
+                    zip(views[name], bulk) if several else [(views[name], bulk)]
+                )
             ]
             every_lane += lanes
             setattr(lane, name, lanes if several else lanes[0])
@@ -1374,13 +1394,13 @@
         back, gain_one, shift_one = norm_back(d_normed, r.x[part(mp, strip), :].astype(F32), norm_row(0))
         grad = r.dh[...].reshape(strip, model) + back
         r.ig_mine[...] = grad.astype(BF16)
-        lane.in_rows.start_all()
-        r.input_grad[part(mp, strip), :] = grad
         for index, row in enumerate((gain_one, shift_one, gain_two, shift_two)):
             for b in range(dp_size):
                 place = (b % 2) * 4 + index
                 r.gn_send[b // 2, place : place + 1, :] = row[:, b * shard : (b + 1) * shard]
         lane.g_norms.start_all()
+        lane.in_rows.start_all()
+        r.input_grad[part(mp, strip), :] = grad
         r.gn_recv[cross_me] = r.gn_send[chip]
 
         def square(own, distant):
@@ -1447,7 +1467,7 @@
         r.sq_pair[...] = total
         lane.squares_pair.start_all()
         lane.squares_pair.take_all()
-        r.square_sum[...] = total + r.sq_far[...]
+        r.square_sum[...] = (total + r.sq_far[...])[:1, :1]
         for entry in every_lane:
             entry.sent_all()
         for index in range(3):
@@ -1460,7 +1480,8 @@
     sem_shapes = [pltpu.SemaphoreType.DMA((4,)), pltpu.SemaphoreType.DMA((8,))]
     for name, kind in LANES.items():
         count = 2 * HALVED.get(name, 1)
-        sem_shapes += [pltpu.SemaphoreType.DMA((vars(groups)[kind].size,))] * count
+        slots = vars(groups)[kind].size - 1 if kind == PAIR or name in STEPWISE else 1
+        sem_shapes += [pltpu.SemaphoreType.DMA((slots,))] * count
     sem_shapes += [pltpu.SemaphoreType.DMA((4,))] * 2 * (4 + pieces)
     sem_shapes += [pltpu.SemaphoreType.DMA((6,))] * 2 * (4 + pieces)
     sem_shapes += [pltpu.SemaphoreType.DMA((3,))] * 2
@@ -1490,7 +1511,7 @@
         r.home_contract + r.home_far_contract.astype(F32),
         r.own_norms,
     )
-    gradient_norm = jnp.sqrt(r.square_sum[0, 0])
+    gradient_norm = jnp.sqrt(r.square_sum.reshape(()))
     clip_factor = jnp.minimum(1.0, MAX_NORM / (gradient_norm + CLIP_EPSILON))
     updates = [
         adam_update(params[k], grads[k], firsts[k], seconds[k], LEARN_RATES[k], clip_factor)

time: 214 us -> 205 us (0.958)
  Pallas kernels: 188 us -> 180 us
    pallas_call x1, Pallas kernels: 188 us -> 180 us  [layer(): pl.pallas_call(kernel, out_shape=list(outs.values()) + list(homes.values(...]
where the time goes in v6:
time: 205 us
  Pallas kernels  180 us (88%)
  other arithmetic  18.2 us (9%)
  local copies, waits for them, and re-layouts  4.05 us (2%)
  between operations  2.74 us (1%)
    pallas_call x1, Pallas kernels, layer(): pl.pallas_call(kernel, out_shape=list(outs.values()) + list(homes.values(...  180 us
    convert_element_type x4, other arithmetic, local(): copies = [entry[2].astype(BF16) for entry in updates]  18.2 us

profile of v6, /device:TPU:0, one launch (start us, length us, event | category | flops | bytes accessed | tf_op | source)
XLA Modules:
  0.0 205.3 jit_solution(6826854958592500780)
XLA Ops:
  0.7 0.0 copy-start
  0.7 180.3 %shard_map.393 = (bf16[128,2048]{1,0:T(8,128)(2,1)}, f32[128,2048]{1,0:T(8,128)}, f32[4,256]{1,0:T(4,128)}, f32[1,1]{1,0:T(1,128)}, f32[3,256,512]{2,1,0:T(8,128...) custom-call(bf16[128,2048]{1,0:T(8,128)(2,1)} %refs_0_.1, ...), custom_call_target="tpu_custom_call" | custom-call | tf_op jit(solution)/shard_map/pallas_call | solution.py:1488
  181.8 0.0 copy-done
  181.8 0.0 copy-start.2
  181.8 0.0 copy-start.8
  181.8 0.0 copy-start.9
  181.8 0.0 copy-start.10
  181.8 0.0 copy-start.12
  181.8 0.0 copy-start.5
  181.8 0.0 copy-start.7
  181.8 12.4 %fusion.7 = (bf16[256,2048]{1,0:T(8,128)(2,1)}, f32[256,2048]{1,0:T(8,128)}, f32[256,2048]{1,0:T(8,128)}, f32[256,2048]{1,0:T(8,128)}, f32[256,2048]{1,0:T(8,128...) fusion(f32[256,2048]{1,0:T(8,128)} %refs_6_.1, ...), kind=kLoop, calls=%fused_computation.25 | loop fusion | flops 19922944 | bytes 37748740 | tf_op jit(solution)/shard_map/convert_element_type | solution.py:1520
  194.2 0.0 copy-done.2
  194.2 0.0 copy-done.8
  194.3 0.0 copy-done.9
  194.3 0.0 copy-done.10
  194.3 0.0 copy-done.12
  194.3 0.0 copy-start.1
  194.3 0.0 copy-start.3
  194.3 0.0 copy-start.4
  194.3 1.6 fusion.11
  195.9 0.0 copy-done.5
  195.9 0.0 copy-done.7
  195.9 0.5 copy-done.1
  196.4 0.7 copy-done.3
  197.0 0.5 copy-done.4
  197.5 0.0 copy-start.13
  197.5 0.0 copy-start.14
  197.5 0.0 copy-start.15
  197.5 0.0 copy-start.16
  197.5 0.0 copy-start.11
  197.5 0.0 copy-start.6
  197.5 3.6 %fusion.13 = (bf16[3,256,512]{2,1,0:T(8,128)(2,1)}, f32[3,256,512]{2,1,0:T(8,128)}, f32[3,256,512]{2,1,0:T(8,128)}, f32[3,256,512]{2,1,0:T(8,128)}, f32[3,256,512]{2,1,0:T(8,128)}) fusion(f32[3,256,512]{2,1,0:T(8,128)S(1)} %copy-done.1, f32[]{:T(128)S(6)} %min_shard_map.3, f32[3,256,512]{2,1,0:T(8,128)S(1)} %copy-done.3, f32[3,256,512]{2,1,0:T(8,128)S(1)} %copy-done.4, ...), kind=kLoop, calls=%fused_computation.28 | loop fusion | flops 7471104 | bytes 14155780 | tf_op jit(solution)/shard_map/convert_element_type | solution.py:1520
  201.2 0.0 copy-done.13
  201.2 0.0 copy-done.14
  201.2 0.0 copy-done.15
  201.2 0.0 copy-done.16
  201.2 0.6 fusion.5
  201.8 0.0 copy-done.11
  201.8 0.8 copy.49
  202.6 0.0 copy-done.6
  202.6 1.0 copy.50
  203.6 0.6 copy.51
Async XLA Ops:
  0.7 181.1 %copy-start = (f32[256,2048]{1,0:T(8,128)S(1)}, f32[256,2048]{1,0:T(8,128)}, u32[]{:S(2)}) copy-start(f32[256,2048]{1,0:T(8,128)} %refs_5_.1) | copy-start | bytes 6291460
  181.8 12.5 %copy-start.2 = (f32[64,2048]{1,0:T(8,128)S(1)}, f32[64,2048]{1,0:T(8,128)}, u32[]{:S(2)}) copy-start(f32[64,2048]{1,0:T(8,128)} %refs_4_.1) | copy-start | bytes 1572868
  181.8 12.5 %copy-start.8 = (f32[64,2048]{1,0:T(8,128)S(1)}, f32[64,2048]{1,0:T(8,128)}, u32[]{:S(2)}) copy-start(f32[64,2048]{1,0:T(8,128)} %param.32) | copy-start | bytes 1572868
  181.8 12.5 %copy-start.9 = (f32[64,2048]{1,0:T(8,128)S(1)}, f32[64,2048]{1,0:T(8,128)}, u32[]{:S(2)}) copy-start(f32[64,2048]{1,0:T(8,128)} %param.27) | copy-start | bytes 1572868
  181.8 12.5 %copy-start.10 = (f32[64,2048]{1,0:T(8,128)S(1)}, f32[64,2048]{1,0:T(8,128)}, u32[]{:S(2)}) copy-start(f32[64,2048]{1,0:T(8,128)} %get-tuple-element.44) | copy-start | bytes 1572868
  181.8 12.5 %copy-start.12 = (bf16[64,2048]{1,0:T(8,128)(2,1)S(1)}, bf16[64,2048]{1,0:T(8,128)(2,1)}, u32[]{:S(2)}) copy-start(bf16[64,2048]{1,0:T(8,128)(2,1)} %get-tuple-element.45) | copy-start | bytes 786436
  181.8 14.1 %copy-start.5 = (f32[3,256,512]{2,1,0:T(8,128)S(1)}, f32[3,256,512]{2,1,0:T(8,128)}, u32[]{:S(2)}) copy-start(f32[3,256,512]{2,1,0:T(8,128)} %get-tuple-element.42) | copy-start | bytes 4718596
  181.8 14.0 %copy-start.7 = (bf16[3,256,512]{2,1,0:T(8,128)(2,1)S(1)}, bf16[3,256,512]{2,1,0:T(8,128)(2,1)}, u32[]{:S(2)}) copy-start(bf16[3,256,512]{2,1,0:T(8,128)(2,1)} %get-tuple-element.43) | copy-start | bytes 2359300
  194.3 2.1 %copy-start.1 = (f32[3,256,512]{2,1,0:T(8,128)S(1)}, f32[3,256,512]{2,1,0:T(8,128)}, u32[]{:S(2)}) copy-start(f32[3,256,512]{2,1,0:T(8,128)} %refs_3_.1) | copy-start | bytes 4718596
  194.3 2.7 %copy-start.3 = (f32[3,256,512]{2,1,0:T(8,128)S(1)}, f32[3,256,512]{2,1,0:T(8,128)}, u32[]{:S(2)}) copy-start(f32[3,256,512]{2,1,0:T(8,128)} %param.31) | copy-start | bytes 4718596
  194.3 3.2 %copy-start.4 = (f32[3,256,512]{2,1,0:T(8,128)S(1)}, f32[3,256,512]{2,1,0:T(8,128)}, u32[]{:S(2)}) copy-start(f32[3,256,512]{2,1,0:T(8,128)} %param.26) | copy-start | bytes 4718596
  197.5 3.7 %copy-start.13 = (f32[4,256]{1,0:T(4,128)S(1)}, f32[4,256]{1,0:T(4,128)}, u32[]{:S(2)}) copy-start(f32[4,256]{1,0:T(4,128)} %refs_7_.1) | copy-start | bytes 12292
  197.5 3.7 %copy-start.14 = (f32[4,256]{1,0:T(4,128)S(1)}, f32[4,256]{1,0:T(4,128)}, u32[]{:S(2)}) copy-start(f32[4,256]{1,0:T(4,128)} %get-tuple-element.115) | copy-start | bytes 12292
  197.5 3.7 %copy-start.15 = (f32[4,256]{1,0:T(4,128)S(1)}, f32[4,256]{1,0:T(4,128)}, u32[]{:S(2)}) copy-start(f32[4,256]{1,0:T(4,128)} %param.35) | copy-start | bytes 12292
  197.5 3.7 %copy-start.16 = (f32[4,256]{1,0:T(4,128)S(1)}, f32[4,256]{1,0:T(4,128)}, u32[]{:S(2)}) copy-start(f32[4,256]{1,0:T(4,128)} %param.30) | copy-start | bytes 12292
  197.5 4.3 %copy-start.11 = (bf16[128,2048]{1,0:T(8,128)(2,1)S(1)}, bf16[128,2048]{1,0:T(8,128)(2,1)}, u32[]{:S(2)}) copy-start(bf16[128,2048]{1,0:T(8,128)(2,1)} %get-tuple-element.109) | copy-start | bytes 1572868
  197.5 5.1 %copy-start.6 = (f32[128,2048]{1,0:T(8,128)S(1)}, f32[128,2048]{1,0:T(8,128)}, u32[]{:S(2)}) copy-start(f32[128,2048]{1,0:T(8,128)} %get-tuple-element.110) | copy-start | bytes 3145732

commit v7 on v6

--- a/solution.py
+++ b/solution.py
@@ -758,7 +758,6 @@
     out_strip=COLUMN,
     d_first=CROSS,
     g_joint=PAIR,
-    out_rows=COLUMN,
     in_rows=COLUMN,
     g_norms=CROSS,
     g_norms_pair=PAIR,
@@ -792,8 +791,8 @@
     piece = width // pieces
 
     outs = dict(
-        layer_output=shape((length, model)),
-        input_grad=shape((length, model), F32),
+        out_mine=shape((strip, model)),
+        grad_rows=shape((mp_size, strip, model)),
         own_norms=shape((4, shard), F32),
         square_sum=shape((1, 1), F32),
     )
@@ -854,19 +853,13 @@
         da_rows=((mp_size, 2, half_strip, model), BF16),
         dq_mine=((pieces, length, 3 * piece), BF16),
         dq_all=((pieces, chips, length, 3 * piece), BF16),
-        go_send=((chips, 2, out_rows, model), BF16),
-        go_recv=((3, 2, out_rows, model), BF16),
-        go_mid=((2, out_rows, model), BF16),
         go_pair=((2, out_rows, model), BF16),
         y2_send=((mp_size, strip, model), BF16),
         y2_recv=((mp_size, strip, model), BF16),
-        y_mine=((strip, model), BF16),
-        y_rows=((mp_size, strip, model), BF16),
         df_send=((chips, mp_size, strip, slab), BF16),
         df_recv=((chips, mp_size, strip, slab), BF16),
         gj_send=((3, shard, width), BF16),
         ig_mine=((strip, model), BF16),
-        ig_rows=((mp_size, strip, model), BF16),
         gn_send=((chips, 8, shard), F32),
         gn_recv=((chips * mp_size, 8, shard), F32),
         gn_pair=((8, shard), F32),
@@ -939,8 +932,7 @@
                 r.df_recv.at[lax.div(s, mp_size), lax.rem(s, mp_size)],
             ),
             g_joint=lambda s, t: (r.gj_send, r.far_joint),
-            out_rows=lambda s, t: (r.y_mine, r.y_rows.at[s]),
-            in_rows=lambda s, t: (r.ig_mine, r.ig_rows.at[s]),
+            in_rows=lambda s, t: (r.ig_mine, r.grad_rows.at[s]),
             g_norms=lambda s, t: (r.gn_send.at[lax.div(t, mp_size)], r.gn_recv.at[s]),
             g_norms_pair=lambda s, t: (r.gn_pair, r.gn_far),
             squares=lambda s, t: (r.sq_mine, r.sq_recv.at[s]),
@@ -956,8 +948,7 @@
             d_hidden=[r.da_rows.at[column_blocks, h] for h in range(2)],
             out_strip=r.y2_recv.at[column_blocks],
             d_first=r.bulk,
-            out_rows=r.y_rows.at[column_blocks],
-            in_rows=r.ig_rows.at[column_blocks],
+            in_rows=r.grad_rows.at[column_blocks],
             g_norms=r.gn_recv.at[pl.ds(0, others)],
             squares=r.sq_recv.at[pl.ds(0, others)],
         )
@@ -1007,7 +998,7 @@
         joint = [reduce(r.j_send.at[p], r.j_recv.at[p], r.j_mid.at[p]) for p in range(pieces)]
         pre_sum = [reduce(r.u_send.at[h], r.u_recv.at[h], r.u_mid.at[h]) for h in range(2)]
         out_sum = reduce(r.y_send, r.y_recv, r.y_mid)
-        g_out_sum = reduce(r.go_send, r.go_recv, r.go_mid)
+        g_out_sum = reduce(r.y_send, r.y_recv, r.y_mid)
         pass_sems = pair_of()
 
         def passing(index, to_me):
@@ -1322,25 +1313,13 @@
             d_joint[p].start()
             r.dq_all[p, chip] = r.dq_mine[p]
 
+        out_sum.sent_all()
+        every_lane.remove(out_sum)
         grad_out = mul(r.attended[...], flat(r.da_rows), ROWS_ROWS).astype(BF16)
         for c in range(chips):
             for k in range(2):
                 first = (2 * c + k) * out_rows
-                r.go_send[c, k] = grad_out[first : first + out_rows]
-        for p in range(pieces):
-            d_joint[p].forward()
-        lane.out_strip.take_all()
-        total = r.hid[...].reshape(strip, model) + r.y2_send[mp].astype(F32)
-        for step in range(1, mp_size):
-            total = total + r.y2_recv[lane.out_strip.source(step)].astype(F32)
-        r.y_mine[...] = total.astype(BF16)
-        lane.out_rows.start_all()
-        r.layer_output[part(mp, strip), :] = r.y_mine[...]
-        for c in range(chips):
-            r.own_expand[:, c * units : (c + 1) * units] = mul(
-                flat(r.c_all, mine), flat(r.du_all.at[:, c]), ROWS_ROWS
-            )
-        send_home(2, r.own_expand, r.home_expand)
+                r.y_send[c, k] = grad_out[first : first + out_rows]
 
         def first_block(block):
             total = jnp.zeros((length, slab), F32)
@@ -1362,6 +1341,8 @@
 
         first_block(chip)
         first_send(chip, range(1, mp_size))
+        for p in range(pieces):
+            d_joint[p].forward()
         for way in range(2):
             first_block(hop.chips[way])
             first_send(hop.chips[way], range(mp_size))
@@ -1386,6 +1367,16 @@
         for c in range(3):
             joint_grad(c, mine, r.own_joint)
         send_home(0, r.own_joint, r.home_joint)
+        for c in range(chips):
+            r.own_expand[:, c * units : (c + 1) * units] = mul(
+                flat(r.c_all, mine), flat(r.du_all.at[:, c]), ROWS_ROWS
+            )
+        send_home(2, r.own_expand, r.home_expand)
+        lane.out_strip.take_all()
+        total = r.hid[...].reshape(strip, model) + r.y2_send[mp].astype(F32)
+        for step in range(1, mp_size):
+            total = total + r.y2_recv[lane.out_strip.source(step)].astype(F32)
+        r.out_mine[...] = total.astype(BF16)
         g_out_sum.forward()
 
         lane.d_first.take_all()
@@ -1400,7 +1391,7 @@
                 r.gn_send[b // 2, place : place + 1, :] = row[:, b * shard : (b + 1) * shard]
         lane.g_norms.start_all()
         lane.in_rows.start_all()
-        r.input_grad[part(mp, strip), :] = grad
+        r.grad_rows[mp] = r.ig_mine[...]
         r.gn_recv[cross_me] = r.gn_send[chip]
 
         def square(own, distant):
@@ -1452,14 +1443,7 @@
         lane.squares.start_all()
         r.sq_recv[cross_me] = r.sq_mine[...]
 
-        def place(rows_lane, rows, output):
-            rows_lane.take_all()
-            for step in range(1, mp_size):
-                source = rows_lane.source(step)
-                output[part(source, strip), :] = rows[source].astype(output.dtype)
-
-        place(lane.out_rows, r.y_rows, r.layer_output)
-        place(lane.in_rows, r.ig_rows, r.input_grad)
+        lane.in_rows.take_all()
         lane.squares.take_all()
         total = r.sq_recv[0]
         for index in range(1, chips * mp_size):
@@ -1501,6 +1485,33 @@
 VMEM_LIMIT = 60 * 2**20
 
 
+def finish_kernel(mp_size, *refs):
+    blocks, (grad_rows, norms, output, input_grad, grad_norms) = refs[:mp_size], refs[mp_size:]
+    strip = blocks[0].shape[0]
+    for step, block in enumerate(blocks):
+        source = lax.rem(lax.axis_index("mp") + mp_size - step, mp_size)
+        output[part(source, strip), :] = block[...]
+    for m in range(mp_size):
+        input_grad[m * strip : (m + 1) * strip, :] = grad_rows[m].astype(F32)
+    grad_norms[...] = norms[...]
+
+
+def finish(r, mp_size):
+    blocks = [r.out_mine] + [
+        lax.ppermute(r.out_mine, "mp", [(i, (i + step) % mp_size) for i in range(mp_size)])
+        for step in range(1, mp_size)
+    ]
+    strip, model = r.out_mine.shape
+    return pl.pallas_call(
+        functools.partial(finish_kernel, mp_size),
+        out_shape=[
+            shape((mp_size * strip, model)),
+            shape((mp_size * strip, model), F32),
+            shape(r.own_norms.shape, F32),
+        ],
+    )(*blocks, r.grad_rows, r.own_norms)
+
+
 def local(dp_size, mp_size, *arrays):
     params, firsts, seconds = arrays[3:8], arrays[8:13], arrays[13:18]
     r = layer(dp_size, mp_size, arrays[:8])
@@ -1518,10 +1529,12 @@
         for k in range(5)
     ]
     copies = [entry[2].astype(BF16) for entry in updates]
+    layer_output, input_grad, grad_norms = finish(r, mp_size)
     return (
-        r.layer_output,
-        r.input_grad,
-        *grads,
+        layer_output,
+        input_grad,
+        *grads[:4],
+        grad_norms,
         *[entry[0] for entry in updates],
         *[entry[1] for entry in updates],
         *[entry[2] for entry in updates],

time: 205 us -> 202 us (0.985)
  Pallas kernels: 180 us -> 175 us
  starting transfers between devices: 0 us -> 3.88 us
  local copies, waits for them, and re-layouts: 4.05 us -> 1.91 us
    pallas_call x1, Pallas kernels: 180 us -> 172 us  [layer(): pl.pallas_call(kernel, out_shape=list(outs.values()) + list(homes.values(...]
    ppermute x0 -> x3, starting transfers between devices: none -> 3.88 us  [finish(): lax.ppermute(r.out_mine, 'mp', [(i, (i + step) % mp_size) for i in range(...]
    pallas_call x0 -> x1, Pallas kernels: none -> 2.55 us  [finish(): pl.pallas_call(functools.partial(finish_kernel, mp_size), out_shape=[shap...]
    unnamed x37 -> x32, local copies, waits for them, and re-layouts: 4.05 us -> 1.91 us
  transfers between devices with their start and end apart: 0 -> 3, of which waited for: 0 -> 0; matrix products, arithmetic and copies ran while one was open for 0% -> 9% of each run, Pallas kernels for 0% -> 0%
where the time goes in v7:
time: 202 us
  Pallas kernels  175 us (87%)
  other arithmetic  19 us (9%)
  starting transfers between devices  3.88 us (2%)
  between operations  2.77 us (1%)
    pallas_call x1, Pallas kernels, layer(): pl.pallas_call(kernel, out_shape=list(outs.values()) + list(homes.values(...  172 us
    convert_element_type x4, other arithmetic, local(): copies = [entry[2].astype(BF16) for entry in updates]  19 us
  transfers between devices with their start and end apart: 3, of which 0 were waited for; matrix products, arithmetic and copies ran while one was open for 9% of the time, Pallas kernels for 0%

profile of v7, /device:TPU:0, one launch (start us, length us, event | category | flops | bytes accessed | tf_op | source)
XLA Modules:
  0.0 202.1 jit_solution(1574013601093229225)
XLA Ops:
  0.7 0.0 copy-start.9
  0.7 0.0 copy-start.11
  0.7 0.0 copy-start.10
  0.7 172.1 %shard_map.393 = (bf16[32,2048]{1,0:T(8,128)(2,1)}, bf16[4,32,2048]{2,1,0:T(8,128)(2,1)}, f32[4,256]{1,0:T(4,128)}, f32[1,1]{1,0:T(1,128)}, f32[3,256,512]{2,1,0...) custom-call(bf16[128,2048]{1,0:T(8,128)(2,1)} %refs_0_.1, ...), custom_call_target="tpu_custom_call" | custom-call | tf_op jit(solution)/shard_map/pallas_call | solution.py:1472
  172.8 0.7 collective-permute-start
  173.4 0.6 collective-permute-start.1
  174.0 2.6 %collective-permute-start.2 = (bf16[32,2048]{1,0:T(8,128)(2,1)}, bf16[32,2048]{1,0:T(8,128)(2,1)}, u32[]{:S(2)}, u32[]{:S(2)}) collective-permute-start(bf16[32,2048]{1,0:T(8,128)(2,1)} %get-tuple-element.43.refs_0_), channel_id=1, source_target_pairs={{0,3},{1,0},{2,1},{3,2},{4,7},{5,4},{6,5},{7,6},{8,11},{9,8},{10,9... | collective-permute-start | bytes 393224 | tf_op jit(solution)/shard_map/ppermute | solution.py:1501
  177.4 0.0 copy-done.9
  177.4 0.0 copy-done.11
  177.5 0.0 copy-start.2
  177.5 0.0 copy-start.7
  177.5 0.0 copy-start.8
  177.5 3.0 %fusion.11 = (bf16[64,2048]{1,0:T(8,128)(2,1)}, f32[64,2048]{1,0:T(8,128)}, f32[64,2048]{1,0:T(8,128)}, f32[64,2048]{1,0:T(8,128)}, f32[64,2048]{1,0:T(8,128)}) fusion(f32[64,2048]{1,0:T(8,128)S(1)} %copy-done.9, f32[]{:T(128)S(6)} %min_shard_map.3, f32[64,2048]{1,0:T(8,128)S(1)} %copy-done.11, f32[64,2048]{1,0:T(8,128)} %param.27, ...), kind=kLoop, calls=%fused_computation.27 | loop fusion | flops 2490368 | bytes 4718596 | tf_op jit(solution)/shard_map/convert_element_type | solution.py:1531
  180.5 0.0 copy-done.10
  180.5 0.0 copy-done.2
  180.5 0.0 copy-start
  180.5 0.0 copy-start.1
  180.5 0.0 copy-start.3
  180.5 0.0 copy-start.4
  180.5 0.0 copy-start.5
  180.5 0.0 copy-start.6
  180.5 6.5 %fusion.13 = (bf16[3,256,512]{2,1,0:T(8,128)(2,1)}, f32[3,256,512]{2,1,0:T(8,128)}, f32[3,256,512]{2,1,0:T(8,128)}, f32[3,256,512]{2,1,0:T(8,128)}, f32[3,256,512]{2,1,0:T(8,128)}) fusion(f32[3,256,512]{2,1,0:T(8,128)S(1)} %copy-done.2, f32[]{:T(128)S(6)} %min_shard_map.3, f32[3,256,512]{2,1,0:T(8,128)S(1)} %copy-done.10, f32[3,256,512]{2,1,0:T(8,128)} %param.26, ...), kind=kLoop, calls=%fused_computation.28 | loop fusion | flops 7471104 | bytes 14155780 | tf_op jit(solution)/shard_map/convert_element_type | solution.py:1531
  187.0 0.0 copy-done.7
  187.0 0.0 copy-done.8
  187.0 0.0 copy-done
  187.0 0.0 copy-done.1
  187.0 0.0 copy-done.3
  187.1 0.0 copy-done.4
  187.1 1.2 copy-done.5
  188.3 0.6 copy-done.6
  188.9 0.0 copy-start.12
  188.9 0.0 copy-start.13
  188.9 0.0 copy-start.14
  188.9 0.0 copy-start.15
  188.9 8.9 %fusion.7 = (bf16[256,2048]{1,0:T(8,128)(2,1)}, f32[256,2048]{1,0:T(8,128)}, f32[256,2048]{1,0:T(8,128)}, f32[256,2048]{1,0:T(8,128)}, f32[256,2048]{1,0:T(8,128...) fusion(f32[256,2048]{1,0:T(8,128)S(1)} %copy-done.1, ...), kind=kLoop, calls=%fused_computation.25 | loop fusion | flops 19922944 | bytes 37748740 | tf_op jit(solution)/shard_map/convert_element_type | solution.py:1531
  197.8 0.0 copy-done.12
  197.8 0.0 copy-done.13
  197.8 0.0 copy-done.14
  197.8 0.0 copy-done.15
  197.8 0.6 fusion.5
  198.4 0.0 collective-permute-done.refs_1_
  198.4 0.0 collective-permute-done.1.refs_2_
  198.5 0.0 collective-permute-done.2.refs_3_
  198.5 2.6 %shard_map.394 = (bf16[128,2048]{1,0:T(8,128)(2,1)}, f32[128,2048]{1,0:T(8,128)}, f32[4,256]{1,0:T(4,128)}) custom-call(bf16[32,2048]{1,0:T(8,128)(2,1)} %get-tuple-element.43.refs_0_, bf16[32,2048]{1,0:T(8,128)(2,1)} %collective-permute-done.refs_1_, bf16[32,2048]{1,0:T(8,128)(2,1)} %collective-permute-done.1.refs_2_, ...), custom_call_target="tpu_custom_call" | custom-call | tf_op jit(solution)/shard_map/pallas_call | solution.py:1505
Async XLA Ops:
  0.7 176.8 %copy-start.9 = (f32[64,2048]{1,0:T(8,128)S(1)}, f32[64,2048]{1,0:T(8,128)}, u32[]{:S(2)}) copy-start(f32[64,2048]{1,0:T(8,128)} %refs_4_.1) | copy-start | bytes 1572868
  0.7 176.8 %copy-start.11 = (f32[64,2048]{1,0:T(8,128)S(1)}, f32[64,2048]{1,0:T(8,128)}, u32[]{:S(2)}) copy-start(f32[64,2048]{1,0:T(8,128)} %param.32) | copy-start | bytes 1572868
  0.7 179.8 %copy-start.10 = (f32[3,256,512]{2,1,0:T(8,128)S(1)}, f32[3,256,512]{2,1,0:T(8,128)}, u32[]{:S(2)}) copy-start(f32[3,256,512]{2,1,0:T(8,128)} %param.31) | copy-start | bytes 4718596
  172.8 25.7 %collective-permute-start = (bf16[32,2048]{1,0:T(8,128)(2,1)}, bf16[32,2048]{1,0:T(8,128)(2,1)}, u32[]{:S(2)}, u32[]{:S(2)}) collective-permute-start(bf16[32,2048]{1,0:T(8,128)(2,1)} %get-tuple-element.43.refs_0_), channel_id=1, source_target_pairs={{0,1},{1,2},{2,3},{3,0},{4,5},{5,6},{6,7},{7,4},{8,9},{9,10},{10,1... | collective-permute-start | bytes 393224 | tf_op jit(solution)/shard_map/ppermute | solution.py:1501
  173.4 25.0 %collective-permute-start.1 = (bf16[32,2048]{1,0:T(8,128)(2,1)}, bf16[32,2048]{1,0:T(8,128)(2,1)}, u32[]{:S(2)}, u32[]{:S(2)}) collective-permute-start(bf16[32,2048]{1,0:T(8,128)(2,1)} %get-tuple-element.43.refs_0_), channel_id=1, source_target_pairs={{0,2},{1,3},{2,0},{3,1},{4,6},{5,7},{6,4},{7,5},{8,10},{9,11},{10,... | collective-permute-start | bytes 393224 | tf_op jit(solution)/shard_map/ppermute | solution.py:1501
  174.0 24.4 %collective-permute-start.2 = (bf16[32,2048]{1,0:T(8,128)(2,1)}, bf16[32,2048]{1,0:T(8,128)(2,1)}, u32[]{:S(2)}, u32[]{:S(2)}) collective-permute-start(bf16[32,2048]{1,0:T(8,128)(2,1)} %get-tuple-element.43.refs_0_), channel_id=1, source_target_pairs={{0,3},{1,0},{2,1},{3,2},{4,7},{5,4},{6,5},{7,6},{8,11},{9,8},{10,9... | collective-permute-start | bytes 393224 | tf_op jit(solution)/shard_map/ppermute | solution.py:1501
  177.5 3.0 %copy-start.2 = (f32[3,256,512]{2,1,0:T(8,128)S(1)}, f32[3,256,512]{2,1,0:T(8,128)}, u32[]{:S(2)}) copy-start(f32[3,256,512]{2,1,0:T(8,128)} %refs_3_.1) | copy-start | bytes 4718596
  177.5 9.6 %copy-start.7 = (f32[256,2048]{1,0:T(8,128)S(1)}, f32[256,2048]{1,0:T(8,128)}, u32[]{:S(2)}) copy-start(f32[256,2048]{1,0:T(8,128)} %get-tuple-element.52) | copy-start | bytes 6291460
  177.5 9.6 %copy-start.8 = (f32[256,2048]{1,0:T(8,128)S(1)}, f32[256,2048]{1,0:T(8,128)}, u32[]{:S(2)}) copy-start(f32[256,2048]{1,0:T(8,128)} %get-tuple-element.54) | copy-start | bytes 6291460
  180.5 6.6 %copy-start = (f32[256,2048]{1,0:T(8,128)S(1)}, f32[256,2048]{1,0:T(8,128)}, u32[]{:S(2)}) copy-start(f32[256,2048]{1,0:T(8,128)} %refs_5_.1) | copy-start | bytes 6291460
  180.5 6.6 %copy-start.1 = (f32[256,2048]{1,0:T(8,128)S(1)}, f32[256,2048]{1,0:T(8,128)}, u32[]{:S(2)}) copy-start(f32[256,2048]{1,0:T(8,128)} %refs_6_.1) | copy-start | bytes 6291460
  180.5 6.6 %copy-start.3 = (f32[256,2048]{1,0:T(8,128)S(1)}, f32[256,2048]{1,0:T(8,128)}, u32[]{:S(2)}) copy-start(f32[256,2048]{1,0:T(8,128)} %param.34) | copy-start | bytes 6291460
  180.5 6.6 %copy-start.4 = (f32[256,2048]{1,0:T(8,128)S(1)}, f32[256,2048]{1,0:T(8,128)}, u32[]{:S(2)}) copy-start(f32[256,2048]{1,0:T(8,128)} %param.29) | copy-start | bytes 6291460
  180.5 7.8 %copy-start.5 = (f32[256,2048]{1,0:T(8,128)S(1)}, f32[256,2048]{1,0:T(8,128)}, u32[]{:S(2)}) copy-start(f32[256,2048]{1,0:T(8,128)} %param.33) | copy-start | bytes 6291460
  180.5 8.4 %copy-start.6 = (f32[256,2048]{1,0:T(8,128)S(1)}, f32[256,2048]{1,0:T(8,128)}, u32[]{:S(2)}) copy-start(f32[256,2048]{1,0:T(8,128)} %param.28) | copy-start | bytes 6291460
  188.9 8.9 %copy-start.12 = (f32[4,256]{1,0:T(4,128)S(1)}, f32[4,256]{1,0:T(4,128)}, u32[]{:S(2)}) copy-start(f32[4,256]{1,0:T(4,128)} %refs_7_.1) | copy-start | bytes 12292
  188.9 8.9 %copy-start.13 = (f32[4,256]{1,0:T(4,128)S(1)}, f32[4,256]{1,0:T(4,128)}, u32[]{:S(2)}) copy-start(f32[4,256]{1,0:T(4,128)} %get-tuple-element.45.refs_5_) | copy-start | bytes 12292
  188.9 8.9 %copy-start.14 = (f32[4,256]{1,0:T(4,128)S(1)}, f32[4,256]{1,0:T(4,128)}, u32[]{:S(2)}) copy-start(f32[4,256]{1,0:T(4,128)} %param.35) | copy-start | bytes 12292
  188.9 8.9 %copy-start.15 = (f32[4,256]{1,0:T(4,128)S(1)}, f32[4,256]{1,0:T(4,128)}, u32[]{:S(2)}) copy-start(f32[4,256]{1,0:T(4,128)} %param.30) | copy-start | bytes 12292

commit v8 on v6

--- a/solution.py
+++ b/solution.py
@@ -793,19 +793,15 @@
 
     outs = dict(
         layer_output=shape((length, model)),
-        input_grad=shape((length, model), F32),
+        grad_rows=shape((mp_size, strip, model)),
         own_norms=shape((4, shard), F32),
         square_sum=shape((1, 1), F32),
     )
     homes = dict(
-        home_joint=shape((3, shard, width), F32),
-        home_out=shape((out_rows, model), F32),
-        home_expand=shape((shard, hidden), F32),
-        home_contract=shape((own_units, model), F32),
-        home_far_joint=shape((3, shard, width)),
-        home_far_out=shape((out_rows, model)),
-        home_far_expand=shape((shard, hidden)),
-        home_far_contract=shape((own_units, model)),
+        sum_joint=shape((3, shard, width)),
+        sum_out=shape((out_rows, model)),
+        sum_expand=shape((shard, hidden)),
+        sum_contract=shape((own_units, model)),
     )
     scratch = dict(
         own_joint=((3, shard, width), F32),
@@ -866,7 +862,6 @@
         df_recv=((chips, mp_size, strip, slab), BF16),
         gj_send=((3, shard, width), BF16),
         ig_mine=((strip, model), BF16),
-        ig_rows=((mp_size, strip, model), BF16),
         gn_send=((chips, 8, shard), F32),
         gn_recv=((chips * mp_size, 8, shard), F32),
         gn_pair=((8, shard), F32),
@@ -940,7 +935,7 @@
             ),
             g_joint=lambda s, t: (r.gj_send, r.far_joint),
             out_rows=lambda s, t: (r.y_mine, r.y_rows.at[s]),
-            in_rows=lambda s, t: (r.ig_mine, r.ig_rows.at[s]),
+            in_rows=lambda s, t: (r.ig_mine, r.grad_rows.at[s]),
             g_norms=lambda s, t: (r.gn_send.at[lax.div(t, mp_size)], r.gn_recv.at[s]),
             g_norms_pair=lambda s, t: (r.gn_pair, r.gn_far),
             squares=lambda s, t: (r.sq_mine, r.sq_recv.at[s]),
@@ -957,7 +952,7 @@
             out_strip=r.y2_recv.at[column_blocks],
             d_first=r.bulk,
             out_rows=r.y_rows.at[column_blocks],
-            in_rows=r.ig_rows.at[column_blocks],
+            in_rows=r.grad_rows.at[column_blocks],
             g_norms=r.gn_recv.at[pl.ds(0, others)],
             squares=r.sq_recv.at[pl.ds(0, others)],
         )
@@ -1290,7 +1285,6 @@
             ).astype(BF16)
         lane.g_expand.start_all()
         r.own_contract[...] = contract_grad(part(core, own_units))
-        send_home(3, r.own_contract, r.home_contract)
         for h in range(2):
             lane.d_hidden[h].take_all()
 
@@ -1327,20 +1321,6 @@
             for k in range(2):
                 first = (2 * c + k) * out_rows
                 r.go_send[c, k] = grad_out[first : first + out_rows]
-        for p in range(pieces):
-            d_joint[p].forward()
-        lane.out_strip.take_all()
-        total = r.hid[...].reshape(strip, model) + r.y2_send[mp].astype(F32)
-        for step in range(1, mp_size):
-            total = total + r.y2_recv[lane.out_strip.source(step)].astype(F32)
-        r.y_mine[...] = total.astype(BF16)
-        lane.out_rows.start_all()
-        r.layer_output[part(mp, strip), :] = r.y_mine[...]
-        for c in range(chips):
-            r.own_expand[:, c * units : (c + 1) * units] = mul(
-                flat(r.c_all, mine), flat(r.du_all.at[:, c]), ROWS_ROWS
-            )
-        send_home(2, r.own_expand, r.home_expand)
 
         def first_block(block):
             total = jnp.zeros((length, slab), F32)
@@ -1362,6 +1342,8 @@
 
         first_block(chip)
         first_send(chip, range(1, mp_size))
+        for p in range(pieces):
+            d_joint[p].forward()
         for way in range(2):
             first_block(hop.chips[way])
             first_send(hop.chips[way], range(mp_size))
@@ -1369,6 +1351,13 @@
             d_joint[p].finish()
         first_block(hop.far)
         first_send(hop.far, range(mp_size))
+        lane.out_strip.take_all()
+        total = r.hid[...].reshape(strip, model) + r.y2_send[mp].astype(F32)
+        for step in range(1, mp_size):
+            total = total + r.y2_recv[lane.out_strip.source(step)].astype(F32)
+        r.y_mine[...] = total.astype(BF16)
+        lane.out_rows.start_all()
+        r.layer_output[part(mp, strip), :] = r.y_mine[...]
         g_out_sum.start(0)
         g_out_sum.start(1)
 
@@ -1385,7 +1374,10 @@
         lane.g_joint.start_all()
         for c in range(3):
             joint_grad(c, mine, r.own_joint)
-        send_home(0, r.own_joint, r.home_joint)
+        for c in range(chips):
+            r.own_expand[:, c * units : (c + 1) * units] = mul(
+                flat(r.c_all, mine), flat(r.du_all.at[:, c]), ROWS_ROWS
+            )
         g_out_sum.forward()
 
         lane.d_first.take_all()
@@ -1400,26 +1392,27 @@
                 r.gn_send[b // 2, place : place + 1, :] = row[:, b * shard : (b + 1) * shard]
         lane.g_norms.start_all()
         lane.in_rows.start_all()
-        r.input_grad[part(mp, strip), :] = grad
+        r.grad_rows[mp] = r.ig_mine[...]
         r.gn_recv[cross_me] = r.gn_send[chip]
 
-        def square(own, distant):
-            whole = own + distant.astype(F32)
+        def settle(own, distant):
+            whole = own[...] + distant[...].astype(F32)
+            distant[...] = whole.astype(BF16)
             return jnp.sum(whole * whole, axis=0, keepdims=True)
 
         def folded(row):
             return sum(row[:, i : i + 128] for i in range(0, row.shape[1], 128))
 
         lane.g_contract.take_all()
-        send_home(7, r.far_contract, r.home_far_contract)
-        squares = folded(square(r.own_contract[...], r.far_contract[...]))
+        squares = folded(settle(r.own_contract, r.far_contract))
+        send_home(3, r.far_contract, r.sum_contract)
         lane.g_expand.take_all()
-        send_home(6, r.far_expand, r.home_far_expand)
-        squares = squares + folded(square(r.own_expand[...], r.far_expand[...]))
+        squares = squares + folded(settle(r.own_expand, r.far_expand))
+        send_home(2, r.far_expand, r.sum_expand)
         lane.g_joint.take_all()
-        send_home(4, r.far_joint, r.home_far_joint)
         for c in range(3):
-            squares = squares + folded(square(r.own_joint[c], r.far_joint[c]))
+            squares = squares + folded(settle(r.own_joint.at[c], r.far_joint.at[c]))
+        send_home(0, r.far_joint, r.sum_joint)
 
         for k in range(2):
             g_out_sum.take(k)
@@ -1431,7 +1424,6 @@
 
             r.go_pair[k] = total.astype(BF16)
         lane.g_out_pair.start_all()
-        send_home(1, r.own_out, r.home_out)
 
         lane.g_norms.take_all()
         summed = r.gn_recv[0]
@@ -1440,8 +1432,8 @@
         r.gn_pair[...] = summed
         lane.g_norms_pair.start_all()
         lane.g_out_pair.take_all()
-        send_home(5, r.far_out, r.home_far_out)
-        squares = squares + folded(square(r.own_out[...], r.far_out[...]))
+        squares = squares + folded(settle(r.own_out, r.far_out))
+        send_home(1, r.far_out, r.sum_out)
         lane.g_norms_pair.take_all()
         summed = summed + r.gn_far[...]
         own_norms = jnp.where(core == 0, summed[:4], summed[4:])
@@ -1459,7 +1451,7 @@
                 output[part(source, strip), :] = rows[source].astype(output.dtype)
 
         place(lane.out_rows, r.y_rows, r.layer_output)
-        place(lane.in_rows, r.ig_rows, r.input_grad)
+        lane.in_rows.take_all()
         lane.squares.take_all()
         total = r.sq_recv[0]
         for index in range(1, chips * mp_size):
@@ -1477,7 +1469,7 @@
 
     vmem = pl.BlockSpec(memory_space=pltpu.VMEM)
     any_space = pl.BlockSpec(memory_space=pl.ANY)
-    sem_shapes = [pltpu.SemaphoreType.DMA((4,)), pltpu.SemaphoreType.DMA((8,))]
+    sem_shapes = [pltpu.SemaphoreType.DMA((4,)), pltpu.SemaphoreType.DMA((4,))]
     for name, kind in LANES.items():
         count = 2 * HALVED.get(name, 1)
         slots = vars(groups)[kind].size - 1 if kind == PAIR or name in STEPWISE else 1
@@ -1501,33 +1493,131 @@
 VMEM_LIMIT = 60 * 2**20
 
 
+CHUNKS = 4
+TILE_ROWS = 16
+
+
+def adam_kernel(shapes, *refs):
+    squares, output, grad_rows = refs[:3]
+    ins = [refs[3 + 4 * k : 7 + 4 * k] for k in range(4)]
+    norm_ins = refs[19:23]
+    norm_out, output_out, input_grad = refs[23:26]
+    outs = [refs[26 + 5 * k : 31 + 5 * k] for k in range(5)]
+    held = [refs[51 + 5 * k : 56 + 5 * k] for k in range(4)]
+    output_held, rows_held, grad_held, in_sems, out_sems, row_sems = refs[71:]
+
+    chunks = []
+    for k in (2, 3, 0, 1):
+        total = shapes[k][0]
+        count = max(total // CHUNKS, 64)
+        chunks += [(k, first, count) for first in range(0, total, count)]
+    loads = [
+        [
+            pltpu.make_async_copy(
+                ins[k][a].at[pl.ds(first, count), :],
+                held[k][a].at[pl.ds(first, count), :],
+                in_sems.at[4 * index + a],
+            )
+            for a in range(4)
+        ]
+        for index, (k, first, count) in enumerate(chunks)
+    ]
+    for group in loads:
+        for load in group:
+            load.start()
+    row_loads = [
+        pltpu.make_async_copy(output, output_held, row_sems.at[0]),
+        pltpu.make_async_copy(grad_rows, rows_held, row_sems.at[1]),
+    ]
+    for load in row_loads:
+        load.start()
+    norm = jnp.sqrt(squares[...])
+    norm_out[...] = norm
+    clip = jnp.minimum(1.0, MAX_NORM / (norm + CLIP_EPSILON))
+
+    stores = []
+    for index, (k, first, count) in enumerate(chunks):
+        for load in loads[index]:
+            load.wait()
+        low, weight, moment, square, whole = held[k]
+
+        def tile(i, none, k=k, first=first, refs=held[k]):
+            low, weight, moment, square, whole = refs
+            here = pl.ds(pl.multiple_of(first + i * TILE_ROWS, TILE_ROWS), TILE_ROWS)
+            grad = low[here, :].astype(F32)
+            entries = adam_update(
+                weight[here, :], grad, moment[here, :], square[here, :], LEARN_RATES[k], clip
+            )
+            whole[here, :] = grad
+            moment[here, :], square[here, :], weight[here, :] = entries
+            low[here, :] = entries[2].astype(BF16)
+            return none
+
+        lax.fori_loop(0, count // TILE_ROWS, tile, None)
+        for a, source in enumerate((whole, moment, square, weight, low)):
+            stores.append(
+                pltpu.make_async_copy(
+                    source.at[pl.ds(first, count), :],
+                    outs[k][a].at[pl.ds(first, count), :],
+                    out_sems.at[5 * index + a],
+                )
+            )
+            stores[-1].start()
+    for load in row_loads:
+        load.wait()
+    grad_held[...] = rows_held[...].astype(F32)
+    stores.append(pltpu.make_async_copy(output_held, output_out, row_sems.at[2]))
+    stores[-1].start()
+    stores.append(pltpu.make_async_copy(grad_held, input_grad, row_sems.at[3]))
+    stores[-1].start()
+    own, weight, moment, square = (entry[...] for entry in norm_ins)
+    entries = adam_update(weight, own, moment, square, LEARN_RATES[4], clip)
+    for target, entry in zip(outs[4], (own, *entries, entries[2].astype(BF16))):
+        target[...] = entry
+    for store in stores:
+        store.wait()
+
+
+def optimizer(r, params, firsts, seconds):
+    def rows(array):
+        return array.reshape(-1, array.shape[-1])
+
+    vmem, any_space = pl.BlockSpec(memory_space=pltpu.VMEM), pl.BlockSpec(memory_space=pl.ANY)
+    sums = (r.sum_joint, r.sum_out, r.sum_expand, r.sum_contract)
+    operands = [r.square_sum, r.layer_output, rows(r.grad_rows)]
+    results = [shape((1, 1), F32), shape(operands[1].shape), shape(operands[2].shape, F32)]
+    scratch, shapes = [], []
+    for total, weight, first, second in zip(sums, params, firsts, seconds):
+        arrays = [rows(a) for a in (total, weight, first, second)]
+        operands += arrays
+        shapes.append(arrays[0].shape)
+        results += [shape(shapes[-1], F32)] * 4 + [shape(shapes[-1])]
+        scratch += [pltpu.VMEM(a.shape, a.dtype) for a in arrays] + [pltpu.VMEM(shapes[-1], F32)]
+    operands += [r.own_norms, params[4], firsts[4], seconds[4]]
+    results += [shape(r.own_norms.shape, F32)] * 4 + [shape(r.own_norms.shape)]
+    count = sum(entry[0] // max(entry[0] // CHUNKS, 64) for entry in shapes)
+    out = pl.pallas_call(
+        functools.partial(adam_kernel, shapes),
+        in_specs=[vmem] + [any_space] * 18 + [vmem] * 4,
+        out_specs=[vmem] + [any_space] * 22 + [vmem] * 5,
+        out_shape=results,
+        scratch_shapes=scratch
+        + [pltpu.VMEM(entry.shape, entry.dtype) for entry in (operands[1], operands[2], results[2])]
+        + [pltpu.SemaphoreType.DMA((4 * count,)), pltpu.SemaphoreType.DMA((5 * count,))]
+        + [pltpu.SemaphoreType.DMA((4,))],
+        compiler_params=pltpu.CompilerParams(vmem_limit_bytes=VMEM_LIMIT),
+    )(*operands)
+    sets = [
+        [entry.reshape(params[k].shape) for entry in out[3 + 5 * k : 8 + 5 * k]] for k in range(5)
+    ]
+    return (out[1], out[2]), sets, out[0].reshape(())
+
+
 def local(dp_size, mp_size, *arrays):
     params, firsts, seconds = arrays[3:8], arrays[8:13], arrays[13:18]
     r = layer(dp_size, mp_size, arrays[:8])
-    grads = (
-        r.home_joint + r.home_far_joint.astype(F32),
-        r.home_out + r.home_far_out.astype(F32),
-        r.home_expand + r.home_far_expand.astype(F32),
-        r.home_contract + r.home_far_contract.astype(F32),
-        r.own_norms,
-    )
-    gradient_norm = jnp.sqrt(r.square_sum.reshape(()))
-    clip_factor = jnp.minimum(1.0, MAX_NORM / (gradient_norm + CLIP_EPSILON))
-    updates = [
-        adam_update(params[k], grads[k], firsts[k], seconds[k], LEARN_RATES[k], clip_factor)
-        for k in range(5)
-    ]
-    copies = [entry[2].astype(BF16) for entry in updates]
-    return (
-        r.layer_output,
-        r.input_grad,
-        *grads,
-        *[entry[0] for entry in updates],
-        *[entry[1] for entry in updates],
-        *[entry[2] for entry in updates],
-        *copies,
-        gradient_norm,
-    )
+    rows, sets, gradient_norm = optimizer(r, params, firsts, seconds)
+    return (*rows, *[sets[k][c] for c in range(5) for k in range(5)], gradient_norm)
 
 
 def solution(mesh):

time: 205 us -> 200 us (0.976)
  Pallas kernels: 180 us -> 199 us
  other arithmetic: 18.2 us -> 0 us
  local copies, waits for them, and re-layouts: 4.05 us -> 0 us
    pallas_call x0 -> x1, Pallas kernels: none -> 21.8 us  [optimizer(): pl.pallas_call(functools.partial(adam_kernel, shapes), in_specs=[vmem] +...]
    convert_element_type x4 -> x0, other arithmetic: 18.2 us -> none  [local(): copies = [entry[2].astype(BF16) for entry in updates]]
    unnamed x37 -> x0, local copies, waits for them, and re-layouts: 4.05 us -> none
    pallas_call x1, Pallas kernels: 180 us -> 177 us  [layer(): pl.pallas_call(kernel, out_shape=list(outs.values()) + list(homes.values(...]
where the time goes in v8:
time: 200 us
  Pallas kernels  199 us (100%)
    pallas_call x1, Pallas kernels, layer(): pl.pallas_call(kernel, out_shape=list(outs.values()) + list(homes.values(...  177 us
    pallas_call x1, Pallas kernels, optimizer(): pl.pallas_call(functools.partial(adam_kernel, shapes), in_specs=[vmem] +...  21.8 us

profile of v8, /device:TPU:0, one launch (start us, length us, event | category | flops | bytes accessed | tf_op | source)
XLA Modules:
  0.0 200.1 jit_solution(1355542790220756078)
XLA Ops:
  0.7 177.5 %shard_map.393 = (bf16[128,2048]{1,0:T(8,128)(2,1)}, bf16[4,32,2048]{2,1,0:T(8,128)(2,1)}, f32[4,256]{1,0:T(4,128)}, f32[1,1]{1,0:T(1,128)}, bf16[3,256,512]{2,1...) custom-call(bf16[128,2048]{1,0:T(8,128)(2,1)} %refs_0_.1, ...), custom_call_target="tpu_custom_call" | custom-call | tf_op jit(solution)/shard_map/pallas_call | solution.py:1480
  178.2 21.8 %shard_map.394 = (f32[1,1]{1,0:T(1,128)}, bf16[128,2048]{1,0:T(8,128)(2,1)}, f32[128,2048]{1,0:T(8,128)}, f32[768,512]{1,0:T(8,128)}, f32[768,512]{1,0:T(8,128)}...) custom-call(f32[1,1]{1,0:T(1,128)} %get-tuple-element.64.refs_0_, ...), custom_call_target="tpu_custom_call" | custom-call | tf_op jit(solution)/shard_map/pallas_call | solution.py:1599

commit v9 on v8

--- a/solution.py
+++ b/solution.py
@@ -792,18 +792,21 @@
     piece = width // pieces
 
     outs = dict(
-        layer_output=shape((length, model)),
-        grad_rows=shape((mp_size, strip, model)),
         own_norms=shape((4, shard), F32),
         square_sum=shape((1, 1), F32),
     )
     homes = dict(
+        home_output=shape((length, model)),
+        home_rows=shape((mp_size, strip, model)),
         sum_joint=shape((3, shard, width)),
         sum_out=shape((out_rows, model)),
         sum_expand=shape((shard, hidden)),
         sum_contract=shape((own_units, model)),
     )
     scratch = dict(
+        layer_output=((length, model), BF16),
+        grad_rows=((mp_size, strip, model), BF16),
+        cot=((length, model), BF16),
         own_joint=((3, shard, width), F32),
         own_out=((out_rows, model), F32),
         own_expand=((shard, hidden), F32),
@@ -872,7 +875,7 @@
         sq_far=((8, 128), F32),
     )
     in_names = dict(
-        x=0, seg_row=1, cot=2, f_joint=3, f_out=4, f_expand=5, f_contract=6, norm_own=7
+        x=0, seg_row=1, f_cot=2, f_joint=3, f_out=4, f_expand=5, f_contract=6, norm_own=7
     )
     names = list(in_names) + list(outs) + list(homes) + list(scratch)
 
@@ -1025,10 +1028,11 @@
                     (r.f_out, r.own_out),
                     (r.f_expand, r.own_expand),
                     (r.f_contract, r.own_contract),
+                    (r.f_cot, r.cot),
                 )
             )
         ]
-        for load in (loads[1], loads[0], loads[2], loads[3]):
+        for load in (loads[1], loads[0], loads[2], loads[3], loads[4]):
             load.start()
 
         leaving = []
@@ -1109,6 +1113,7 @@
             joint_part(p, hop.far)
             joint[p].start(0)
             joint_part(p, chip)
+        loads[4].wait()
         for h in range(2):
             for m in range(mp_size):
                 first = m * strip + h * half_strip
@@ -1451,7 +1456,9 @@
                 output[part(source, strip), :] = rows[source].astype(output.dtype)
 
         place(lane.out_rows, r.y_rows, r.layer_output)
+        send_home(4, r.layer_output, r.home_output)
         lane.in_rows.take_all()
+        send_home(5, r.grad_rows, r.home_rows)
         lane.squares.take_all()
         total = r.sq_recv[0]
         for index in range(1, chips * mp_size):
@@ -1469,7 +1476,7 @@
 
     vmem = pl.BlockSpec(memory_space=pltpu.VMEM)
     any_space = pl.BlockSpec(memory_space=pl.ANY)
-    sem_shapes = [pltpu.SemaphoreType.DMA((4,)), pltpu.SemaphoreType.DMA((4,))]
+    sem_shapes = [pltpu.SemaphoreType.DMA((5,)), pltpu.SemaphoreType.DMA((6,))]
     for name, kind in LANES.items():
         count = 2 * HALVED.get(name, 1)
         slots = vars(groups)[kind].size - 1 if kind == PAIR or name in STEPWISE else 1
@@ -1480,7 +1487,7 @@
     results = pl.pallas_call(
         kernel,
         out_shape=list(outs.values()) + list(homes.values()),
-        in_specs=[vmem] * 3 + [any_space] * 4 + [vmem],
+        in_specs=[vmem] * 2 + [any_space] * 5 + [vmem],
         out_specs=[vmem] * len(outs) + [any_space] * len(homes),
         scratch_shapes=[pltpu.VMEM(*entry) for entry in scratch.values()] + sem_shapes,
         compiler_params=pltpu.CompilerParams(
@@ -1584,7 +1591,7 @@
 
     vmem, any_space = pl.BlockSpec(memory_space=pltpu.VMEM), pl.BlockSpec(memory_space=pl.ANY)
     sums = (r.sum_joint, r.sum_out, r.sum_expand, r.sum_contract)
-    operands = [r.square_sum, r.layer_output, rows(r.grad_rows)]
+    operands = [r.square_sum, r.home_output, rows(r.home_rows)]
     results = [shape((1, 1), F32), shape(operands[1].shape), shape(operands[2].shape, F32)]
     scratch, shapes = [], []
     for total, weight, first, second in zip(sums, params, firsts, seconds):

time: 200 us -> 200 us (level)
  no operation moved by 1% of the time
where the time goes in v9:
time: 200 us; the launch traced here: 199 us
  Pallas kernels  199 us (100%)
    pallas_call x1, Pallas kernels, layer(): pl.pallas_call(kernel, out_shape=list(outs.values()) + list(homes.values(...  177 us
    pallas_call x1, Pallas kernels, optimizer(): pl.pallas_call(functools.partial(adam_kernel, shapes), in_specs=[vmem] +...  21.8 us

profile of v9, /device:TPU:0, one launch (start us, length us, event | category | flops | bytes accessed | tf_op | source)
XLA Modules:
  0.0 199.4 jit_solution(12990549617629077555)
XLA Ops:
  0.7 176.8 %shard_map.393 = (f32[4,256]{1,0:T(4,128)}, f32[1,1]{1,0:T(1,128)}, bf16[128,2048]{1,0:T(8,128)(2,1)}, bf16[4,32,2048]{2,1,0:T(8,128)(2,1)}, bf16[3,256,512]{2,1...) custom-call(bf16[128,2048]{1,0:T(8,128)(2,1)} %refs_0_.1, ...), custom_call_target="tpu_custom_call" | custom-call | tf_op jit(solution)/shard_map/pallas_call | solution.py:1487
  177.4 21.8 %shard_map.394 = (f32[1,1]{1,0:T(1,128)}, bf16[128,2048]{1,0:T(8,128)(2,1)}, f32[128,2048]{1,0:T(8,128)}, f32[768,512]{1,0:T(8,128)}, f32[768,512]{1,0:T(8,128)}...) custom-call(f32[1,1]{1,0:T(1,128)} %get-tuple-element.64.refs_0_, ...), custom_call_target="tpu_custom_call" | custom-call | tf_op jit(solution)/shard_map/pallas_call | solution.py:1606
